TPU v7x, 512 devices: a whole 4x4x16 slice. The times are simulated.
512 devices in a mesh: region: 64 (over y, z), season: 8 (over x, core).
Axes of the slice: x: 4, y: 4, z: 16, core: 2. Of those that a mesh axis runs over, the one named last changes fastest.
Arguments:
- demand: float32 [4096, 1024], P('region', 'season'), may hold values from 0.3 to 5.1, as said below
- avail: bfloat16 [16384, 1024], P('region', 'season'), may hold values from 0 to 1
- asset_bus: int32 [16384], P('region'), may hold values from 0 to 63
- run_cost: float32 [16384], P('region'), may hold values from 0.1 to 2
- build_cost: float32 [16384], P('region'), may hold values from 0.05 to 0.5
- line_from: int32 [16384], P('region'), may hold values from 0 to 63
- line_to: int32 [16384], P('region'), may hold values from 0 to 63
- link_count: int32 [64, 64], P('region'), may hold values from 0 to 4, as said below
- line_limit: float32 [16384], P('region'), may hold values from 0.5 to 2
- efficiency: float32 [4096], P('region'), may hold values from 0.6 to 1
- power_limit: float32 [4096], P('region'), may hold values from 0.5 to 2
- energy_limit: float32 [4096], P('region'), may hold values from 1 to 4
- season_link: int32 [4096, 8], P('region', 'season'), may hold values 0 or 1
- dispatch: float32 [16384, 1024], P('region', 'season'), may hold values from 0 to 1
- capacity: float32 [16384], P('region'), may hold values from 0.5 to 2
- flow: float32 [16384, 1024], P('region', 'season'), may hold values from -3 to 3
- charge: float32 [4096, 1024], P('region', 'season'), may hold values from -3 to 3
- soc: float32 [4096, 1024], P('region', 'season'), may hold values from 0 to 1
- price: float32 [4096, 1024], P('region', 'season'), may hold values from -5 to 5
- scarcity: float32 [16384, 1024], P('region', 'season'), may hold values from 0 to 1
- soc_dual: float32 [4096, 1024], P('region', 'season'), may hold values from -3 to 3
Outputs:
- next_dispatch: float32 [16384, 1024], P('region', 'season')
- next_capacity: float32 [16384], P('region')
- next_flow: float32 [16384, 1024], P('region', 'season')
- next_charge: float32 [4096, 1024], P('region', 'season')
- next_soc: float32 [4096, 1024], P('region', 'season')
- next_price: float32 [4096, 1024], P('region', 'season')
- next_scarcity: float32 [16384, 1024], P('region', 'season')
- next_soc_dual: float32 [4096, 1024], P('region', 'season')
Inputs may be any that keep to these rules, and one draw needn't show every extreme that they name: `link_count`: each row has at least one entry equal to 4. `demand`: positive.
All inputs are finite; a program needn't handle non-finite values. No bound on the sum of `season_link` on one device may be relied on, other than what follows from the above.
Results may differ from a plain program's by a relative error of at most 0.002.
Values may be sent and summed in bfloat16 or wider, within the bound.
No kernel may reach another device: no remote copies, remote signals or barrier semaphores. Data moves between devices by JAX's collectives and lax.ppermute only.
A program may use at most 64 MiB of HBM per device.

v0:
```python
import jax
import jax.numpy as jnp
from jax import lax
from jax.sharding import PartitionSpec as P

LINK_CAP = 4


step_size = 0.2


def passed_along(value, axis, steps):
    count = lax.axis_size(axis)
    pairs = [(source, (source + steps) % count) for source in range(count)]
    return lax.ppermute(value, axis, pairs)


def on_device(
    demand,
    avail,
    asset_bus,
    run_cost,
    build_cost,
    line_from,
    line_to,
    link_count,
    line_limit,
    efficiency,
    power_limit,
    energy_limit,
    season_link,
    dispatch,
    capacity,
    flow,
    charge,
    soc,
    price,
    scarcity,
    soc_dual,
):
    seasons = lax.axis_size("season")
    regions = lax.axis_size("region")
    bus_count = demand.shape[0]
    hour_count = demand.shape[1]
    total_hours = hour_count * seasons
    slot_index = jnp.arange(line_from.shape[0], dtype=jnp.int32)
    slot_target = slot_index // LINK_CAP
    region_ids = jnp.arange(regions, dtype=jnp.int32)
    slot_count = jnp.sum(
        jnp.where(slot_target[:, None] == region_ids[None, :], link_count[0][None, :], 0), axis=1
    )
    line_live = (slot_index % LINK_CAP < slot_count).astype(jnp.float32)
    limit_live = (line_limit * line_live)[:, None]
    bus_ids = jnp.arange(bus_count, dtype=jnp.int32)
    asset_onehot = (asset_bus[None, :] == bus_ids[:, None]).astype(jnp.bfloat16)
    leave_onehot = (line_from[None, :] == bus_ids[:, None]).astype(jnp.bfloat16)
    arrived_ends = lax.all_to_all(line_to, "region", split_axis=0, concat_axis=0, tiled=True)
    arrive_onehot = (arrived_ends[None, :] == bus_ids[:, None]).astype(jnp.bfloat16)
    far_global = slot_target * bus_count + line_to
    link_float = season_link.astype(jnp.float32)
    link_narrow = season_link.astype(jnp.bfloat16)
    decay = efficiency[:, None]

    def adjoint_apply(price_b, scarcity_b, dual_b):
        grad_dispatch = jnp.einsum(
            "ba,bh->ah", asset_onehot, price_b, preferred_element_type=jnp.float32
        ) - scarcity_b.astype(jnp.float32)
        near_prices = jnp.einsum(
            "bl,bh->lh", leave_onehot, price_b, preferred_element_type=jnp.float32
        )
        whole_prices = lax.all_gather(price_b, "region", axis=0, tiled=True)
        far_prices = jnp.take(whole_prices, far_global, axis=0).astype(jnp.float32)
        grad_flow = far_prices - near_prices
        local_sums = jnp.einsum("ah,ah->a", avail, scarcity_b, preferred_element_type=jnp.float32)
        grad_build = lax.psum(local_sums, "season") / total_hours
        dual_f = dual_b.astype(jnp.float32)
        grad_charge = price_b.astype(jnp.float32) + dual_f
        sending = dual_b[:, 0:1] * link_narrow
        arriving = passed_along(sending, "season", -1)
        after_last = (1.0 - link_float) * dual_f[:, 0:1] + arriving.astype(jnp.float32)
        following = jnp.concatenate([dual_f[:, 1:], after_last], axis=1)
        grad_soc = dual_f - decay * following
        return (grad_dispatch, grad_build, grad_flow, grad_charge, grad_soc)

    def forward_apply(dispatch_b, build_b, flow_b, charge_b, soc_b):
        generated = jnp.dot(asset_onehot, dispatch_b, preferred_element_type=jnp.float32)
        leaving = jnp.dot(leave_onehot, flow_b, preferred_element_type=jnp.float32)
        came_flows = lax.all_to_all(flow_b, "region", split_axis=0, concat_axis=0, tiled=True)
        arriving = jnp.dot(arrive_onehot, came_flows, preferred_element_type=jnp.float32)
        charge_f = charge_b.astype(jnp.float32)
        balance_rows = generated + charge_f + arriving - leaving
        avail_rows = avail.astype(jnp.float32) * build_b.astype(jnp.float32)[
            :, None
        ] - dispatch_b.astype(jnp.float32)
        last_hour = soc_b[:, -1:]
        before = passed_along(last_hour, "season", 1)
        soc_f = soc_b.astype(jnp.float32)
        carried = jnp.where(season_link == 1, before.astype(jnp.float32), soc_f[:, -1:])
        previous = jnp.concatenate([carried, soc_f[:, :-1]], axis=1)
        soc_rows = soc_f - decay * previous + charge_f
        return (balance_rows, avail_rows, soc_rows)

    def extrapolate(newer, older):
        return (2.0 * newer - older).astype(jnp.bfloat16)

    def primal_dual(state, tau, sigma):
        disp, build, flows, disch, level, duals, scarce, sdual = state
        grad_dispatch, grad_build, grad_flow, grad_charge, grad_soc = adjoint_apply(
            duals.astype(jnp.bfloat16), scarce.astype(jnp.bfloat16), sdual.astype(jnp.bfloat16)
        )
        disp_new = jnp.maximum(disp - tau * (run_cost[:, None] - grad_dispatch), 0.0)
        build_new = jnp.maximum(build - tau * (build_cost - grad_build), 0.0)
        flows_new = jnp.clip(flows + tau * grad_flow, -limit_live, limit_live)
        disch_new = jnp.clip(disch + tau * grad_charge, -power_limit[:, None], power_limit[:, None])
        level_new = jnp.clip(level + tau * grad_soc, 0.0, energy_limit[:, None])
        balance_rows, avail_rows, soc_rows = forward_apply(
            extrapolate(disp_new, disp),
            extrapolate(build_new, build),
            extrapolate(flows_new, flows),
            extrapolate(disch_new, disch),
            extrapolate(level_new, level),
        )
        duals_new = duals + sigma * (demand - balance_rows)
        scarce_new = jnp.maximum(scarce - sigma * avail_rows, 0.0)
        sdual_new = sdual - sigma * soc_rows
        return (
            disp_new,
            build_new,
            flows_new,
            disch_new,
            level_new,
            duals_new,
            scarce_new,
            sdual_new,
        )

    def halpern(state, tau, sigma):
        mapped = primal_dual(state, tau, sigma)
        return tuple((0.5 * (newer + older) for newer, older in zip(mapped, state)))

    start = (dispatch, capacity, flow * line_live[:, None], charge, soc, price, scarcity, soc_dual)
    half = halpern(start, step_size, step_size)
    moves = [jnp.sum((newer - older) * (newer - older)) for newer, older in zip(half, start)]
    primal_local = moves[0] + moves[1] / seasons + moves[2] + moves[3] + moves[4]
    dual_local = moves[5] + moves[6] + moves[7]
    primal_move, dual_move = lax.psum((primal_local, dual_local), ("region", "season"))
    weight = jnp.sqrt(jnp.sqrt((dual_move + 1e-06) / (primal_move + 1e-06)))
    final = halpern(half, step_size / weight, step_size * weight)
    return (final[0], final[1], final[2], final[3], final[4], final[5], final[6], final[7])


def solution(mesh):
    in_specs = (
        P("region", "season"),
        P("region", "season"),
        P("region"),
        P("region"),
        P("region"),
        P("region"),
        P("region"),
        P("region", None),
        P("region"),
        P("region"),
        P("region"),
        P("region"),
        P("region", "season"),
        P("region", "season"),
        P("region"),
        P("region", "season"),
        P("region", "season"),
        P("region", "season"),
        P("region", "season"),
        P("region", "season"),
        P("region", "season"),
    )
    out_specs = (
        P("region", "season"),
        P("region"),
        P("region", "season"),
        P("region", "season"),
        P("region", "season"),
        P("region", "season"),
        P("region", "season"),
        P("region", "season"),
    )
    return jax.shard_map(
        on_device, mesh=mesh, in_specs=in_specs, out_specs=out_specs, check_vma=False
    )
```

profile of v0, /device:TPU:2, one launch (start us, length us, event | category | flops | bytes accessed | tf_op | source)
XLA Modules:
  0.0 465.9 jit_solution(10206769053221762358)
XLA Ops:
  7.2 0.0 all-gather.3.cloned.1.call-start
  7.2 0.8 copy.119
  8.1 0.6 copy-done.6
  8.8 0.0 collective-permute-start
  8.8 0.6 copy-done.8
  9.4 0.1 copy-done.2
  9.5 0.1 copy.120
  9.6 0.7 copy-done.3
  10.3 0.1 copy.131
  10.4 0.6 copy-done.7
  11.1 0.6 multiply_reduce_fusion.3
  11.7 1.2 collective-permute-start.1
  12.9 0.1 copy.118
  13.0 5.2 %collective-permute-done.1 = bf16[64,1]{0,1:T(2,128)(2,1)S(1)} collective-permute-done((bf16[64,1]{0,1:T(2,128)(2,1)S(1)}, bf16[64,1]{0,1:T(2,128)(2,1)S(1)}, u32[]{:S(2)}, u32[]{:S(2)}) %collective-permute-start.1) | collective-permute-done | bytes 160 | tf_op jit(solution)/shard_map/ppermute | solution.py:15
  18.3 0.1 fusion.79
  18.3 0.7 copy.124
  19.0 0.0 all-gather.3.cloned.1.call-update
  19.1 0.7 all_to_all.22
  19.8 15.3 %all-to-all-start = ((s32[64,4,1]{1,2,0:T(1,128)}), s32[64,4,1]{1,2,0:T(1,128)S(1)}, u32[]{:S(2)}, u32[]{:S(2)}) async-start(s32[64,4,1]{1,2,0:T(1,128)} %bitcast), calls=%async_computation | async-start | bytes 65536 | tf_op jit(solution)/shard_map/all_to_all | solution.py:57
  35.1 0.1 select_reduce_fusion
  35.3 0.1 copy.127
  35.4 0.6 copy-done.1
  35.9 0.1 fusion.39
  36.1 13.0 %psum.28 = f32[256]{0:T(256)S(1)} all-reduce(f32[256]{0:T(256)S(1)} %fusion.39), channel_id=1, replica_groups=mesh['region'=64,'season'=8] {'season'}, use_global_device_ids=true, to_apply=%region_2.4 | all-reduce | flops 256 | bytes 2048 | tf_op jit(solution)/shard_map/psum | solution.py:75
  49.0 0.6 multiply_reduce_fusion.7
  50.4 2.8 collective-permute-start.2
  53.2 0.6 multiply_reduce_fusion.5
  53.8 0.6 multiply_reduce_fusion.4
  54.5 105.2 %all-gather.3.cloned.1.call-done = bf16[4096,128]{1,0:T(8,128)(2,1)} async-done(((bf16[64,128]{1,0:T(8,128)(2,1)}), bf16[4096,128]{1,0:T(8,128)(2,1)}) %all-gather.3.cloned.1.call-update) | async-done | bytes 1048592 | tf_op jit(solution)/shard_map/all_gather | solution.py:71
  159.7 2.1 gather_fusion
  161.8 0.7 copy-done.10
  162.4 1.5 multiply_reduce_fusion
  163.9 10.5 %all-to-all-start.1 = ((bf16[64,4,128]{2,1,0:T(4,128)(2,1)}), bf16[64,4,128]{2,1,0:T(4,128)(2,1)S(1)}, u32[]{:S(2)}, u32[]{:S(2)}) async-start(bf16[64,4,128]{2,1,0:T(4,128)(2,1)} %bitcast.2), calls=%async_computation.1 | async-start | bytes 131072 | tf_op jit(solution)/shard_map/all_to_all | solution.py:88
  174.5 0.0 all-gather.5.cloned.1.call-start
  174.5 0.6 copy-done.9
  175.1 0.9 fusion.38
  176.7 0.2 convolution_add_fusion.3
  176.9 0.5 broadcast.249
  177.4 0.7 reduce.7
  178.2 0.1 eq.63
  180.2 8.9 %all-to-all-done.1 = bf16[64,4,128]{2,1,0:T(4,128)(2,1)S(1)} async-done(((bf16[64,4,128]{2,1,0:T(4,128)(2,1)}), bf16[64,4,128]{2,1,0:T(4,128)(2,1)S(1)}, u32[]{:S(2)}, u32[]{:S(2)}) %all-to-all-start.1) | async-done | bytes 65568 | tf_op jit(solution)/shard_map/all_to_all | solution.py:88
  189.1 0.2 convolution_add_fusion.2
  189.3 1.7 multiply_reduce_fusion.6
  193.0 98.0 %all-reduce = (f32[]{:T(128)}, f32[]{:T(128)}) all-reduce(f32[]{:T(128)S(6)} %add.174, f32[]{:T(128)S(6)} %add.183), channel_id=1, replica_groups=mesh['region'=64,'season'=8] {'region','season'}, use_global_device_ids=true, to_apply=%region_5.7 | all-reduce | flops 2 | bytes 16 | tf_op jit(solution)/shard_map/psum | solution.py:146
  292.6 2.9 collective-permute-done.3
  295.5 0.1 fusion.43
  295.6 0.7 copy.140
  296.3 0.0 all-gather.5.cloned.1.call-update
  296.3 12.7 %psum.31 = f32[256]{0:T(256)S(1)} all-reduce(f32[256]{0:T(256)S(1)} %get-tuple-element.25), channel_id=1, replica_groups=mesh['region'=64,'season'=8] {'season'}, use_global_device_ids=true, to_apply=%region_12.14 | all-reduce | flops 256 | bytes 2048 | tf_op jit(solution)/shard_map/psum | solution.py:75
  309.0 0.7 copy.146
  309.7 0.6 fusion.77
  310.3 1.0 fusion.37
  311.2 117.8 %all-gather.5.cloned.1.call-done = bf16[4096,128]{1,0:T(8,128)(2,1)} async-done(((bf16[64,128]{1,0:T(8,128)(2,1)}), bf16[4096,128]{1,0:T(8,128)(2,1)}) %all-gather.5.cloned.1.call-update) | async-done | bytes 1048592 | tf_op jit(solution)/shard_map/all_gather | solution.py:71
  429.0 2.1 gather_fusion.1
  431.1 0.9 subtract_convert_fusion
  432.0 10.4 %all-to-all-start.2 = ((bf16[64,4,128]{2,1,0:T(4,128)(2,1)}), bf16[64,4,128]{2,1,0:T(4,128)(2,1)S(1)}, u32[]{:S(2)}, u32[]{:S(2)}) async-start(bf16[64,4,128]{2,1,0:T(4,128)(2,1)} %bitcast.4), calls=%async_computation.2 | async-start | bytes 131072 | tf_op jit(solution)/shard_map/all_to_all | solution.py:88
  442.4 0.1 add_multiply_fusion.5
  442.4 0.7 copy.145
  443.1 0.7 copy.148
  443.8 0.2 convolution_add_fusion.1
  444.1 13.0 %all-to-all-done.2 = bf16[64,4,128]{2,1,0:T(4,128)(2,1)S(1)} async-done(((bf16[64,4,128]{2,1,0:T(4,128)(2,1)}), bf16[64,4,128]{2,1,0:T(4,128)(2,1)S(1)}, u32[]{:S(2)}, u32[]{:S(2)}) %all-to-all-start.2) | async-done | bytes 65568 | tf_op jit(solution)/shard_map/all_to_all | solution.py:88
  457.1 0.2 convolution_add_fusion
  457.3 1.1 fusion.25
  458.3 0.7 copy.147
  (56 shorter events, 0.3 us)
Async XLA Ops:
  7.2 152.5 %all-gather.3.cloned.1.call-start = ((), (), s32[]{:S(2)}) async-start(), calls=%async_computation.3 | async-start | bytes 1064960 | tf_op jit(solution)/shard_map/all_gather | solution.py:71
  8.1 0.7 copy-start.6
  8.7 0.7 copy-start.8
  8.7 0.8 copy-start.2
  8.8 1.6 collective-permute-start
  9.5 0.8 copy-start.3
  10.4 0.7 copy-start.7
  10.4 0.7 copy-start.13
  11.1 1.9 copy-start.4
  11.7 6.5 %collective-permute-start.1 = (bf16[64,1]{0,1:T(2,128)(2,1)S(1)}, bf16[64,1]{0,1:T(2,128)(2,1)S(1)}, u32[]{:S(2)}, u32[]{:S(2)}) collective-permute-start(bf16[64,1]{0,1:T(2,128)(2,1)S(1)} %slice.55), channel_id=1, source_target_pairs={{0,1},{1,2},{2,3},{3,4},{4,5},{5,6},{6,7},{7,0},{8,9},{9,10},{10,1... | collective-permute-start | bytes 392 | tf_op jit(solution)/shard_map/ppermute | solution.py:15
  18.3 0.8 copy-start.11
  18.3 17.0 %copy-start = (f32[256,128]{1,0:T(8,128)S(1)}, f32[256,128]{1,0:T(8,128)}, u32[]{:S(2)}) copy-start(f32[256,128]{1,0:T(8,128)} %param.42) | copy-start | bytes 393220
  19.8 15.3 %copy-start.16 = (s32[1,64]{1,0:T(1,128)S(1)}, s32[1,64]{1,0:T(1,128)}, u32[]{:S(2)}) copy-start(s32[1,64]{1,0:T(1,128)} %param.30) | copy-start | bytes 772
  19.8 15.4 %copy-start.14 = (f32[256]{0:T(256)S(1)}, f32[256]{0:T(256)}, u32[]{:S(2)}) copy-start(f32[256]{0:T(256)} %param.31) | copy-start | bytes 3076
  19.8 15.5 %copy-start.5 = (f32[64,128]{1,0:T(8,128)S(1)}, f32[64,128]{1,0:T(8,128)}, u32[]{:S(2)}) copy-start(f32[64,128]{1,0:T(8,128)} %param.23) | copy-start | bytes 98308
  19.8 144.1 %all-to-all-start = ((s32[64,4,1]{1,2,0:T(1,128)}), s32[64,4,1]{1,2,0:T(1,128)S(1)}, u32[]{:S(2)}, u32[]{:S(2)}) async-start(s32[64,4,1]{1,2,0:T(1,128)} %bitcast), calls=%async_computation | async-start | bytes 65536 | tf_op jit(solution)/shard_map/all_to_all | solution.py:57
  35.1 0.8 copy-start.1
  36.0 13.0 %copy-start.12 = (f32[256]{0:T(256)S(1)}, f32[256]{0:T(256)}, u32[]{:S(2)}) copy-start(f32[256]{0:T(256)} %param.27) | copy-start | bytes 3076
  36.1 13.0 %copy-start.15 = (f32[256]{0:T(256)S(1)}, f32[256]{0:T(256)}, u32[]{:S(2)}) copy-start(f32[256]{0:T(256)} %param.37) | copy-start | bytes 3076
  50.4 142.6 %collective-permute-start.2 = (bf16[64,1]{0,1:T(2,128)(2,1)S(1)}, bf16[64,1]{0,1:T(2,128)(2,1)S(1)}, u32[]{:S(2)}, u32[]{:S(2)}) collective-permute-start(bf16[64,1]{0,1:T(2,128)(2,1)S(1)} %slice_multiply_fusion), channel_id=1, source_target_pairs={{0,7},{1,0},{2,1},{3,2},{4,3},{5,4},{6,5},{7,6},{8,15},{9,8},{10,9... | collective-permute-start | bytes 392 | tf_op jit(solution)/shard_map/ppermute | solution.py:15
  54.5 107.3 %copy-start.17 = (f32[256,128]{1,0:T(8,128)S(1)}, f32[256,128]{1,0:T(8,128)}, u32[]{:S(2)}) copy-start(f32[256,128]{1,0:T(8,128)} %param.38) | copy-start | bytes 393220
  161.7 0.7 copy-start.10
  163.9 10.6 %copy-start.18 = (f32[256,128]{1,0:T(8,128)S(1)}, f32[256,128]{1,0:T(8,128)}, u32[]{:S(2)}) copy-start(f32[256,128]{1,0:T(8,128)} %param.36) | copy-start | bytes 393220
  163.9 10.6 %copy-start.19 = (f32[256]{0:T(256)S(1)}, f32[256]{0:T(256)}, u32[]{:S(2)}) copy-start(f32[256]{0:T(256)} %param.26) | copy-start | bytes 3076
  163.9 25.2 %all-to-all-start.1 = ((bf16[64,4,128]{2,1,0:T(4,128)(2,1)}), bf16[64,4,128]{2,1,0:T(4,128)(2,1)S(1)}, u32[]{:S(2)}, u32[]{:S(2)}) async-start(bf16[64,4,128]{2,1,0:T(4,128)(2,1)} %bitcast.2), calls=%async_computation.1 | async-start | bytes 131072 | tf_op jit(solution)/shard_map/all_to_all | solution.py:88
  174.4 0.7 copy-start.9
  174.5 254.5 %all-gather.5.cloned.1.call-start = ((), (), s32[]{:S(2)}) async-start(), calls=%async_computation.4 | async-start | bytes 1064960 | tf_op jit(solution)/shard_map/all_gather | solution.py:71
  292.5 3.0 collective-permute-start.3
  432.0 25.1 %all-to-all-start.2 = ((bf16[64,4,128]{2,1,0:T(4,128)(2,1)}), bf16[64,4,128]{2,1,0:T(4,128)(2,1)S(1)}, u32[]{:S(2)}, u32[]{:S(2)}) async-start(bf16[64,4,128]{2,1,0:T(4,128)(2,1)} %bitcast.4), calls=%async_computation.2 | async-start | bytes 131072 | tf_op jit(solution)/shard_map/all_to_all | solution.py:88
Sparse Core Ops, SparseCore 0:
  19.2 140.4 all-gather.2
  296.4 132.5 all-gather.4
where the time goes:
time: 467 us; the launch traced here: 466 us
  waiting for transfers between devices  253 us (54%)
  blocking collectives  124 us (27%)
  starting transfers between devices  40.4 us (9%)
  between operations  21.1 us (5%)
  local copies, waits for them, and re-layouts  15.5 us (3%)
  matrix products  7.86 us (2%)
    all_gather x2, waiting for transfers between devices, adjoint_apply(): whole_prices = lax.all_gather(price_b, 'region', axis=0, tiled=True)  223 us
    psum x1, blocking collectives, on_device(): lax.psum((primal_local, dual_local), ('region', 'season'))  98 us
    psum x2, blocking collectives, adjoint_apply(): grad_build = lax.psum(local_sums, 'season') / total_hours  25.6 us
    all_to_all x2, waiting for transfers between devices, forward_apply(): lax.all_to_all(flow_b, 'region', split_axis=0, concat_axis=0, tiled=True)  21.9 us
    all_to_all x2, starting transfers between devices, forward_apply(): lax.all_to_all(flow_b, 'region', split_axis=0, concat_axis=0, tiled=True)  20.9 us
    all_to_all x1, starting transfers between devices, on_device(): lax.all_to_all(line_to, 'region', split_axis=0, concat_axis=0, tiled=True)  15.3 us
  transfers between devices with their start and end apart: 9, of which 6 were waited for; matrix products, arithmetic and copies ran while one was open for 3% of the time, Pallas kernels for 0%

commit v1 on v0

v1 whole, which is shorter than its diff:
```python
import jax
import jax.numpy as jnp
from jax import lax
from jax.experimental import pallas as pl
from jax.experimental.pallas import tpu as pltpu
from jax.sharding import PartitionSpec as P

LINK_CAP = 4
PACK = 3 * LINK_CAP
GROUP = 16
step_size = 0.2
F32 = jnp.float32
BF16 = jnp.bfloat16
I32 = jnp.int32
REGIONS, SEASONS = 64, 8
BUS, SLOT, HOUR = 64, 256, 128
PACKED = GROUP * PACK
UNPACKED = 2 * GROUP * LINK_CAP + GROUP


def iota(shape, axis):
    return lax.broadcasted_iota(I32, shape, axis)


def dot(a, b):
    return jnp.dot(a, b, preferred_element_type=F32)


def dot_t(a, b):
    return lax.dot_general(a, b, (((0,), (0,)), ((), ())), preferred_element_type=F32)


def as_bf(mask):
    return jnp.where(mask, 1.0, 0.0).astype(BF16)


def narrow(value):
    return value.astype(BF16)


def wide(value):
    return value.astype(F32)


def extrapolate(newer, older):
    return narrow(2.0 * newer - older)


def mean(newer, older):
    return 0.5 * (newer + older)


def total(value):
    return jnp.sum(jnp.sum(value, axis=1, keepdims=True), axis=0, keepdims=True)


def square(newer, older):
    moved = newer - older
    return total(moved * moved)


def row256(ref):
    return jnp.concatenate([ref[0:1, :], ref[1:2, :]], axis=1)


def pack_target(packed):
    q = lax.shift_right_logical(packed * 171, 11)
    j = packed - PACK * q
    first = LINK_CAP * q + j
    second = GROUP * LINK_CAP + LINK_CAP * q + j - LINK_CAP
    third = 2 * GROUP * LINK_CAP + q
    return jnp.where(
        j < LINK_CAP,
        first,
        jnp.where(j < 2 * LINK_CAP, second, jnp.where(j == 2 * LINK_CAP, third, -1)),
    )


def pack(first, second, third, out_ref):
    shape = (PACKED, UNPACKED)
    place = as_bf(pack_target(iota(shape, 0)) == iota(shape, 1))
    lines = GROUP * LINK_CAP
    for g in range(REGIONS // GROUP):
        rows = jnp.concatenate(
            [
                first[g * lines : (g + 1) * lines],
                second[g * lines : (g + 1) * lines],
                third[g * GROUP : (g + 1) * GROUP],
            ],
            axis=0,
        )
        out_ref[g * PACKED : (g + 1) * PACKED, :] = narrow(dot(place, rows))


def unpack(ref):
    shape = (UNPACKED, PACKED)
    place = as_bf(pack_target(iota(shape, 1)) == iota(shape, 0))
    parts = [
        dot(place, ref[g * PACKED : (g + 1) * PACKED, :]) for g in range(REGIONS // GROUP)
    ]
    lines = GROUP * LINK_CAP
    first = jnp.concatenate([p[:lines] for p in parts], axis=0)
    second = jnp.concatenate([p[lines : 2 * lines] for p in parts], axis=0)
    third = jnp.concatenate([p[2 * lines :] for p in parts], axis=0)
    return first, second, third


def columns(ref):
    return jnp.transpose(ref[...])


def long_column(turned, at):
    return jnp.concatenate([turned[:, at : at + 1], turned[:, at + 1 : at + 2]], axis=0)


def onehot_rows(column, count):
    return as_bf(column == wide(iota((SLOT, count), 1)))


def lines_out(
    flow, price, line_from, line_to, line_limit, link_count,
    sent, flow0, near0, cap, leave, turn,
):
    lane = iota((1, SLOT), 1)
    spread = as_bf(iota((REGIONS, SLOT), 0) == lax.shift_right_logical(iota((REGIONS, SLOT), 1), 2))
    counts = jnp.broadcast_to(narrow(wide(link_count[...])), (8, REGIONS))
    counts = dot(counts, spread)[0:1]
    live = jnp.where(wide(lane & (LINK_CAP - 1)) < counts, 1.0, 0.0)
    limit = row256(line_limit) * live
    turn[0:2, :] = wide(line_from[...])
    turn[2:3, :] = live[:, :128]
    turn[3:4, :] = live[:, 128:]
    turn[4:5, :] = limit[:, :128]
    turn[5:6, :] = limit[:, 128:]
    turned = columns(turn)
    leave_t = onehot_rows(long_column(turned, 0), BUS)
    f0 = flow[...] * long_column(turned, 2)
    near = narrow(dot(leave_t, narrow(price[...])))
    flow0[...] = f0
    near0[...] = near
    cap[...] = jnp.broadcast_to(long_column(turned, 4), (SLOT, HOUR))
    leave[...] = leave_t
    high = wide(narrow(limit))
    low = limit - high
    held = jnp.zeros((REGIONS, 128), F32)
    slot_kind = iota((SLOT, 128), 0) & (LINK_CAP - 1)
    for at, value in enumerate((wide(row256(line_to)), high, low)):
        spots = as_bf(iota((SLOT, 128), 1) == slot_kind + LINK_CAP * at)
        held = held + dot(spread * narrow(value), spots)
    pack(narrow(f0), near, narrow(held), sent)


def season_block(sums, level, dual_f, link_column, sent, move_row=None):
    lane = iota((128, 128), 1)
    tail = jnp.concatenate([level[:, HOUR - 1 : HOUR], dual_f[:, HOUR - 1 : HOUR]], axis=0)
    head = jnp.concatenate([dual_f[:, 0:1], link_column], axis=0)
    held = jnp.where(
        lane == 0,
        sums[:128],
        jnp.where(lane == 1, sums[128:], jnp.where(lane == 2, tail, jnp.where(lane == 3, head, 0.0))),
    )
    return jnp.transpose(held)[0:8]


def season_out(avail, scarcity, soc, soc_dual, link, sent, turn):
    turn[0:1, 0:BUS] = wide(link[...])
    turned = columns(turn)
    sums = jnp.sum(wide(avail[...]) * wide(narrow(scarcity[...])), axis=1, keepdims=True)
    rows = season_block(sums, soc[...], wide(narrow(soc_dual[...])), turned[:BUS, 0:1], sent)
    for s in range(SEASONS):
        sent[s] = rows


def ends_in(got, price, sent, arrive, cap):
    _, _, held = unpack(got)
    shape = (SLOT, REGIONS)
    spread = as_bf(iota(shape, 1) == lax.shift_right_logical(iota(shape, 0), 2))
    lines = dot(spread, narrow(held))
    lane = iota((SLOT, 128), 1)
    kind = iota((SLOT, 128), 0) & (LINK_CAP - 1)
    ends = jnp.sum(jnp.where(lane == kind, lines, 0.0), axis=1, keepdims=True)
    limits = (lane == kind + LINK_CAP) | (lane == kind + 2 * LINK_CAP)
    limit = jnp.sum(jnp.where(limits, lines, 0.0), axis=1, keepdims=True)
    arrive_t = onehot_rows(ends, BUS)
    sent[...] = narrow(dot(arrive_t, narrow(price[...])))
    arrive[...] = arrive_t
    cap[...] = jnp.broadcast_to(limit, (SLOT, HOUR))


def line_step(flows, near, far, cap, tau):
    moved = jnp.clip(flows + tau * (far - near), -cap, cap)
    return moved, extrapolate(moved, flows)


def local_step(season, consts, state, price_v, got, turn, tau, sigma):
    avail, asset_bus, run_cost, build_cost, efficiency, power, energy, link = consts
    disp, build, disch, level, scarce, sdual = state
    before_at = (season + SEASONS - 1) & (SEASONS - 1)
    after_at = (season + 1) & (SEASONS - 1)
    sums = got[0, 0:2]
    for s in range(1, SEASONS):
        sums = sums + got[s, 0:2]
    grad_build = sums * (1.0 / (HOUR * SEASONS))
    build_new = jnp.maximum(build - tau * (build_cost[...] - grad_build), 0.0)
    turn[0:8, :] = got[before_at]
    turn[8:16, :] = got[after_at]
    turn[16:18, :] = wide(extrapolate(build_new, build))
    turn[18:20, :] = run_cost[...]
    turn[20:22, :] = wide(asset_bus[...])
    turn[22:23, 0:BUS] = efficiency[...]
    turn[23:24, 0:BUS] = power[...]
    turn[24:25, 0:BUS] = energy[...]
    turn[25:26, 0:BUS] = wide(link[...])
    turned = columns(turn)
    build_x = long_column(turned, 16)
    cost = long_column(turned, 18)
    asset_t = onehot_rows(long_column(turned, 20), BUS)
    asset_row = row256(asset_bus)
    asset_onehot = as_bf(iota((BUS, SLOT), 0) == asset_row)
    decay = turned[:BUS, 22:23]
    power_c = turned[:BUS, 23:24]
    energy_c = turned[:BUS, 24:25]
    link_c = turned[:BUS, 25:26]
    before_level, before_dual = turned[:BUS, 2:3], turned[BUS:, 2:3]
    before_first, before_link = turned[:BUS, 3:4], turned[BUS:, 3:4]
    after_first, after_link = turned[:BUS, 11:12], turned[BUS:, 11:12]
    price_b = narrow(price_v)
    dual_f = wide(narrow(sdual))
    grad_dispatch = dot(asset_t, price_b) - wide(narrow(scarce))
    grad_charge = wide(price_b) + dual_f
    first = dual_f[:, 0:1]
    after_last = (1.0 - link_c) * first + after_link * after_first
    following = jnp.concatenate([dual_f[:, 1:], after_last], axis=1)
    grad_soc = dual_f - decay * following
    before_grad = before_dual - decay * ((1.0 - before_link) * before_first + link_c * first)
    disp_new = jnp.maximum(disp - tau * (cost - grad_dispatch), 0.0)
    disch_new = jnp.clip(disch + tau * grad_charge, -power_c, power_c)
    level_new = jnp.clip(level + tau * grad_soc, 0.0, energy_c)
    before_new = jnp.clip(before_level + tau * before_grad, 0.0, energy_c)
    disp_x = extrapolate(disp_new, disp)
    charge_f = wide(extrapolate(disch_new, disch))
    soc_f = wide(extrapolate(level_new, level))
    before_x = wide(extrapolate(before_new, before_level))
    balance = dot(asset_onehot, disp_x) + charge_f
    avail_rows = wide(avail[...]) * build_x - wide(disp_x)
    carried = jnp.where(link_c == 1.0, before_x, soc_f[:, HOUR - 1 : HOUR])
    previous = jnp.concatenate([carried, soc_f[:, : HOUR - 1]], axis=1)
    soc_rows = soc_f - decay * previous + charge_f
    scarce_new = jnp.maximum(scarce - sigma * avail_rows, 0.0)
    sdual_new = sdual - sigma * soc_rows
    halves = (
        mean(disp_new, disp),
        mean(build_new, build),
        mean(disch_new, disch),
        mean(level_new, level),
        mean(scarce_new, scarce),
        mean(sdual_new, sdual),
    )
    return balance, halves, link_c


def first_local(
    season, avail, asset_bus, run_cost, build_cost, efficiency, power, energy, link,
    disp, build, disch, level, scarce, sdual, price, got, lines_got, arrive, cap, far,
    disp1, build1, disch1, level1, scarce1, sdual1, came1, balance, rows, moves, turn,
):
    consts = (avail, asset_bus, run_cost, build_cost, efficiency, power, energy, link)
    state = (disp[...], build[...], disch[...], level[...], scarce[...], sdual[...])
    came0, near, _ = unpack(lines_got)
    moved, came_x = line_step(came0, near, wide(far[...]), cap[...], step_size)
    came1[...] = mean(moved, came0)
    local, halves, link_c = local_step(
        season[0], consts, state, price[...], got, turn, step_size, step_size
    )
    balance[...] = local + dot_t(arrive[...], came_x)
    for ref, value in zip((disp1, build1, disch1, level1, scarce1, sdual1), halves):
        ref[...] = value
    sums = jnp.sum(wide(avail[...]) * wide(narrow(halves[4])), axis=1, keepdims=True)
    rows[...] = season_block(sums, halves[3], wide(narrow(halves[5])), link_c, None)
    primal = (
        square(halves[0], state[0])
        + square(halves[1], state[1]) * (1.0 / SEASONS)
        + square(halves[2], state[2])
        + square(halves[3], state[3])
    )
    dual = square(halves[4], state[4]) + square(halves[5], state[5])
    lane = iota((8, 128), 1)
    moves[...] = jnp.where(lane == 0, primal, dual)


def price_step(
    flow0, near0, cap, leave, arrive, got, demand, price, balance, moves,
    price1, flow1, far0, sent,
):
    f0 = flow0[...]
    leave_t = leave[...]
    moved, flow_x = line_step(f0, wide(near0[...]), wide(got[...]), cap[...], step_size)
    f1 = mean(moved, f0)
    flow1[...] = f1
    p0 = price[...]
    whole = balance[...] - dot_t(leave_t, flow_x)
    p1 = mean(p0 + step_size * (demand[...] - whole), p0)
    price1[...] = p1
    primal = moves[0:1, 0:1] + square(f1, f0)
    dual = moves[0:1, 1:2] + square(p1, p0)
    lane = iota((GROUP, 128), 1)
    held = jnp.zeros((GROUP, 128), F32)
    for at, value in ((0, primal), (3, dual)):
        for step in range(3):
            piece = wide(narrow(value))
            held = jnp.where(lane == at + step, piece, held)
            value = value - piece
    held = narrow(held)
    price_b = narrow(p1)
    near = narrow(dot(leave_t, price_b))
    far = narrow(dot(arrive[...], price_b))
    far0[...] = far
    pack(near, far, jnp.concatenate([held] * (REGIONS // GROUP), axis=0), sent)


def moves_out(got, rows, sent):
    shape = (8, REGIONS * PACK)
    at = iota(shape, 1)
    q = lax.shift_right_logical(at * 21846, 18)
    mask = as_bf(at - PACK * q == 2 * LINK_CAP)
    moves = dot(mask, got[...])
    held = jnp.where(iota((8, 128), 0) == 4, moves, rows[...])
    for s in range(SEASONS):
        sent[s] = held


def second_step(
    season, avail, asset_bus, run_cost, build_cost, efficiency, power, energy, link,
    disp, build, disch, level, scarce, sdual, price, got, lines_got, arrive, came_cap,
    came_far, came, demand, flow, cap, leave,
    disp2, build2, flow2, disch2, level2, price2, scarce2, sdual2, turn,
):
    moves = got[0, 4:5]
    for s in range(1, SEASONS):
        moves = moves + got[s, 4:5]
    primal = moves[:, 0:1] + moves[:, 1:2] + moves[:, 2:3]
    dual = moves[:, 3:4] + moves[:, 4:5] + moves[:, 5:6]
    weight = jnp.sqrt(jnp.sqrt((dual + 1e-06) / (primal + 1e-06)))
    tau = step_size / weight
    sigma = step_size * weight
    consts = (avail, asset_bus, run_cost, build_cost, efficiency, power, energy, link)
    state = (disp[...], build[...], disch[...], level[...], scarce[...], sdual[...])
    came_near, far, _ = unpack(lines_got)
    _, came_x = line_step(came[...], came_near, wide(came_far[...]), came_cap[...], tau)
    f1 = flow[...]
    p1 = price[...]
    leave_t = leave[...]
    near = dot(leave_t, narrow(p1))
    moved, flow_x = line_step(f1, near, far, cap[...], tau)
    flow2[...] = mean(moved, f1)
    local, halves, _ = local_step(season[0], consts, state, p1, got, turn, tau, sigma)
    whole = local + dot_t(arrive[...], came_x) - dot_t(leave_t, flow_x)
    price2[...] = mean(p1 + sigma * (demand[...] - whole), p1)
    for ref, value in zip((disp2, build2, disch2, level2, scarce2, sdual2), halves):
        ref[...] = value


def call(body, outs, *operands, scalar=False, turn=False):
    in_specs = [pl.BlockSpec(memory_space=pltpu.VMEM)] * len(operands)
    if scalar:
        in_specs[0] = pl.BlockSpec(memory_space=pltpu.SMEM)
    return pl.pallas_call(
        body,
        out_shape=[jax.ShapeDtypeStruct(shape, kind) for shape, kind in outs],
        in_specs=in_specs,
        out_specs=[pl.BlockSpec(memory_space=pltpu.VMEM)] * len(outs),
        scratch_shapes=[pltpu.VMEM((128, 128), F32)] if turn else [],
        compiler_params=pltpu.CompilerParams(vmem_limit_bytes=32 * 1024 * 1024),
    )(*operands)


def region_exchange(value, per_pair):
    cut = value.reshape(REGIONS, per_pair, LINK_CAP, HOUR)
    got = lax.all_to_all(cut, "region", split_axis=0, concat_axis=0, tiled=True)
    return got.reshape(value.shape)


def season_exchange(value):
    return lax.all_to_all(value, "season", split_axis=0, concat_axis=0, tiled=True)


def on_device(
    demand,
    avail,
    asset_bus,
    run_cost,
    build_cost,
    line_from,
    line_to,
    link_count,
    line_limit,
    efficiency,
    power_limit,
    energy_limit,
    season_link,
    dispatch,
    capacity,
    flow,
    charge,
    soc,
    price,
    scarcity,
    soc_dual,
):
    season = lax.axis_index("season").astype(I32).reshape(1)
    pair = lambda v: v.reshape(2, 128)
    short = lambda v: v.reshape(1, BUS)
    link = short(season_link)
    lines = ((SLOT, HOUR), F32)
    lines_b = ((SLOT, HOUR), BF16)
    buses = ((BUS, HOUR), F32)
    picks = ((SLOT, BUS), BF16)
    packed = ((REGIONS * PACK, HOUR), BF16)
    seasons = ((SEASONS, 8, 128), F32)
    consts = (
        avail,
        pair(asset_bus),
        pair(run_cost),
        pair(build_cost),
        short(efficiency),
        short(power_limit),
        short(energy_limit),
        link,
    )
    sent1, flow0, near0, cap, leave = call(
        lines_out,
        [packed, lines, lines_b, lines, picks],
        flow,
        price,
        pair(line_from),
        pair(line_to),
        pair(line_limit),
        link_count,
        turn=True,
    )
    got1 = region_exchange(sent1, 3)
    (rows1,) = call(season_out, [seasons], avail, scarcity, soc, soc_dual, link, turn=True)
    season1 = season_exchange(rows1)
    sent2, arrive, came_cap = call(ends_in, [lines_b, picks, lines], got1, price)
    got2 = region_exchange(sent2, 1)
    disp1, build1, disch1, level1, scarce1, sdual1, came1, balance, rows2, moves = call(
        first_local,
        [lines, ((2, 128), F32), buses, buses, lines, buses, lines, buses, ((8, 128), F32), ((8, 128), F32)],
        season,
        *consts,
        dispatch,
        pair(capacity),
        charge,
        soc,
        scarcity,
        soc_dual,
        price,
        season1,
        got1,
        arrive,
        came_cap,
        sent2,
        scalar=True,
        turn=True,
    )
    price1, flow1, came_far1, sent3 = call(
        price_step,
        [buses, lines, lines_b, packed],
        flow0,
        near0,
        cap,
        leave,
        arrive,
        got2,
        demand,
        price,
        balance,
        moves,
    )
    got3 = region_exchange(sent3, 3)
    (rows3,) = call(moves_out, [seasons], got3, rows2)
    season2 = season_exchange(rows3)
    disp2, build2, flow2, disch2, level2, price2, scarce2, sdual2 = call(
        second_step,
        [lines, ((2, 128), F32), lines, buses, buses, buses, lines, buses],
        season,
        *consts,
        disp1,
        build1,
        disch1,
        level1,
        scarce1,
        sdual1,
        price1,
        season2,
        got3,
        arrive,
        came_cap,
        came_far1,
        came1,
        demand,
        flow1,
        cap,
        leave,
        scalar=True,
        turn=True,
    )
    return (disp2, build2.reshape(capacity.shape), flow2, disch2, level2, price2, scarce2, sdual2)


def solution(mesh):
    both = P("region", "season")
    rows = P("region")
    in_specs = (
        both,
        both,
        rows,
        rows,
        rows,
        rows,
        rows,
        P("region", None),
        rows,
        rows,
        rows,
        rows,
        both,
        both,
        rows,
        both,
        both,
        both,
        both,
        both,
        both,
    )
    out_specs = (both, rows, both, both, both, both, both, both)
    return jax.shard_map(
        on_device, mesh=mesh, in_specs=in_specs, out_specs=out_specs, check_vma=False
    )
```

time: 467 us -> 106 us (0.23)
  the two profiles are of different devices: /device:TPU:2 before, /device:TPU:1 now
where the time goes in v1:
time: 106 us; the launch traced here: 105 us
  starting transfers between devices  32.4 us (31%)
  blocking collectives  30.7 us (29%)
  waiting for transfers between devices  29.5 us (28%)
  Pallas kernels  8.05 us (8%)
  local copies, waits for them, and re-layouts  3.67 us (3%)
    all_to_all x2, waiting for transfers between devices, region_exchange(): got = lax.all_to_all(cut, 'region', split_axis=0, concat_axis=0, tiled=True)  26 us
    all_to_all x2, starting transfers between devices, region_exchange(): got = lax.all_to_all(cut, 'region', split_axis=0, concat_axis=0, tiled=True)  25.6 us
    all_to_all x1, blocking collectives, region_exchange(): got = lax.all_to_all(cut, 'region', split_axis=0, concat_axis=0, tiled=True)  19.8 us
    all_to_all x1, blocking collectives, season_exchange(): lax.all_to_all(value, 'season', split_axis=0, concat_axis=0, tiled=True)  10.9 us
    pallas_call x7, Pallas kernels, call(): pl.pallas_call(body, out_shape=[jax.ShapeDtypeStruct(shape, kind) for sha...  8.05 us
    all_to_all x1, starting transfers between devices, season_exchange(): lax.all_to_all(value, 'season', split_axis=0, concat_axis=0, tiled=True)  6.83 us
    unnamed x44, local copies, waits for them, and re-layouts  3.67 us
    all_to_all x1, waiting for transfers between devices, season_exchange(): lax.all_to_all(value, 'season', split_axis=0, concat_axis=0, tiled=True)  3.5 us
  transfers between devices with their start and end apart: 3, of which 3 were waited for; matrix products, arithmetic and copies ran while one was open for 0% of the time, Pallas kernels for 4%

profile of v1, /device:TPU:1, one launch (start us, length us, event | category | flops | bytes accessed | tf_op | source)
XLA Modules:
  0.0 105.1 jit_solution(3228296411839114360)
XLA Ops:
  0.6 0.0 copy-start.18
  0.6 0.0 copy-start.19
  0.7 0.0 copy-start.17
  0.7 0.0 copy-start.21
  0.7 0.6 copy-done.18
  1.3 0.0 copy-done.19
  1.3 0.0 copy-done.17
  1.3 0.0 copy-done.21
  1.3 0.0 copy-start.2
  1.4 0.8 copy-done.2
  2.1 0.0 copy-start.7
  2.1 0.9 copy-done.7
  3.0 1.4 %shard_map.261 = (bf16[768,128]{1,0:T(8,128)(2,1)}, f32[256,128]{1,0:T(8,128)S(1)}, bf16[256,128]{1,0:T(8,128)(2,1)S(1)}, f32[256,128]{1,0:T(8,128)S(1)}, bf16[256,64]{1,0:T(8,128)(2,1)S(1)}) custom-call(f32[256,128]{1,0:T(8,128)S(1)} %copy-done.7, f32[64,128]{1,0:T(8,128)S(1)} %copy-done.2, s32[2,128]{1,0:T(2,128)S(1)} %bitcast.42, s32[2,128]{1,0:T(2,128)S(1)} %bitcast.43, ...), custom_call_target="tpu_custom_call" | custom-call | tf_op jit(solution)/shard_map/pallas_call | solution.py:367
  4.4 0.0 copy-start
  4.4 0.0 copy-start.1
  4.4 0.0 copy-start.5
  4.4 0.0 copy-start.6
  4.4 19.4 %all-to-all-start.1 = ((bf16[64,3,4,128]{3,2,1,0:T(4,128)(2,1)}), bf16[64,3,4,128]{3,2,1,0:T(4,128)(2,1)S(1)}, u32[]{:S(2)}, u32[]{:S(2)}) async-start(bf16[64,3,4,128]{3,2,1,0:T(4,128)(2,1)} %bitcast.12), calls=%async_computation.1 | async-start | bytes 393216 | tf_op jit(solution)/shard_map/all_to_all | solution.py:379
  23.9 0.0 copy-start.10
  23.9 0.0 copy-done
  23.9 0.0 copy-done.1
  23.9 0.0 copy-done.5
  23.9 0.0 copy-done.6
  23.9 0.6 copy-done.10
  24.5 0.9 shard_map.260
  25.4 0.0 copy-start.3
  25.4 15.1 %all-to-all-done.1 = bf16[64,3,4,128]{3,2,1,0:T(4,128)(2,1)S(1)} async-done(((bf16[64,3,4,128]{3,2,1,0:T(4,128)(2,1)}), bf16[64,3,4,128]{3,2,1,0:T(4,128)(2,1)S(1)}, u32[]{:S(2)}, u32[]{:S(2)}) %all-to-all-start.1) | async-done | bytes 196640 | tf_op jit(solution)/shard_map/all_to_all | solution.py:379
  40.5 6.8 %all-to-all-start = ((f32[8,8,128]{2,1,0:T(8,128)}), f32[8,8,128]{2,1,0:T(8,128)S(1)}, u32[]{:S(2)}, u32[]{:S(2)}) async-start(f32[8,8,128]{2,1,0:T(8,128)} %shard_map.260), calls=%async_computation | async-start | bytes 65536 | tf_op jit(solution)/shard_map/all_to_all | solution.py:384
  47.3 0.0 copy-done.3
  47.3 0.0 copy-start.9
  47.3 1.2 %shard_map.262 = (bf16[256,128]{1,0:T(8,128)(2,1)}, bf16[256,64]{1,0:T(8,128)(2,1)S(1)}, f32[256,128]{1,0:T(8,128)S(1)}) custom-call(bf16[768,128]{1,0:T(8,128)(2,1)S(1)} %bitcast.21, f32[64,128]{1,0:T(8,128)S(1)} %copy-done.3), custom_call_target="tpu_custom_call" | custom-call | tf_op jit(solution)/shard_map/pallas_call | solution.py:367
  48.6 0.0 copy-start.4
  48.6 3.5 %all-to-all-done.got = f32[8,8,128]{2,1,0:T(8,128)S(1)} async-done(((f32[8,8,128]{2,1,0:T(8,128)}), f32[8,8,128]{2,1,0:T(8,128)S(1)}, u32[]{:S(2)}, u32[]{:S(2)}) %all-to-all-start) | async-done | bytes 32800 | tf_op jit(solution)/shard_map/all_to_all | solution.py:384
  52.1 6.2 %all-to-all-start.2 = ((bf16[64,1,4,128]{3,2,1,0:T(4,128)(2,1)}), bf16[64,1,4,128]{3,2,1,0:T(4,128)(2,1)S(1)}, u32[]{:S(2)}, u32[]{:S(2)}) async-start(bf16[64,1,4,128]{3,2,1,0:T(4,128)(2,1)} %bitcast.15), calls=%async_computation.2 | async-start | bytes 131072 | tf_op jit(solution)/shard_map/all_to_all | solution.py:379
  58.3 0.0 copy-start.12
  58.3 0.0 copy-start.13
  58.3 0.0 copy-start.15
  58.3 0.0 copy-start.16
  58.3 0.0 copy-start.20
  58.3 0.0 copy-start.11
  58.3 0.0 copy-start.14
  58.3 0.0 copy-done.9
  58.4 0.0 copy-done.4
  58.4 0.6 copy-done.12
  58.9 0.0 copy-done.13
  59.0 0.0 copy-done.15
  59.0 0.0 copy-done.16
  59.0 0.0 copy-done.20
  59.0 0.0 copy-done.11
  59.0 0.0 copy-done.14
  59.0 0.0 copy-start.8
  59.0 1.9 %shard_map.263 = (f32[256,128]{1,0:T(8,128)S(1)}, f32[2,128]{1,0:T(2,128)S(1)}, f32[64,128]{1,0:T(8,128)S(1)}, f32[64,128]{1,0:T(8,128)S(1)}, f32[256,128]{1,0:T...) custom-call(s32[1]{0:T(128)} %bitcast.season, ...), custom_call_target="tpu_custom_call" | custom-call | tf_op jit(solution)/shard_map/pallas_call | solution.py:367
  60.9 10.8 %all-to-all-done.2 = bf16[64,1,4,128]{3,2,1,0:T(4,128)(2,1)S(1)} async-done(((bf16[64,1,4,128]{3,2,1,0:T(4,128)(2,1)}), bf16[64,1,4,128]{3,2,1,0:T(4,128)(2,1)S(1)}, u32[]{:S(2)}, u32[]{:S(2)}) %all-to-all-start.2) | async-done | bytes 65568 | tf_op jit(solution)/shard_map/all_to_all | solution.py:379
  71.8 0.0 copy-done.8
  71.8 0.6 shard_map.264
  72.4 19.8 %all_to_all.25 = bf16[64,3,4,128]{3,2,1,0:T(4,128)(2,1)S(1)} all-to-all(bf16[64,3,4,128]{3,2,1,0:T(4,128)(2,1)S(1)} %bitcast.26), channel_id=1, replica_groups=mesh['region'=64,'season'=8] {'region'}, dimensions={0} | all-to-all | bytes 393216 | tf_op jit(solution)/shard_map/all_to_all | solution.py:379
  92.3 0.1 shard_map.265
  92.4 10.9 %all_to_all.26.got = f32[8,8,128]{2,1,0:T(8,128)S(1)} all-to-all(f32[8,8,128]{2,1,0:T(8,128)S(1)} %shard_map.265), channel_id=1, replica_groups=mesh['region'=64,'season'=8] {'season'}, dimensions={0} | all-to-all | bytes 65536 | tf_op jit(solution)/shard_map/all_to_all | solution.py:384
  103.3 1.9 %shard_map.266 = (f32[256,128]{1,0:T(8,128)}, f32[2,128]{1,0:T(2,128)}, f32[256,128]{1,0:T(8,128)}, f32[64,128]{1,0:T(8,128)}, f32[64,128]{1,0:T(8,128)}, /*inde...) custom-call(s32[1]{0:T(128)} %bitcast.season, bf16[256,128]{1,0:T(8,128)(2,1)S(1)} %copy-done, ...), custom_call_target="tpu_custom_call" | custom-call | tf_op jit(solution)/shard_map/pallas_call | solution.py:367
Async XLA Ops:
  0.6 0.7 copy-start.18
  0.6 0.7 copy-start.19
  0.7 0.7 copy-start.17
  0.7 0.7 copy-start.21
  1.3 0.8 copy-start.2
  2.1 0.9 copy-start.7
  4.4 19.5 %copy-start = (bf16[256,128]{1,0:T(8,128)(2,1)S(1)}, bf16[256,128]{1,0:T(8,128)(2,1)}, u32[]{:S(2)}) copy-start(bf16[256,128]{1,0:T(8,128)(2,1)} %avail.5) | copy-start | bytes 196612
  4.4 19.5 %copy-start.1 = (f32[256,128]{1,0:T(8,128)S(1)}, f32[256,128]{1,0:T(8,128)}, u32[]{:S(2)}) copy-start(f32[256,128]{1,0:T(8,128)} %scarce.1) | copy-start | bytes 393220
  4.4 19.5 %copy-start.5 = (f32[64,128]{1,0:T(8,128)S(1)}, f32[64,128]{1,0:T(8,128)}, u32[]{:S(2)}) copy-start(f32[64,128]{1,0:T(8,128)} %level.1) | copy-start | bytes 98308
  4.4 19.5 %copy-start.6 = (f32[64,128]{1,0:T(8,128)S(1)}, f32[64,128]{1,0:T(8,128)}, u32[]{:S(2)}) copy-start(f32[64,128]{1,0:T(8,128)} %sdual.1) | copy-start | bytes 98308
  4.4 36.1 %all-to-all-start.1 = ((bf16[64,3,4,128]{3,2,1,0:T(4,128)(2,1)}), bf16[64,3,4,128]{3,2,1,0:T(4,128)(2,1)S(1)}, u32[]{:S(2)}, u32[]{:S(2)}) async-start(bf16[64,3,4,128]{3,2,1,0:T(4,128)(2,1)} %bitcast.12), calls=%async_computation.1 | async-start | bytes 393216 | tf_op jit(solution)/shard_map/all_to_all | solution.py:379
  23.9 0.7 copy-start.10
  25.4 22.0 %copy-start.3 = (f32[64,128]{1,0:T(8,128)S(1)}, f32[64,128]{1,0:T(8,128)}, u32[]{:S(2)}) copy-start(f32[64,128]{1,0:T(8,128)} %price.7) | copy-start | bytes 98308
  40.5 11.5 %all-to-all-start = ((f32[8,8,128]{2,1,0:T(8,128)}), f32[8,8,128]{2,1,0:T(8,128)S(1)}, u32[]{:S(2)}, u32[]{:S(2)}) async-start(f32[8,8,128]{2,1,0:T(8,128)} %shard_map.260), calls=%async_computation | async-start | bytes 65536 | tf_op jit(solution)/shard_map/all_to_all | solution.py:384
  47.3 11.0 %copy-start.9 = (f32[64,128]{1,0:T(8,128)S(1)}, f32[64,128]{1,0:T(8,128)}, u32[]{:S(2)}) copy-start(f32[64,128]{1,0:T(8,128)} %disch.1) | copy-start | bytes 98308
  48.6 9.8 %copy-start.4 = (f32[256,128]{1,0:T(8,128)S(1)}, f32[256,128]{1,0:T(8,128)}, u32[]{:S(2)}) copy-start(f32[256,128]{1,0:T(8,128)} %disp.1) | copy-start | bytes 393220
  52.1 19.7 %all-to-all-start.2 = ((bf16[64,1,4,128]{3,2,1,0:T(4,128)(2,1)}), bf16[64,1,4,128]{3,2,1,0:T(4,128)(2,1)S(1)}, u32[]{:S(2)}, u32[]{:S(2)}) async-start(bf16[64,1,4,128]{3,2,1,0:T(4,128)(2,1)} %bitcast.15), calls=%async_computation.2 | async-start | bytes 131072 | tf_op jit(solution)/shard_map/all_to_all | solution.py:379
  58.3 0.7 copy-start.12
  58.3 0.7 copy-start.13
  58.3 0.7 copy-start.15
  58.3 0.7 copy-start.16
  58.3 0.7 copy-start.20
  58.3 0.7 copy-start.11
  58.3 0.7 copy-start.14
  59.0 12.8 %copy-start.8 = (f32[64,128]{1,0:T(8,128)S(1)}, f32[64,128]{1,0:T(8,128)}, u32[]{:S(2)}) copy-start(f32[64,128]{1,0:T(8,128)} %demand.3) | copy-start | bytes 98308

commit v2 on v1

--- a/solution.py
+++ b/solution.py
@@ -13,6 +13,9 @@
 BF16 = jnp.bfloat16
 I32 = jnp.int32
 REGIONS, SEASONS = 64, 8
+SIDE_Y, SIDE_Z = 4, 16
+Z_GROUPS = [[SIDE_Z * y + z for z in range(SIDE_Z)] for y in range(SIDE_Y)]
+Y_GROUPS = [[SIDE_Z * y + z for y in range(SIDE_Y)] for z in range(SIDE_Z)]
 BUS, SLOT, HOUR = 64, 256, 128
 PACKED = GROUP * PACK
 UNPACKED = 2 * GROUP * LINK_CAP + GROUP
@@ -76,18 +79,31 @@
     )
 
 
+def send_target(packed):
+    q = lax.shift_right_logical(packed * 171, 11)
+    j = packed - PACK * q
+    place = GROUP * (q & 3) + (q & -4)
+    first = place + j
+    second = GROUP * LINK_CAP + place + j - LINK_CAP
+    third = 2 * GROUP * LINK_CAP + q
+    return jnp.where(
+        j < LINK_CAP,
+        first,
+        jnp.where(j < 2 * LINK_CAP, second, jnp.where(j == 2 * LINK_CAP, third, -1)),
+    )
+
+
+def across(value, g):
+    lines = GROUP * LINK_CAP
+    return [value[y * lines + g * GROUP : y * lines + (g + 1) * GROUP] for y in range(SIDE_Y)]
+
+
 def pack(first, second, third, out_ref):
     shape = (PACKED, UNPACKED)
-    place = as_bf(pack_target(iota(shape, 0)) == iota(shape, 1))
-    lines = GROUP * LINK_CAP
+    place = as_bf(send_target(iota(shape, 0)) == iota(shape, 1))
     for g in range(REGIONS // GROUP):
         rows = jnp.concatenate(
-            [
-                first[g * lines : (g + 1) * lines],
-                second[g * lines : (g + 1) * lines],
-                third[g * GROUP : (g + 1) * GROUP],
-            ],
-            axis=0,
+            across(first, g) + across(second, g) + [third[g * GROUP : (g + 1) * GROUP]], axis=0
         )
         out_ref[g * PACKED : (g + 1) * PACKED, :] = narrow(dot(place, rows))
 
@@ -122,7 +138,10 @@
     sent, flow0, near0, cap, leave, turn,
 ):
     lane = iota((1, SLOT), 1)
-    spread = as_bf(iota((REGIONS, SLOT), 0) == lax.shift_right_logical(iota((REGIONS, SLOT), 1), 2))
+    target = iota((REGIONS, SLOT), 0)
+    spread = as_bf(target == lax.shift_right_logical(iota((REGIONS, SLOT), 1), 2))
+    reorder = SIDE_Z * (target & 3) + lax.shift_right_logical(target, 2)
+    sending = as_bf(reorder == lax.shift_right_logical(iota((REGIONS, SLOT), 1), 2))
     counts = jnp.broadcast_to(narrow(wide(link_count[...])), (8, REGIONS))
     counts = dot(counts, spread)[0:1]
     live = jnp.where(wide(lane & (LINK_CAP - 1)) < counts, 1.0, 0.0)
@@ -146,11 +165,11 @@
     slot_kind = iota((SLOT, 128), 0) & (LINK_CAP - 1)
     for at, value in enumerate((wide(row256(line_to)), high, low)):
         spots = as_bf(iota((SLOT, 128), 1) == slot_kind + LINK_CAP * at)
-        held = held + dot(spread * narrow(value), spots)
+        held = held + dot(sending * narrow(value), spots)
     pack(narrow(f0), near, narrow(held), sent)
 
 
-def season_block(sums, level, dual_f, link_column, sent, move_row=None):
+def season_block(sums, level, dual_f, link_column):
     lane = iota((128, 128), 1)
     tail = jnp.concatenate([level[:, HOUR - 1 : HOUR], dual_f[:, HOUR - 1 : HOUR]], axis=0)
     head = jnp.concatenate([dual_f[:, 0:1], link_column], axis=0)
@@ -166,12 +185,12 @@
     turn[0:1, 0:BUS] = wide(link[...])
     turned = columns(turn)
     sums = jnp.sum(wide(avail[...]) * wide(narrow(scarcity[...])), axis=1, keepdims=True)
-    rows = season_block(sums, soc[...], wide(narrow(soc_dual[...])), turned[:BUS, 0:1], sent)
+    rows = season_block(sums, soc[...], wide(narrow(soc_dual[...])), turned[:BUS, 0:1])
     for s in range(SEASONS):
         sent[s] = rows
 
 
-def ends_in(got, price, sent, arrive, cap):
+def ends_in(got, price, sent, far, arrive, cap):
     _, _, held = unpack(got)
     shape = (SLOT, REGIONS)
     spread = as_bf(iota(shape, 1) == lax.shift_right_logical(iota(shape, 0), 2))
@@ -182,7 +201,12 @@
     limits = (lane == kind + LINK_CAP) | (lane == kind + 2 * LINK_CAP)
     limit = jnp.sum(jnp.where(limits, lines, 0.0), axis=1, keepdims=True)
     arrive_t = onehot_rows(ends, BUS)
-    sent[...] = narrow(dot(arrive_t, narrow(price[...])))
+    values = narrow(dot(arrive_t, narrow(price[...])))
+    far[...] = values
+    row = iota((SLOT, SLOT), 0)
+    z = lax.shift_right_logical(row, 4)
+    source = GROUP * LINK_CAP * (lax.shift_right_logical(row, 2) & 3) + LINK_CAP * z + (row & 3)
+    sent[...] = narrow(dot(as_bf(source == iota((SLOT, SLOT), 1)), values))
     arrive[...] = arrive_t
     cap[...] = jnp.broadcast_to(limit, (SLOT, HOUR))
 
@@ -276,7 +300,7 @@
     for ref, value in zip((disp1, build1, disch1, level1, scarce1, sdual1), halves):
         ref[...] = value
     sums = jnp.sum(wide(avail[...]) * wide(narrow(halves[4])), axis=1, keepdims=True)
-    rows[...] = season_block(sums, halves[3], wide(narrow(halves[5])), link_c, None)
+    rows[...] = season_block(sums, halves[3], wide(narrow(halves[5])), link_c)
     primal = (
         square(halves[0], state[0])
         + square(halves[1], state[1]) * (1.0 / SEASONS)
@@ -375,8 +399,11 @@
 
 
 def region_exchange(value, per_pair):
-    cut = value.reshape(REGIONS, per_pair, LINK_CAP, HOUR)
-    got = lax.all_to_all(cut, "region", split_axis=0, concat_axis=0, tiled=True)
+    cut = value.reshape(SIDE_Z, SIDE_Y * per_pair, LINK_CAP, HOUR)
+    came = lax.all_to_all(cut, "region", 0, 0, axis_index_groups=Z_GROUPS, tiled=True)
+    came = came.reshape(SIDE_Z, SIDE_Y, per_pair, LINK_CAP, HOUR).transpose(1, 0, 2, 3, 4)
+    came = came.reshape(SIDE_Y, SIDE_Z * per_pair, LINK_CAP, HOUR)
+    got = lax.all_to_all(came, "region", 0, 0, axis_index_groups=Y_GROUPS, tiled=True)
     return got.reshape(value.shape)
 
 
@@ -441,7 +468,9 @@
     got1 = region_exchange(sent1, 3)
     (rows1,) = call(season_out, [seasons], avail, scarcity, soc, soc_dual, link, turn=True)
     season1 = season_exchange(rows1)
-    sent2, arrive, came_cap = call(ends_in, [lines_b, picks, lines], got1, price)
+    sent2, came_far0, arrive, came_cap = call(
+        ends_in, [lines_b, lines_b, picks, lines], got1, price
+    )
     got2 = region_exchange(sent2, 1)
     disp1, build1, disch1, level1, scarce1, sdual1, came1, balance, rows2, moves = call(
         first_local,
@@ -459,7 +488,7 @@
         got1,
         arrive,
         came_cap,
-        sent2,
+        came_far0,
         scalar=True,
         turn=True,
     )

time: 106 us -> 123 us (1.16)
  blocking collectives: 30.7 us -> 73.2 us
  waiting for transfers between devices: 29.5 us -> 16.7 us
  starting transfers between devices: 32.4 us -> 20.3 us
  Pallas kernels: 8.05 us -> 6.7 us
    all_to_all x1 -> x4, blocking collectives: 19.8 us -> 59.7 us  [the longest x2 43 us: region_exchange(): lax.all_to_all(cut, 'region', 0, 0, axis_index_groups=Z_GROUPS, tiled=True)]
    all_to_all x2, waiting for transfers between devices: 26 us -> 12.7 us  [the longest x1 10 us: region_exchange(): lax.all_to_all(cut, 'region', 0, 0, axis_index_groups=Z_GROUPS, tiled=True)]
    all_to_all x2, starting transfers between devices: 25.6 us -> 12.4 us  [the longest x1 8.94 us: region_exchange(): lax.all_to_all(cut, 'region', 0, 0, axis_index_groups=Z_GROUPS, tiled=True)]
    all_to_all x1, blocking collectives: 10.9 us -> 13.4 us  [season_exchange(): lax.all_to_all(value, 'season', split_axis=0, concat_axis=0, tiled=True)]
    pallas_call x7, Pallas kernels: 8.05 us -> 6.7 us  [call(): pl.pallas_call(body, out_shape=[jax.ShapeDtypeStruct(shape, kind) for sha...]
  transfers between devices with their start and end apart: 3 -> 3, of which waited for: 3 -> 3; matrix products, arithmetic and copies ran while one was open for 0% -> 1% of each run, Pallas kernels for 4% -> 2%
where the time goes in v2:
time: 123 us; the launch traced here: 122 us
  blocking collectives  73.2 us (60%)
  starting transfers between devices  20.3 us (17%)
  waiting for transfers between devices  16.7 us (14%)
  Pallas kernels  6.7 us (5%)
  local copies, waits for them, and re-layouts  4.45 us (4%)
    all_to_all x2, blocking collectives, region_exchange(): lax.all_to_all(cut, 'region', 0, 0, axis_index_groups=Z_GROUPS, tiled=True)  43 us
    all_to_all x2, blocking collectives, region_exchange(): lax.all_to_all(came, 'region', 0, 0, axis_index_groups=Y_GROUPS, tiled=True)  16.7 us
    all_to_all x1, blocking collectives, season_exchange(): lax.all_to_all(value, 'season', split_axis=0, concat_axis=0, tiled=True)  13.4 us
    all_to_all x1, waiting for transfers between devices, region_exchange(): lax.all_to_all(cut, 'region', 0, 0, axis_index_groups=Z_GROUPS, tiled=True)  10 us
    all_to_all x1, starting transfers between devices, region_exchange(): lax.all_to_all(cut, 'region', 0, 0, axis_index_groups=Z_GROUPS, tiled=True)  8.94 us
    all_to_all x1, starting transfers between devices, season_exchange(): lax.all_to_all(value, 'season', split_axis=0, concat_axis=0, tiled=True)  7.91 us
    pallas_call x7, Pallas kernels, call(): pl.pallas_call(body, out_shape=[jax.ShapeDtypeStruct(shape, kind) for sha...  6.7 us
    all_to_all x1, waiting for transfers between devices, season_exchange(): lax.all_to_all(value, 'season', split_axis=0, concat_axis=0, tiled=True)  4.06 us
  transfers between devices with their start and end apart: 3, of which 3 were waited for; matrix products, arithmetic and copies ran while one was open for 1% of the time, Pallas kernels for 2%

profile of v2, /device:TPU:1, one launch (start us, length us, event | category | flops | bytes accessed | tf_op | source)
XLA Modules:
  0.0 122.1 jit_solution(5239551639043385587)
XLA Ops:
  0.6 0.0 copy-start.18
  0.6 0.0 copy-start.19
  0.7 0.0 copy-start.17
  0.7 0.0 copy-start.21
  0.7 0.6 copy-done.18
  1.3 0.0 copy-done.19
  1.3 0.0 copy-done.17
  1.3 0.0 copy-done.21
  1.3 0.0 copy-start.2
  1.4 0.8 copy-done.2
  2.1 0.0 copy-start.7
  2.1 0.9 copy-done.7
  3.0 0.7 shard_map.261
  3.8 28.1 %all_to_all.40 = bf16[16,12,4,128]{3,2,1,0:T(4,128)(2,1)S(1)} all-to-all(bf16[16,12,4,128]{3,2,1,0:T(4,128)(2,1)S(1)} %bitcast.38), channel_id=1, replica_groups={{0,8,16,24,32,40,48,56,64,72,80,88,96,104,112,120},{128,136,144,152,160..., dimensions={0} | all-to-all | bytes 393216 | tf_op jit(solution)/shard_map/all_to_all | solution.py:403
  31.9 0.1 copy.35
  31.9 9.2 %all_to_all.41 = bf16[4,48,4,128]{3,2,1,0:T(4,128)(2,1)S(1)} all-to-all(bf16[4,48,4,128]{3,2,1,0:T(4,128)(2,1)S(1)} %bitcast.59), channel_id=1, replica_groups={{0,128,256,384},{8,136,264,392},{16,144,272,400},{24,152,280,408},{32,1..., dimensions={0} | all-to-all | bytes 393216 | tf_op jit(solution)/shard_map/all_to_all | solution.py:406
  41.1 0.0 copy-start.1
  41.1 1.4 %shard_map.262 = (bf16[256,128]{1,0:T(8,128)(2,1)}, bf16[256,128]{1,0:T(8,128)(2,1)S(1)}, bf16[256,64]{1,0:T(8,128)(2,1)S(1)}, f32[256,128]{1,0:T(8,128)S(1)}) custom-call(bf16[768,128]{1,0:T(8,128)(2,1)S(1)} %bitcast.32, f32[64,128]{1,0:T(8,128)S(1)} %copy-done.2), custom_call_target="tpu_custom_call" | custom-call | tf_op jit(solution)/shard_map/pallas_call | solution.py:391
  42.5 0.0 copy-start
  42.5 0.0 copy-start.5
  42.5 0.0 copy-start.6
  42.5 8.9 %all-to-all-start.3 = ((bf16[16,4,4,128]{3,2,1,0:T(4,128)(2,1)}), bf16[16,4,4,128]{3,2,1,0:T(4,128)(2,1)S(1)}, u32[]{:S(2)}, u32[]{:S(2)}) async-start(bf16[16,4,4,128]{3,2,1,0:T(4,128)(2,1)} %bitcast.17), calls=%async_computation.3 | async-start | bytes 131072 | tf_op jit(solution)/shard_map/all_to_all | solution.py:403
  51.5 0.0 copy-start.10
  51.5 0.0 copy-done.1
  51.5 0.0 copy-done
  51.5 0.0 copy-done.5
  51.5 0.0 copy-done.6
  51.5 0.6 copy-done.10
  52.1 0.9 shard_map.260
  53.0 10.0 %all-to-all-done.3 = bf16[16,4,4,128]{3,2,1,0:T(4,128)(2,1)S(1)} async-done(((bf16[16,4,4,128]{3,2,1,0:T(4,128)(2,1)}), bf16[16,4,4,128]{3,2,1,0:T(4,128)(2,1)S(1)}, u32[]{:S(2)}, u32[]{:S(2)}) %all-to-all-start.3) | async-done | bytes 65568 | tf_op jit(solution)/shard_map/all_to_all | solution.py:403
  63.0 7.9 %all-to-all-start = ((f32[8,8,128]{2,1,0:T(8,128)}), f32[8,8,128]{2,1,0:T(8,128)S(1)}, u32[]{:S(2)}, u32[]{:S(2)}) async-start(f32[8,8,128]{2,1,0:T(8,128)} %shard_map.260), calls=%async_computation | async-start | bytes 65536 | tf_op jit(solution)/shard_map/all_to_all | solution.py:411
  70.9 0.0 copy-start.4
  70.9 0.7 copy.36
  71.6 4.1 %all-to-all-done.got = f32[8,8,128]{2,1,0:T(8,128)S(1)} async-done(((f32[8,8,128]{2,1,0:T(8,128)}), f32[8,8,128]{2,1,0:T(8,128)S(1)}, u32[]{:S(2)}, u32[]{:S(2)}) %all-to-all-start) | async-done | bytes 32800 | tf_op jit(solution)/shard_map/all_to_all | solution.py:411
  75.7 0.0 copy-start.3
  75.7 0.0 copy-start.9
  75.7 3.4 %all-to-all-start.4 = ((bf16[4,16,4,128]{3,2,1,0:T(4,128)(2,1)}), bf16[4,16,4,128]{3,2,1,0:T(4,128)(2,1)S(1)}, u32[]{:S(2)}, u32[]{:S(2)}) async-start(bf16[4,16,4,128]{3,2,1,0:T(4,128)(2,1)} %copy.36), calls=%async_computation.4 | async-start | bytes 131072 | tf_op jit(solution)/shard_map/all_to_all | solution.py:406
  79.1 0.0 copy-start.12
  79.1 0.0 copy-start.13
  79.1 0.0 copy-start.15
  79.1 0.0 copy-start.16
  79.1 0.0 copy-start.20
  79.2 0.0 copy-start.11
  79.2 0.0 copy-start.14
  79.2 0.0 copy-done.4
  79.2 0.0 copy-done.3
  79.2 0.0 copy-done.9
  79.2 0.6 copy-done.12
  79.8 0.0 copy-done.13
  79.8 0.0 copy-done.15
  79.8 0.0 copy-done.16
  79.8 0.0 copy-done.20
  79.8 0.0 copy-done.11
  79.8 0.0 copy-done.14
  79.9 1.1 shard_map.263
  80.9 2.6 %all-to-all-done.4 = bf16[4,16,4,128]{3,2,1,0:T(4,128)(2,1)S(1)} async-done(((bf16[4,16,4,128]{3,2,1,0:T(4,128)(2,1)}), bf16[4,16,4,128]{3,2,1,0:T(4,128)(2,1)S(1)}, u32[]{:S(2)}, u32[]{:S(2)}) %all-to-all-start.4) | async-done | bytes 65568 | tf_op jit(solution)/shard_map/all_to_all | solution.py:406
  83.5 0.0 copy-done.8
  83.5 0.6 shard_map.264
  84.2 14.9 %all_to_all.42 = bf16[16,12,4,128]{3,2,1,0:T(4,128)(2,1)S(1)} all-to-all(bf16[16,12,4,128]{3,2,1,0:T(4,128)(2,1)S(1)} %bitcast.37), channel_id=1, replica_groups={{0,8,16,24,32,40,48,56,64,72,80,88,96,104,112,120},{128,136,144,152,160..., dimensions={0} | all-to-all | bytes 393216 | tf_op jit(solution)/shard_map/all_to_all | solution.py:403
  99.1 0.1 copy.37
  99.2 7.5 %all_to_all.43 = bf16[4,48,4,128]{3,2,1,0:T(4,128)(2,1)S(1)} all-to-all(bf16[4,48,4,128]{3,2,1,0:T(4,128)(2,1)S(1)} %bitcast.61), channel_id=1, replica_groups={{0,128,256,384},{8,136,264,392},{16,144,272,400},{24,152,280,408},{32,1..., dimensions={0} | all-to-all | bytes 393216 | tf_op jit(solution)/shard_map/all_to_all | solution.py:406
  106.7 0.1 shard_map.265
  106.9 13.4 %all_to_all.44.got = f32[8,8,128]{2,1,0:T(8,128)S(1)} all-to-all(f32[8,8,128]{2,1,0:T(8,128)S(1)} %shard_map.265), channel_id=1, replica_groups=mesh['region'=64,'season'=8] {'season'}, dimensions={0} | all-to-all | bytes 65536 | tf_op jit(solution)/shard_map/all_to_all | solution.py:411
  120.3 1.8 %shard_map.266 = (f32[256,128]{1,0:T(8,128)}, f32[2,128]{1,0:T(2,128)}, f32[256,128]{1,0:T(8,128)}, f32[64,128]{1,0:T(8,128)}, f32[64,128]{1,0:T(8,128)}, /*inde...) custom-call(s32[1]{0:T(128)} %bitcast.season, bf16[256,128]{1,0:T(8,128)(2,1)S(1)} %copy-done, ...), custom_call_target="tpu_custom_call" | custom-call | tf_op jit(solution)/shard_map/pallas_call | solution.py:391
  (1 shorter events, 0.0 us)
Async XLA Ops:
  0.6 0.7 copy-start.18
  0.6 0.7 copy-start.19
  0.7 0.7 copy-start.17
  0.7 0.7 copy-start.21
  1.3 0.8 copy-start.2
  2.1 0.9 copy-start.7
  41.1 10.4 %copy-start.1 = (f32[256,128]{1,0:T(8,128)S(1)}, f32[256,128]{1,0:T(8,128)}, u32[]{:S(2)}) copy-start(f32[256,128]{1,0:T(8,128)} %scarce.1) | copy-start | bytes 393220
  42.5 9.0 %copy-start = (bf16[256,128]{1,0:T(8,128)(2,1)S(1)}, bf16[256,128]{1,0:T(8,128)(2,1)}, u32[]{:S(2)}) copy-start(bf16[256,128]{1,0:T(8,128)(2,1)} %avail.5) | copy-start | bytes 196612
  42.5 9.0 %copy-start.5 = (f32[64,128]{1,0:T(8,128)S(1)}, f32[64,128]{1,0:T(8,128)}, u32[]{:S(2)}) copy-start(f32[64,128]{1,0:T(8,128)} %level.1) | copy-start | bytes 98308
  42.5 9.0 %copy-start.6 = (f32[64,128]{1,0:T(8,128)S(1)}, f32[64,128]{1,0:T(8,128)}, u32[]{:S(2)}) copy-start(f32[64,128]{1,0:T(8,128)} %sdual.1) | copy-start | bytes 98308
  42.5 20.5 %all-to-all-start.3 = ((bf16[16,4,4,128]{3,2,1,0:T(4,128)(2,1)}), bf16[16,4,4,128]{3,2,1,0:T(4,128)(2,1)S(1)}, u32[]{:S(2)}, u32[]{:S(2)}) async-start(bf16[16,4,4,128]{3,2,1,0:T(4,128)(2,1)} %bitcast.17), calls=%async_computation.3 | async-start | bytes 131072 | tf_op jit(solution)/shard_map/all_to_all | solution.py:403
  51.5 0.7 copy-start.10
  63.0 12.6 %all-to-all-start = ((f32[8,8,128]{2,1,0:T(8,128)}), f32[8,8,128]{2,1,0:T(8,128)S(1)}, u32[]{:S(2)}, u32[]{:S(2)}) async-start(f32[8,8,128]{2,1,0:T(8,128)} %shard_map.260), calls=%async_computation | async-start | bytes 65536 | tf_op jit(solution)/shard_map/all_to_all | solution.py:411
  70.9 8.2 %copy-start.4 = (f32[256,128]{1,0:T(8,128)S(1)}, f32[256,128]{1,0:T(8,128)}, u32[]{:S(2)}) copy-start(f32[256,128]{1,0:T(8,128)} %disp.1) | copy-start | bytes 393220
  75.7 3.5 %copy-start.3 = (f32[64,128]{1,0:T(8,128)S(1)}, f32[64,128]{1,0:T(8,128)}, u32[]{:S(2)}) copy-start(f32[64,128]{1,0:T(8,128)} %price.7) | copy-start | bytes 98308
  75.7 3.5 %copy-start.9 = (f32[64,128]{1,0:T(8,128)S(1)}, f32[64,128]{1,0:T(8,128)}, u32[]{:S(2)}) copy-start(f32[64,128]{1,0:T(8,128)} %disch.1) | copy-start | bytes 98308
  75.7 7.9 %all-to-all-start.4 = ((bf16[4,16,4,128]{3,2,1,0:T(4,128)(2,1)}), bf16[4,16,4,128]{3,2,1,0:T(4,128)(2,1)S(1)}, u32[]{:S(2)}, u32[]{:S(2)}) async-start(bf16[4,16,4,128]{3,2,1,0:T(4,128)(2,1)} %copy.36), calls=%async_computation.4 | async-start | bytes 131072 | tf_op jit(solution)/shard_map/all_to_all | solution.py:406
  79.1 0.7 copy-start.12
  79.1 0.7 copy-start.13
  79.1 0.7 copy-start.15
  79.1 0.7 copy-start.16
  79.1 0.7 copy-start.20
  79.2 0.7 copy-start.11
  79.2 0.7 copy-start.14
  79.9 3.7 %copy-start.8 = (f32[64,128]{1,0:T(8,128)S(1)}, f32[64,128]{1,0:T(8,128)}, u32[]{:S(2)}) copy-start(f32[64,128]{1,0:T(8,128)} %demand.3) | copy-start | bytes 98308

commit v3 on v1

--- a/solution.py
+++ b/solution.py
@@ -6,7 +6,6 @@
 from jax.sharding import PartitionSpec as P
 
 LINK_CAP = 4
-PACK = 3 * LINK_CAP
 GROUP = 16
 step_size = 0.2
 F32 = jnp.float32
@@ -14,8 +13,9 @@
 I32 = jnp.int32
 REGIONS, SEASONS = 64, 8
 BUS, SLOT, HOUR = 64, 256, 128
-PACKED = GROUP * PACK
-UNPACKED = 2 * GROUP * LINK_CAP + GROUP
+LINES = GROUP * LINK_CAP
+WITH_FLOWS = (LINK_CAP, LINK_CAP, LINK_CAP)
+WITH_MOVES = (LINK_CAP, LINK_CAP, 2)
 
 
 def iota(shape, axis):
@@ -63,46 +63,57 @@
     return jnp.concatenate([ref[0:1, :], ref[1:2, :]], axis=1)
 
 
-def pack_target(packed):
-    q = lax.shift_right_logical(packed * 171, 11)
-    j = packed - PACK * q
+def sizes(kinds):
+    return GROUP * sum(kinds), 2 * LINES + GROUP * (LINK_CAP if kinds[2] == LINK_CAP else 1)
+
+
+def pack_target(packed, kinds):
+    rows = sum(kinds)
+    q = lax.shift_right_logical(packed * (21846 * 12 // rows + 1), 18)
+    j = packed - rows * q
     first = LINK_CAP * q + j
-    second = GROUP * LINK_CAP + LINK_CAP * q + j - LINK_CAP
-    third = 2 * GROUP * LINK_CAP + q
-    return jnp.where(
-        j < LINK_CAP,
-        first,
-        jnp.where(j < 2 * LINK_CAP, second, jnp.where(j == 2 * LINK_CAP, third, -1)),
-    )
-
-
-def pack(first, second, third, out_ref):
-    shape = (PACKED, UNPACKED)
-    place = as_bf(pack_target(iota(shape, 0)) == iota(shape, 1))
-    lines = GROUP * LINK_CAP
+    second = LINES + first - LINK_CAP
+    if kinds[2] == LINK_CAP:
+        third = 2 * LINES + first - 2 * LINK_CAP
+    else:
+        third = jnp.where(j == 2 * LINK_CAP, 2 * LINES + q, -1)
+    return jnp.where(j < LINK_CAP, first, jnp.where(j < 2 * LINK_CAP, second, third))
+
+
+def pack(first, second, third, out_ref, kinds):
+    shape = sizes(kinds)
+    place = as_bf(pack_target(iota(shape, 0), kinds) == iota(shape, 1))
+    thirds = shape[1] - 2 * LINES
     for g in range(REGIONS // GROUP):
         rows = jnp.concatenate(
             [
-                first[g * lines : (g + 1) * lines],
-                second[g * lines : (g + 1) * lines],
-                third[g * GROUP : (g + 1) * GROUP],
+                first[g * LINES : (g + 1) * LINES],
+                second[g * LINES : (g + 1) * LINES],
+                third[g * thirds : (g + 1) * thirds],
             ],
             axis=0,
         )
-        out_ref[g * PACKED : (g + 1) * PACKED, :] = narrow(dot(place, rows))
-
-
-def unpack(ref):
-    shape = (UNPACKED, PACKED)
-    place = as_bf(pack_target(iota(shape, 1)) == iota(shape, 0))
-    parts = [
-        dot(place, ref[g * PACKED : (g + 1) * PACKED, :]) for g in range(REGIONS // GROUP)
-    ]
-    lines = GROUP * LINK_CAP
-    first = jnp.concatenate([p[:lines] for p in parts], axis=0)
-    second = jnp.concatenate([p[lines : 2 * lines] for p in parts], axis=0)
-    third = jnp.concatenate([p[2 * lines :] for p in parts], axis=0)
+        out_ref[g * shape[0] : (g + 1) * shape[0], :] = narrow(dot(place, rows))
+
+
+def unpack(ref, kinds):
+    packed, unpacked = sizes(kinds)
+    shape = (unpacked, packed)
+    place = as_bf(pack_target(iota(shape, 1), kinds) == iota(shape, 0))
+    parts = [dot(place, ref[g * packed : (g + 1) * packed, :]) for g in range(REGIONS // GROUP)]
+    first = jnp.concatenate([p[:LINES] for p in parts], axis=0)
+    second = jnp.concatenate([p[LINES : 2 * LINES] for p in parts], axis=0)
+    third = jnp.concatenate([p[2 * LINES :] for p in parts], axis=0)
     return first, second, third
+
+
+def pieces(value):
+    parts = []
+    for _ in range(3):
+        part = narrow(value)
+        parts.append(part)
+        value = value - wide(part)
+    return parts
 
 
 def columns(ref):
@@ -117,16 +128,31 @@
     return as_bf(column == wide(iota((SLOT, count), 1)))
 
 
-def lines_out(
-    flow, price, line_from, line_to, line_limit, link_count,
-    sent, flow0, near0, cap, leave, turn,
-):
-    lane = iota((1, SLOT), 1)
-    spread = as_bf(iota((REGIONS, SLOT), 0) == lax.shift_right_logical(iota((REGIONS, SLOT), 1), 2))
+def live_limit(line_limit, link_count):
+    shape = (REGIONS, SLOT)
+    spread = as_bf(iota(shape, 0) == lax.shift_right_logical(iota(shape, 1), 2))
     counts = jnp.broadcast_to(narrow(wide(link_count[...])), (8, REGIONS))
     counts = dot(counts, spread)[0:1]
-    live = jnp.where(wide(lane & (LINK_CAP - 1)) < counts, 1.0, 0.0)
-    limit = row256(line_limit) * live
+    kind = iota((1, SLOT), 1) & (LINK_CAP - 1)
+    live = jnp.where(wide(kind) < counts, 1.0, 0.0)
+    return spread, live, row256(line_limit) * live
+
+
+def ends_out(line_to, line_limit, link_count, sent):
+    spread, _, limit = live_limit(line_limit, link_count)
+    lane = iota((SLOT, 128), 1)
+    kind = iota((SLOT, 128), 0) & (LINK_CAP - 1)
+    held = dot(spread * narrow(wide(row256(line_to))), as_bf(lane == kind))
+    spots = as_bf(lane == kind + LINK_CAP)
+    for part in pieces(limit):
+        held = held + dot(spread * part, spots)
+    sent[...] = held
+
+
+def lines_near(
+    flow, price, line_from, line_limit, link_count, flow0, near0, cap, leave, turn
+):
+    _, live, limit = live_limit(line_limit, link_count)
     turn[0:2, :] = wide(line_from[...])
     turn[2:3, :] = live[:, :128]
     turn[3:4, :] = live[:, 128:]
@@ -134,23 +160,13 @@
     turn[5:6, :] = limit[:, 128:]
     turned = columns(turn)
     leave_t = onehot_rows(long_column(turned, 0), BUS)
-    f0 = flow[...] * long_column(turned, 2)
-    near = narrow(dot(leave_t, narrow(price[...])))
-    flow0[...] = f0
-    near0[...] = near
+    flow0[...] = flow[...] * long_column(turned, 2)
+    near0[...] = narrow(dot(leave_t, narrow(price[...])))
     cap[...] = jnp.broadcast_to(long_column(turned, 4), (SLOT, HOUR))
     leave[...] = leave_t
-    high = wide(narrow(limit))
-    low = limit - high
-    held = jnp.zeros((REGIONS, 128), F32)
-    slot_kind = iota((SLOT, 128), 0) & (LINK_CAP - 1)
-    for at, value in enumerate((wide(row256(line_to)), high, low)):
-        spots = as_bf(iota((SLOT, 128), 1) == slot_kind + LINK_CAP * at)
-        held = held + dot(spread * narrow(value), spots)
-    pack(narrow(f0), near, narrow(held), sent)
-
-
-def season_block(sums, level, dual_f, link_column, sent, move_row=None):
+
+
+def season_block(sums, level, dual_f, link_column):
     lane = iota((128, 128), 1)
     tail = jnp.concatenate([level[:, HOUR - 1 : HOUR], dual_f[:, HOUR - 1 : HOUR]], axis=0)
     head = jnp.concatenate([dual_f[:, 0:1], link_column], axis=0)
@@ -166,25 +182,23 @@
     turn[0:1, 0:BUS] = wide(link[...])
     turned = columns(turn)
     sums = jnp.sum(wide(avail[...]) * wide(narrow(scarcity[...])), axis=1, keepdims=True)
-    rows = season_block(sums, soc[...], wide(narrow(soc_dual[...])), turned[:BUS, 0:1], sent)
-    for s in range(SEASONS):
-        sent[s] = rows
-
-
-def ends_in(got, price, sent, arrive, cap):
-    _, _, held = unpack(got)
+    sent[0] = season_block(sums, soc[...], wide(narrow(soc_dual[...])), turned[:BUS, 0:1])
+
+
+def ends_in(got, price, flow0, near0, sent, arrive, cap):
     shape = (SLOT, REGIONS)
     spread = as_bf(iota(shape, 1) == lax.shift_right_logical(iota(shape, 0), 2))
-    lines = dot(spread, narrow(held))
+    high, middle, low = pieces(got[...])
+    lines = dot(spread, high) + dot(spread, middle) + dot(spread, low)
     lane = iota((SLOT, 128), 1)
     kind = iota((SLOT, 128), 0) & (LINK_CAP - 1)
     ends = jnp.sum(jnp.where(lane == kind, lines, 0.0), axis=1, keepdims=True)
-    limits = (lane == kind + LINK_CAP) | (lane == kind + 2 * LINK_CAP)
-    limit = jnp.sum(jnp.where(limits, lines, 0.0), axis=1, keepdims=True)
+    limit = jnp.sum(jnp.where(lane == kind + LINK_CAP, lines, 0.0), axis=1, keepdims=True)
     arrive_t = onehot_rows(ends, BUS)
-    sent[...] = narrow(dot(arrive_t, narrow(price[...])))
+    far = narrow(dot(arrive_t, narrow(price[...])))
     arrive[...] = arrive_t
     cap[...] = jnp.broadcast_to(limit, (SLOT, HOUR))
+    pack(narrow(flow0[...]), near0[...], far, sent, WITH_FLOWS)
 
 
 def line_step(flows, near, far, cap, tau):
@@ -192,14 +206,20 @@
     return moved, extrapolate(moved, flows)
 
 
-def local_step(season, consts, state, price_v, got, turn, tau, sigma):
+def tree(values):
+    while len(values) > 1:
+        values = [values[i] + values[i + 1] for i in range(0, len(values), 2)]
+    return values[0]
+
+
+def local_step(season, consts, state, price_v, got, turn, tau, sigma, paired):
     avail, asset_bus, run_cost, build_cost, efficiency, power, energy, link = consts
     disp, build, disch, level, scarce, sdual = state
     before_at = (season + SEASONS - 1) & (SEASONS - 1)
     after_at = (season + 1) & (SEASONS - 1)
-    sums = got[0, 0:2]
-    for s in range(1, SEASONS):
-        sums = sums + got[s, 0:2]
+    if paired:
+        before_at, after_at = before_at ^ season, after_at ^ season
+    sums = tree([got[s, 0:2] for s in range(SEASONS)])
     grad_build = sums * (1.0 / (HOUR * SEASONS))
     build_new = jnp.maximum(build - tau * (build_cost[...] - grad_build), 0.0)
     turn[0:8, :] = got[before_at]
@@ -261,22 +281,19 @@
 
 def first_local(
     season, avail, asset_bus, run_cost, build_cost, efficiency, power, energy, link,
-    disp, build, disch, level, scarce, sdual, price, got, lines_got, arrive, cap, far,
-    disp1, build1, disch1, level1, scarce1, sdual1, came1, balance, rows, moves, turn,
+    disp, build, disch, level, scarce, sdual, price, got,
+    disp1, build1, disch1, level1, scarce1, sdual1, balance, rows, moves, turn,
 ):
     consts = (avail, asset_bus, run_cost, build_cost, efficiency, power, energy, link)
     state = (disp[...], build[...], disch[...], level[...], scarce[...], sdual[...])
-    came0, near, _ = unpack(lines_got)
-    moved, came_x = line_step(came0, near, wide(far[...]), cap[...], step_size)
-    came1[...] = mean(moved, came0)
     local, halves, link_c = local_step(
-        season[0], consts, state, price[...], got, turn, step_size, step_size
-    )
-    balance[...] = local + dot_t(arrive[...], came_x)
+        season[0], consts, state, price[...], got, turn, step_size, step_size, True
+    )
+    balance[...] = local
     for ref, value in zip((disp1, build1, disch1, level1, scarce1, sdual1), halves):
         ref[...] = value
     sums = jnp.sum(wide(avail[...]) * wide(narrow(halves[4])), axis=1, keepdims=True)
-    rows[...] = season_block(sums, halves[3], wide(narrow(halves[5])), link_c, None)
+    rows[...] = season_block(sums, halves[3], wide(narrow(halves[5])), link_c)
     primal = (
         square(halves[0], state[0])
         + square(halves[1], state[1]) * (1.0 / SEASONS)
@@ -289,16 +306,21 @@
 
 
 def price_step(
-    flow0, near0, cap, leave, arrive, got, demand, price, balance, moves,
-    price1, flow1, far0, sent,
+    flow0, near0, cap, leave, arrive, came_cap, got, demand, price, balance, moves,
+    price1, flow1, came1, far1, sent,
 ):
     f0 = flow0[...]
+    p0 = price[...]
     leave_t = leave[...]
-    moved, flow_x = line_step(f0, wide(near0[...]), wide(got[...]), cap[...], step_size)
+    arrive_t = arrive[...]
+    came0, came_near, far = unpack(got, WITH_FLOWS)
+    came_far = dot(arrive_t, narrow(p0))
+    came_moved, came_x = line_step(came0, came_near, came_far, came_cap[...], step_size)
+    came1[...] = mean(came_moved, came0)
+    moved, flow_x = line_step(f0, wide(near0[...]), far, cap[...], step_size)
     f1 = mean(moved, f0)
     flow1[...] = f1
-    p0 = price[...]
-    whole = balance[...] - dot_t(leave_t, flow_x)
+    whole = balance[...] + dot_t(arrive_t, came_x) - dot_t(leave_t, flow_x)
     p1 = mean(p0 + step_size * (demand[...] - whole), p0)
     price1[...] = p1
     primal = moves[0:1, 0:1] + square(f1, f0)
@@ -306,23 +328,22 @@
     lane = iota((GROUP, 128), 1)
     held = jnp.zeros((GROUP, 128), F32)
     for at, value in ((0, primal), (3, dual)):
-        for step in range(3):
-            piece = wide(narrow(value))
-            held = jnp.where(lane == at + step, piece, held)
-            value = value - piece
+        for step, piece in enumerate(pieces(value)):
+            held = jnp.where(lane == at + step, wide(piece), held)
     held = narrow(held)
     price_b = narrow(p1)
     near = narrow(dot(leave_t, price_b))
-    far = narrow(dot(arrive[...], price_b))
-    far0[...] = far
-    pack(near, far, jnp.concatenate([held] * (REGIONS // GROUP), axis=0), sent)
+    far = narrow(dot(arrive_t, price_b))
+    far1[...] = far
+    pack(near, far, jnp.concatenate([held] * (REGIONS // GROUP), axis=0), sent, WITH_MOVES)
 
 
 def moves_out(got, rows, sent):
-    shape = (8, REGIONS * PACK)
+    rows_each = sum(WITH_MOVES)
+    shape = (8, REGIONS * rows_each)
     at = iota(shape, 1)
-    q = lax.shift_right_logical(at * 21846, 18)
-    mask = as_bf(at - PACK * q == 2 * LINK_CAP)
+    q = lax.shift_right_logical(at * (262144 // rows_each + 1), 18)
+    mask = as_bf(at - rows_each * q == 2 * LINK_CAP)
     moves = dot(mask, got[...])
     held = jnp.where(iota((8, 128), 0) == 4, moves, rows[...])
     for s in range(SEASONS):
@@ -335,9 +356,7 @@
     came_far, came, demand, flow, cap, leave,
     disp2, build2, flow2, disch2, level2, price2, scarce2, sdual2, turn,
 ):
-    moves = got[0, 4:5]
-    for s in range(1, SEASONS):
-        moves = moves + got[s, 4:5]
+    moves = tree([got[s, 4:5] for s in range(SEASONS)])
     primal = moves[:, 0:1] + moves[:, 1:2] + moves[:, 2:3]
     dual = moves[:, 3:4] + moves[:, 4:5] + moves[:, 5:6]
     weight = jnp.sqrt(jnp.sqrt((dual + 1e-06) / (primal + 1e-06)))
@@ -345,7 +364,7 @@
     sigma = step_size * weight
     consts = (avail, asset_bus, run_cost, build_cost, efficiency, power, energy, link)
     state = (disp[...], build[...], disch[...], level[...], scarce[...], sdual[...])
-    came_near, far, _ = unpack(lines_got)
+    came_near, far, _ = unpack(lines_got, WITH_MOVES)
     _, came_x = line_step(came[...], came_near, wide(came_far[...]), came_cap[...], tau)
     f1 = flow[...]
     p1 = price[...]
@@ -353,7 +372,7 @@
     near = dot(leave_t, narrow(p1))
     moved, flow_x = line_step(f1, near, far, cap[...], tau)
     flow2[...] = mean(moved, f1)
-    local, halves, _ = local_step(season[0], consts, state, p1, got, turn, tau, sigma)
+    local, halves, _ = local_step(season[0], consts, state, p1, got, turn, tau, sigma, False)
     whole = local + dot_t(arrive[...], came_x) - dot_t(leave_t, flow_x)
     price2[...] = mean(p1 + sigma * (demand[...] - whole), p1)
     for ref, value in zip((disp2, build2, disch2, level2, scarce2, sdual2), halves):
@@ -374,14 +393,23 @@
     )(*operands)
 
 
-def region_exchange(value, per_pair):
-    cut = value.reshape(REGIONS, per_pair, LINK_CAP, HOUR)
+def region_exchange(value, rows, per_pair):
+    cut = value.reshape(REGIONS, per_pair, rows, HOUR)
     got = lax.all_to_all(cut, "region", split_axis=0, concat_axis=0, tiled=True)
     return got.reshape(value.shape)
 
 
 def season_exchange(value):
     return lax.all_to_all(value, "season", split_axis=0, concat_axis=0, tiled=True)
+
+
+def season_gather(value):
+    apart = 1
+    while apart < SEASONS:
+        pairs = [(s, s ^ apart) for s in range(SEASONS)]
+        value = jnp.concatenate([value, lax.ppermute(value, "season", pairs)], axis=0)
+        apart *= 2
+    return value
 
 
 def on_device(
@@ -415,8 +443,9 @@
     lines_b = ((SLOT, HOUR), BF16)
     buses = ((BUS, HOUR), F32)
     picks = ((SLOT, BUS), BF16)
-    packed = ((REGIONS * PACK, HOUR), BF16)
+    rows_of = lambda kinds: ((REGIONS * sum(kinds), HOUR), BF16)
     seasons = ((SEASONS, 8, 128), F32)
+    pack_row = ((8, 128), F32)
     consts = (
         avail,
         pair(asset_bus),
@@ -427,25 +456,31 @@
         short(energy_limit),
         link,
     )
-    sent1, flow0, near0, cap, leave = call(
-        lines_out,
-        [packed, lines, lines_b, lines, picks],
+    limit = pair(line_limit)
+    (sent1,) = call(ends_out, [((REGIONS, 128), F32)], pair(line_to), limit, link_count)
+    got1 = region_exchange(sent1, 1, 1)
+    (rows1,) = call(
+        season_out, [((1, 8, 128), F32)], avail, scarcity, soc, soc_dual, link, turn=True
+    )
+    season1 = season_gather(rows1)
+    flow0, near0, cap, leave = call(
+        lines_near,
+        [lines, lines_b, lines, picks],
         flow,
         price,
         pair(line_from),
-        pair(line_to),
-        pair(line_limit),
+        limit,
         link_count,
         turn=True,
     )
-    got1 = region_exchange(sent1, 3)
-    (rows1,) = call(season_out, [seasons], avail, scarcity, soc, soc_dual, link, turn=True)
-    season1 = season_exchange(rows1)
-    sent2, arrive, came_cap = call(ends_in, [lines_b, picks, lines], got1, price)
-    got2 = region_exchange(sent2, 1)
-    disp1, build1, disch1, level1, scarce1, sdual1, came1, balance, rows2, moves = call(
+    got1, season1 = lax.optimization_barrier((got1, season1))
+    sent2, arrive, came_cap = call(
+        ends_in, [rows_of(WITH_FLOWS), picks, lines], got1, price, flow0, near0
+    )
+    got2 = region_exchange(sent2, LINK_CAP, 3)
+    disp1, build1, disch1, level1, scarce1, sdual1, balance, rows2, moves = call(
         first_local,
-        [lines, ((2, 128), F32), buses, buses, lines, buses, lines, buses, ((8, 128), F32), ((8, 128), F32)],
+        [lines, ((2, 128), F32), buses, buses, lines, buses, buses, pack_row, pack_row],
         season,
         *consts,
         dispatch,
@@ -456,28 +491,25 @@
         soc_dual,
         price,
         season1,
-        got1,
-        arrive,
-        came_cap,
-        sent2,
         scalar=True,
         turn=True,
     )
-    price1, flow1, came_far1, sent3 = call(
+    price1, flow1, came1, came_far1, sent3 = call(
         price_step,
-        [buses, lines, lines_b, packed],
+        [buses, lines, lines, lines_b, rows_of(WITH_MOVES)],
         flow0,
         near0,
         cap,
         leave,
         arrive,
+        came_cap,
         got2,
         demand,
         price,
         balance,
         moves,
     )
-    got3 = region_exchange(sent3, 3)
+    got3 = region_exchange(sent3, 2, 5)
     (rows3,) = call(moves_out, [seasons], got3, rows2)
     season2 = season_exchange(rows3)
     disp2, build2, flow2, disch2, level2, price2, scarce2, sdual2 = call(

time: 106 us -> 109 us (1.028)
  blocking collectives: 30.7 us -> 33.4 us
  local copies, waits for them, and re-layouts: 3.67 us -> 5.9 us
  waiting for transfers between devices: 29.5 us -> 28 us
  Pallas kernels: 8.05 us -> 6.87 us
    ppermute x0 -> x3, starting transfers between devices: none -> 12.7 us  [season_gather(): lax.ppermute(value, 'season', pairs)]
    all_to_all x1 -> x0, starting transfers between devices: 6.83 us -> none  [season_exchange(): lax.all_to_all(value, 'season', split_axis=0, concat_axis=0, tiled=True)]
    all_to_all x2, starting transfers between devices: 25.6 us -> 20.7 us  [region_exchange(): got = lax.all_to_all(cut, 'region', split_axis=0, concat_axis=0, tiled=True)]
    all_to_all x1 -> x0, waiting for transfers between devices: 3.5 us -> none  [season_exchange(): lax.all_to_all(value, 'season', split_axis=0, concat_axis=0, tiled=True)]
    ppermute x0 -> x3, waiting for transfers between devices: none -> 3.27 us  [season_gather(): lax.ppermute(value, 'season', pairs)]
    unnamed x44 -> x50, local copies, waits for them, and re-layouts: 3.67 us -> 5.9 us
    all_to_all x1, blocking collectives: 19.8 us -> 21.4 us  [region_exchange(): got = lax.all_to_all(cut, 'region', split_axis=0, concat_axis=0, tiled=True)]
    all_to_all x2, waiting for transfers between devices: 26 us -> 24.8 us  [region_exchange(): got = lax.all_to_all(cut, 'region', split_axis=0, concat_axis=0, tiled=True)]
  transfers between devices with their start and end apart: 3 -> 5, of which waited for: 3 -> 4; matrix products, arithmetic and copies ran while one was open for 0% -> 0% of each run, Pallas kernels for 4% -> 2%
where the time goes in v3:
time: 109 us
  starting transfers between devices  33.4 us (31%)
  blocking collectives  33.4 us (31%)
  waiting for transfers between devices  28 us (26%)
  Pallas kernels  6.87 us (6%)
  local copies, waits for them, and re-layouts  5.9 us (5%)
    all_to_all x2, waiting for transfers between devices, region_exchange(): got = lax.all_to_all(cut, 'region', split_axis=0, concat_axis=0, tiled=True)  24.8 us
    all_to_all x1, blocking collectives, region_exchange(): got = lax.all_to_all(cut, 'region', split_axis=0, concat_axis=0, tiled=True)  21.4 us
    all_to_all x2, starting transfers between devices, region_exchange(): got = lax.all_to_all(cut, 'region', split_axis=0, concat_axis=0, tiled=True)  20.7 us
    ppermute x3, starting transfers between devices, season_gather(): lax.ppermute(value, 'season', pairs)  12.7 us
    all_to_all x1, blocking collectives, season_exchange(): lax.all_to_all(value, 'season', split_axis=0, concat_axis=0, tiled=True)  12 us
    pallas_call x8, Pallas kernels, call(): pl.pallas_call(body, out_shape=[jax.ShapeDtypeStruct(shape, kind) for sha...  6.87 us
    unnamed x50, local copies, waits for them, and re-layouts  5.9 us
    ppermute x3, waiting for transfers between devices, season_gather(): lax.ppermute(value, 'season', pairs)  3.27 us
  transfers between devices with their start and end apart: 5, of which 4 were waited for; matrix products, arithmetic and copies ran while one was open for 0% of the time, Pallas kernels for 2%

profile of v3, /device:TPU:1, one launch (start us, length us, event | category | flops | bytes accessed | tf_op | source)
XLA Modules:
  0.0 108.5 jit_solution(15351675573459707649)
XLA Ops:
  0.6 0.0 copy-start.13
  0.6 0.6 copy-done.13
  1.3 0.0 copy-start
  1.3 0.8 copy-done
  2.1 0.0 copy-start.3
  2.1 0.9 copy-done.3
  3.0 0.0 copy-start.8
  3.0 0.8 copy-done.8
  3.8 0.0 copy-start.10
  3.8 0.8 copy-done.10
  4.6 0.0 copy-start.7
  4.6 0.2 shard_map.261
  4.8 8.8 %collective-permute-start = (f32[1,8,128]{2,1,0:T(8,128)S(1)}, f32[1,8,128]{2,1,0:T(8,128)S(1)}, u32[]{:S(2)}, u32[]{:S(2)}) collective-permute-start(f32[1,8,128]{2,1,0:T(8,128)S(1)} %shard_map.261), channel_id=1, source_target_pairs={{0,1},{1,0},{2,3},{3,2},{4,5},{5,4},{6,7},{7,6},{8,9},{9,8},{10,11... | collective-permute-start | bytes 12296 | tf_op jit(solution)/shard_map/ppermute | solution.py:410
  13.6 0.8 collective-permute-done
  14.4 1.9 %collective-permute-start.1 = (f32[2,8,128]{2,1,0:T(8,128)S(1)}, f32[2,8,128]{2,1,0:T(8,128)S(1)}, u32[]{:S(2)}, u32[]{:S(2)}) collective-permute-start(f32[2,8,128]{2,1,0:T(8,128)S(1)} %pad_maximum_fusion.2), channel_id=1, source_target_pairs={{0,2},{1,3},{2,0},{3,1},{4,6},{5,7},{6,4},{7,5},{8,10},{9,11},{10,... | collective-permute-start | bytes 24584 | tf_op jit(solution)/shard_map/ppermute | solution.py:410
  16.3 2.5 %collective-permute-done.1 = f32[2,8,128]{2,1,0:T(8,128)S(1)} collective-permute-done((f32[2,8,128]{2,1,0:T(8,128)S(1)}, f32[2,8,128]{2,1,0:T(8,128)S(1)}, u32[]{:S(2)}, u32[]{:S(2)}) %collective-permute-start.1) | collective-permute-done | bytes 8224 | tf_op jit(solution)/shard_map/ppermute | solution.py:410
  18.8 0.0 copy-start.23
  18.8 2.0 %collective-permute-start.2 = (f32[4,8,128]{2,1,0:T(8,128)S(1)}, f32[4,8,128]{2,1,0:T(8,128)S(1)}, u32[]{:S(2)}, u32[]{:S(2)}) collective-permute-start(f32[4,8,128]{2,1,0:T(8,128)S(1)} %pad_maximum_fusion.1), channel_id=1, source_target_pairs={{0,4},{1,5},{2,6},{3,7},{4,0},{5,1},{6,2},{7,3},{8,12},{9,13},{10,... | collective-permute-start | bytes 49160 | tf_op jit(solution)/shard_map/ppermute | solution.py:410
  20.8 0.0 copy-start.17
  20.8 0.0 copy-start.21
  20.9 0.0 copy-done.23
  20.9 0.6 copy-done.17
  21.5 0.0 copy-done.21
  21.5 0.9 shard_map.260
  22.4 0.0 copy-start.2
  22.4 15.9 %all-to-all-start = ((f32[64,1,1,128]{3,2,1,0:T(1,128)}), f32[64,1,1,128]{3,2,1,0:T(1,128)S(1)}, u32[]{:S(2)}, u32[]{:S(2)}) async-start(f32[64,1,1,128]{3,2,1,0:T(1,128)} %bitcast.12), calls=%async_computation | async-start | bytes 65536 | tf_op jit(solution)/shard_map/all_to_all | solution.py:398
  38.4 0.0 copy-start.24
  38.4 0.0 copy-done.7
  38.4 0.0 copy-done.2
  38.4 0.7 copy-done.24
  39.1 0.5 shard_map.263
  39.5 0.0 collective-permute-done.2
  39.6 12.0 %all-to-all-done = f32[64,1,1,128]{3,2,1,0:T(1,128)S(1)} async-done(((f32[64,1,1,128]{3,2,1,0:T(1,128)}), f32[64,1,1,128]{3,2,1,0:T(1,128)S(1)}, u32[]{:S(2)}, u32[]{:S(2)}) %all-to-all-start) | async-done | bytes 32800 | tf_op jit(solution)/shard_map/all_to_all | solution.py:398
  51.6 1.3 %shard_map.264 = (bf16[768,128]{1,0:T(8,128)(2,1)}, bf16[256,64]{1,0:T(8,128)(2,1)S(1)}, f32[256,128]{1,0:T(8,128)S(1)}) custom-call(f32[64,128]{1,0:T(8,128)S(1)} %bitcast.25, f32[64,128]{1,0:T(8,128)S(1)} %copy-done.2, f32[256,128]{1,0:T(8,128)S(1)} %get-tuple-element.46.flow0, bf16[256,128]{1,0:T(8,128)(2,1)S(1)} %get-tuple-element.47.near0), custom_call_target="tpu_custom_call" | custom-call | tf_op jit(solution)/shard_map/pallas_call | solution.py:386
  52.9 0.0 copy-start.11
  52.9 4.8 %all-to-all-start.1 = ((bf16[64,3,4,128]{3,2,1,0:T(4,128)(2,1)}), bf16[64,3,4,128]{3,2,1,0:T(4,128)(2,1)S(1)}, u32[]{:S(2)}, u32[]{:S(2)}) async-start(bf16[64,3,4,128]{3,2,1,0:T(4,128)(2,1)} %bitcast.15), calls=%async_computation.1 | async-start | bytes 393216 | tf_op jit(solution)/shard_map/all_to_all | solution.py:398
  57.7 0.0 copy-start.15
  57.7 0.0 copy-start.16
  57.7 0.0 copy-start.19
  57.8 0.0 copy-start.20
  57.8 0.0 copy-start.22
  57.8 0.0 copy-start.14
  57.8 0.0 copy-start.18
  57.8 0.0 copy-done.12
  57.8 0.0 copy-done.1
  57.8 0.0 copy-done.4
  57.8 0.0 copy-done.6
  57.8 0.0 copy-done.9
  57.8 0.0 copy-done.11
  57.9 0.5 copy-done.15
  58.4 0.0 copy-done.16
  58.4 0.0 copy-done.19
  58.4 0.0 copy-done.20
  58.4 0.0 copy-done.22
  58.5 0.0 copy-done.14
  58.5 0.0 copy-done.18
  58.5 1.0 shard_map.262
  59.5 12.7 %all-to-all-done.1 = bf16[64,3,4,128]{3,2,1,0:T(4,128)(2,1)S(1)} async-done(((bf16[64,3,4,128]{3,2,1,0:T(4,128)(2,1)}), bf16[64,3,4,128]{3,2,1,0:T(4,128)(2,1)S(1)}, u32[]{:S(2)}, u32[]{:S(2)}) %all-to-all-start.1) | async-done | bytes 196640 | tf_op jit(solution)/shard_map/all_to_all | solution.py:398
  72.2 0.0 copy-done.5
  72.2 0.9 shard_map.265
  73.1 21.4 %all_to_all.20 = bf16[64,5,2,128]{3,2,1,0:T(2,128)(2,1)S(1)} all-to-all(bf16[64,5,2,128]{3,2,1,0:T(2,128)(2,1)S(1)} %bitcast.24), channel_id=1, replica_groups=mesh['region'=64,'season'=8] {'region'}, dimensions={0} | all-to-all | bytes 327680 | tf_op jit(solution)/shard_map/all_to_all | solution.py:398
  94.5 0.1 shard_map.266
  94.7 12.0 %all_to_all.21.got = f32[8,8,128]{2,1,0:T(8,128)S(1)} all-to-all(f32[8,8,128]{2,1,0:T(8,128)S(1)} %shard_map.266), channel_id=1, replica_groups=mesh['region'=64,'season'=8] {'season'}, dimensions={0} | all-to-all | bytes 65536 | tf_op jit(solution)/shard_map/all_to_all | solution.py:403
  106.7 1.8 %shard_map.267 = (f32[256,128]{1,0:T(8,128)}, f32[2,128]{1,0:T(2,128)}, f32[256,128]{1,0:T(8,128)}, f32[64,128]{1,0:T(8,128)}, f32[64,128]{1,0:T(8,128)}, /*inde...) custom-call(s32[1]{0:T(128)} %bitcast.season, bf16[256,128]{1,0:T(8,128)(2,1)S(1)} %copy-done.1, ...), custom_call_target="tpu_custom_call" | custom-call | tf_op jit(solution)/shard_map/pallas_call | solution.py:386
  (9 shorter events, 0.0 us)
Async XLA Ops:
  0.6 0.7 copy-start.13
  1.3 0.8 copy-start
  2.1 0.9 copy-start.3
  3.0 0.8 copy-start.8
  3.8 0.8 copy-start.10
  4.6 33.8 %copy-start.7 = (f32[256,128]{1,0:T(8,128)S(1)}, f32[256,128]{1,0:T(8,128)}, u32[]{:S(2)}) copy-start(f32[256,128]{1,0:T(8,128)} %flow.1) | copy-start | bytes 393220
  4.8 9.6 %collective-permute-start = (f32[1,8,128]{2,1,0:T(8,128)S(1)}, f32[1,8,128]{2,1,0:T(8,128)S(1)}, u32[]{:S(2)}, u32[]{:S(2)}) collective-permute-start(f32[1,8,128]{2,1,0:T(8,128)S(1)} %shard_map.261), channel_id=1, source_target_pairs={{0,1},{1,0},{2,3},{3,2},{4,5},{5,4},{6,7},{7,6},{8,9},{9,8},{10,11... | collective-permute-start | bytes 12296 | tf_op jit(solution)/shard_map/ppermute | solution.py:410
  14.4 4.4 %collective-permute-start.1 = (f32[2,8,128]{2,1,0:T(8,128)S(1)}, f32[2,8,128]{2,1,0:T(8,128)S(1)}, u32[]{:S(2)}, u32[]{:S(2)}) collective-permute-start(f32[2,8,128]{2,1,0:T(8,128)S(1)} %pad_maximum_fusion.2), channel_id=1, source_target_pairs={{0,2},{1,3},{2,0},{3,1},{4,6},{5,7},{6,4},{7,5},{8,10},{9,11},{10,... | collective-permute-start | bytes 24584 | tf_op jit(solution)/shard_map/ppermute | solution.py:410
  18.8 2.1 %copy-start.23 = (s32[256]{0:T(256)S(1)}, s32[256]{0:T(256)}, u32[]{:S(2)}) copy-start(s32[256]{0:T(256)} %param.27) | copy-start | bytes 3076
  18.8 20.8 %collective-permute-start.2 = (f32[4,8,128]{2,1,0:T(8,128)S(1)}, f32[4,8,128]{2,1,0:T(8,128)S(1)}, u32[]{:S(2)}, u32[]{:S(2)}) collective-permute-start(f32[4,8,128]{2,1,0:T(8,128)S(1)} %pad_maximum_fusion.1), channel_id=1, source_target_pairs={{0,4},{1,5},{2,6},{3,7},{4,0},{5,1},{6,2},{7,3},{8,12},{9,13},{10,... | collective-permute-start | bytes 49160 | tf_op jit(solution)/shard_map/ppermute | solution.py:410
  20.8 0.7 copy-start.17
  20.8 0.7 copy-start.21
  22.4 16.0 %copy-start.2 = (f32[64,128]{1,0:T(8,128)S(1)}, f32[64,128]{1,0:T(8,128)}, u32[]{:S(2)}) copy-start(f32[64,128]{1,0:T(8,128)} %price.7) | copy-start | bytes 98308
  22.4 29.2 %all-to-all-start = ((f32[64,1,1,128]{3,2,1,0:T(1,128)}), f32[64,1,1,128]{3,2,1,0:T(1,128)S(1)}, u32[]{:S(2)}, u32[]{:S(2)}) async-start(f32[64,1,1,128]{3,2,1,0:T(1,128)} %bitcast.12), calls=%async_computation | async-start | bytes 65536 | tf_op jit(solution)/shard_map/all_to_all | solution.py:398
  38.4 0.7 copy-start.24
  51.6 6.2 %copy-start.12 = (f32[64,128]{1,0:T(8,128)S(1)}, f32[64,128]{1,0:T(8,128)}, u32[]{:S(2)}) copy-start(f32[64,128]{1,0:T(8,128)} %disch.1) | copy-start | bytes 98308
  52.9 4.9 %copy-start.1 = (bf16[256,128]{1,0:T(8,128)(2,1)S(1)}, bf16[256,128]{1,0:T(8,128)(2,1)}, u32[]{:S(2)}) copy-start(bf16[256,128]{1,0:T(8,128)(2,1)} %avail.5) | copy-start | bytes 196612
  52.9 4.9 %copy-start.4 = (f32[256,128]{1,0:T(8,128)S(1)}, f32[256,128]{1,0:T(8,128)}, u32[]{:S(2)}) copy-start(f32[256,128]{1,0:T(8,128)} %scarce.1) | copy-start | bytes 393220
  52.9 4.9 %copy-start.6 = (f32[256,128]{1,0:T(8,128)S(1)}, f32[256,128]{1,0:T(8,128)}, u32[]{:S(2)}) copy-start(f32[256,128]{1,0:T(8,128)} %disp.1) | copy-start | bytes 393220
  52.9 4.9 %copy-start.9 = (f32[64,128]{1,0:T(8,128)S(1)}, f32[64,128]{1,0:T(8,128)}, u32[]{:S(2)}) copy-start(f32[64,128]{1,0:T(8,128)} %level.1) | copy-start | bytes 98308
  52.9 4.9 %copy-start.11 = (f32[64,128]{1,0:T(8,128)S(1)}, f32[64,128]{1,0:T(8,128)}, u32[]{:S(2)}) copy-start(f32[64,128]{1,0:T(8,128)} %sdual.1) | copy-start | bytes 98308
  52.9 19.3 %all-to-all-start.1 = ((bf16[64,3,4,128]{3,2,1,0:T(4,128)(2,1)}), bf16[64,3,4,128]{3,2,1,0:T(4,128)(2,1)S(1)}, u32[]{:S(2)}, u32[]{:S(2)}) async-start(bf16[64,3,4,128]{3,2,1,0:T(4,128)(2,1)} %bitcast.15), calls=%async_computation.1 | async-start | bytes 393216 | tf_op jit(solution)/shard_map/all_to_all | solution.py:398
  57.7 0.7 copy-start.15
  57.7 0.7 copy-start.16
  57.7 0.7 copy-start.19
  57.8 0.7 copy-start.20
  57.8 0.7 copy-start.22
  57.8 0.7 copy-start.14
  57.8 0.7 copy-start.18
  58.5 13.8 %copy-start.5 = (f32[64,128]{1,0:T(8,128)S(1)}, f32[64,128]{1,0:T(8,128)}, u32[]{:S(2)}) copy-start(f32[64,128]{1,0:T(8,128)} %demand.3) | copy-start | bytes 98308

commit v4 on v3

--- a/solution.py
+++ b/solution.py
@@ -138,27 +138,91 @@
     return spread, live, row256(line_limit) * live
 
 
-def ends_out(line_to, line_limit, link_count, sent):
-    spread, _, limit = live_limit(line_limit, link_count)
+def field_times(season, value):
+    product = (
+        (season & 1) * value
+        ^ (lax.shift_right_logical(season, 1) & 1) * (value << 1)
+        ^ (lax.shift_right_logical(season, 2) & 1) * (value << 2)
+    )
+    product = product ^ ((lax.shift_right_logical(product, 4) & 1) * 22)
+    return product ^ ((lax.shift_right_logical(product, 3) & 1) * 11)
+
+
+def step_of(season):
+    return jnp.where(season == SEASONS - 1, 1, season + 1)
+
+
+def coset_of(season, region):
+    high, low = lax.shift_right_logical(region, 3), region & 7
+    offset = low ^ field_times(season, high)
+    return high, offset, jnp.minimum(offset, offset ^ step_of(season))
+
+
+def coset_groups():
+    def times(a, b):
+        product = 0
+        for bit in range(3):
+            product ^= (b << bit) * ((a >> bit) & 1)
+        for bit in (4, 3):
+            product ^= (0b1011 << (bit - 3)) * ((product >> bit) & 1)
+        return product
+
+    groups = []
+    for s in range(SEASONS):
+        step = 1 if s == SEASONS - 1 else s + 1
+        for base in range(8):
+            if base < base ^ step:
+                groups.append(
+                    [
+                        (8 * a + (times(s, a) ^ base ^ (step * side))) * SEASONS + s
+                        for side in range(2)
+                        for a in range(8)
+                    ]
+                )
+    return groups
+
+
+def ends_out(region, season, line_to, line_limit, link_count, sent):
+    _, _, limit = live_limit(line_limit, link_count)
+    mine, offset, base = coset_of(season[0], region[0])
+    position = mine + 8 * jnp.where(offset == base, 0, 1)
+    shape = (GROUP, SLOT)
+    member = iota(shape, 0)
+    high = member & 7
+    side = lax.shift_right_logical(member, 3)
+    low = field_times(season[0], high) ^ base ^ (side * step_of(season[0]))
+    chosen = as_bf(8 * high + low == lax.shift_right_logical(iota(shape, 1), 2))
     lane = iota((SLOT, 128), 1)
-    kind = iota((SLOT, 128), 0) & (LINK_CAP - 1)
-    held = dot(spread * narrow(wide(row256(line_to))), as_bf(lane == kind))
+    kind = (iota((SLOT, 128), 0) & (LINK_CAP - 1)) + 2 * LINK_CAP * position
+    held = dot(chosen * narrow(wide(row256(line_to))), as_bf(lane == kind))
     spots = as_bf(lane == kind + LINK_CAP)
     for part in pieces(limit):
-        held = held + dot(spread * part, spots)
+        held = held + dot(chosen * part, spots)
     sent[...] = held
 
 
 def lines_near(
-    flow, price, line_from, line_limit, link_count, flow0, near0, cap, leave, turn
+    region, flow, price, line_from, line_limit, link_count,
+    flow0, near0, cap, leave, source, turn,
 ):
+    shape = (SEASONS, SLOT)
+    season = iota(shape, 0)
+    slot = iota(shape, 1)
+    high, offset, base = coset_of(season, lax.shift_right_logical(slot, 2))
+    _, _, own = coset_of(season, jnp.broadcast_to(region[0], shape))
+    position = high + 8 * jnp.where(offset == base, 0, 1)
+    spot = 128 * season + 2 * LINK_CAP * position + (slot & (LINK_CAP - 1))
+    spot = jnp.min(wide(jnp.where(base == own, spot, 1 << 20)), axis=0, keepdims=True)
     _, live, limit = live_limit(line_limit, link_count)
     turn[0:2, :] = wide(line_from[...])
     turn[2:3, :] = live[:, :128]
     turn[3:4, :] = live[:, 128:]
     turn[4:5, :] = limit[:, :128]
     turn[5:6, :] = limit[:, 128:]
+    turn[6:7, :] = spot[:, :128]
+    turn[7:8, :] = spot[:, 128:]
     turned = columns(turn)
+    source[...] = jnp.broadcast_to(long_column(turned, 6), (SLOT, 128))
     leave_t = onehot_rows(long_column(turned, 0), BUS)
     flow0[...] = flow[...] * long_column(turned, 2)
     near0[...] = narrow(dot(leave_t, narrow(price[...])))
@@ -182,18 +246,27 @@
     turn[0:1, 0:BUS] = wide(link[...])
     turned = columns(turn)
     sums = jnp.sum(wide(avail[...]) * wide(narrow(scarcity[...])), axis=1, keepdims=True)
-    sent[0] = season_block(sums, soc[...], wide(narrow(soc_dual[...])), turned[:BUS, 0:1])
-
-
-def ends_in(got, price, flow0, near0, sent, arrive, cap):
-    shape = (SLOT, REGIONS)
-    spread = as_bf(iota(shape, 1) == lax.shift_right_logical(iota(shape, 0), 2))
-    high, middle, low = pieces(got[...])
-    lines = dot(spread, high) + dot(spread, middle) + dot(spread, low)
-    lane = iota((SLOT, 128), 1)
-    kind = iota((SLOT, 128), 0) & (LINK_CAP - 1)
-    ends = jnp.sum(jnp.where(lane == kind, lines, 0.0), axis=1, keepdims=True)
-    limit = jnp.sum(jnp.where(lane == kind + LINK_CAP, lines, 0.0), axis=1, keepdims=True)
+    sent[...] = season_block(sums, soc[...], wide(narrow(soc_dual[...])), turned[:BUS, 0:1])
+
+
+def season_with_ends(rows, ends, sent):
+    gathered = jnp.sum(ends[...], axis=0, keepdims=True)
+    held = jnp.where(iota((8, 128), 0) == 4, gathered, rows[...])
+    for s in range(SEASONS):
+        sent[s] = held
+
+
+def ends_in(got, source, price, flow0, near0, sent, arrive, cap):
+    lane = wide(iota((SLOT, 128), 1))
+    spot = source[...]
+    ends = jnp.zeros((SLOT, 128), F32)
+    limit = jnp.zeros((SLOT, 128), F32)
+    for s in range(SEASONS):
+        row = got[s, 4:5]
+        ends = jnp.where(lane + 128 * s == spot, row, ends)
+        limit = jnp.where(lane + (128 * s - LINK_CAP) == spot, row, limit)
+    ends = jnp.sum(ends, axis=1, keepdims=True)
+    limit = jnp.sum(limit, axis=1, keepdims=True)
     arrive_t = onehot_rows(ends, BUS)
     far = narrow(dot(arrive_t, narrow(price[...])))
     arrive[...] = arrive_t
@@ -212,13 +285,11 @@
     return values[0]
 
 
-def local_step(season, consts, state, price_v, got, turn, tau, sigma, paired):
+def local_step(season, consts, state, price_v, got, turn, tau, sigma):
     avail, asset_bus, run_cost, build_cost, efficiency, power, energy, link = consts
     disp, build, disch, level, scarce, sdual = state
     before_at = (season + SEASONS - 1) & (SEASONS - 1)
     after_at = (season + 1) & (SEASONS - 1)
-    if paired:
-        before_at, after_at = before_at ^ season, after_at ^ season
     sums = tree([got[s, 0:2] for s in range(SEASONS)])
     grad_build = sums * (1.0 / (HOUR * SEASONS))
     build_new = jnp.maximum(build - tau * (build_cost[...] - grad_build), 0.0)
@@ -287,7 +358,7 @@
     consts = (avail, asset_bus, run_cost, build_cost, efficiency, power, energy, link)
     state = (disp[...], build[...], disch[...], level[...], scarce[...], sdual[...])
     local, halves, link_c = local_step(
-        season[0], consts, state, price[...], got, turn, step_size, step_size, True
+        season[0], consts, state, price[...], got, turn, step_size, step_size
     )
     balance[...] = local
     for ref, value in zip((disp1, build1, disch1, level1, scarce1, sdual1), halves):
@@ -372,17 +443,16 @@
     near = dot(leave_t, narrow(p1))
     moved, flow_x = line_step(f1, near, far, cap[...], tau)
     flow2[...] = mean(moved, f1)
-    local, halves, _ = local_step(season[0], consts, state, p1, got, turn, tau, sigma, False)
+    local, halves, _ = local_step(season[0], consts, state, p1, got, turn, tau, sigma)
     whole = local + dot_t(arrive[...], came_x) - dot_t(leave_t, flow_x)
     price2[...] = mean(p1 + sigma * (demand[...] - whole), p1)
     for ref, value in zip((disp2, build2, disch2, level2, scarce2, sdual2), halves):
         ref[...] = value
 
 
-def call(body, outs, *operands, scalar=False, turn=False):
-    in_specs = [pl.BlockSpec(memory_space=pltpu.VMEM)] * len(operands)
-    if scalar:
-        in_specs[0] = pl.BlockSpec(memory_space=pltpu.SMEM)
+def call(body, outs, *operands, scalars=0, turn=False):
+    in_specs = [pl.BlockSpec(memory_space=pltpu.SMEM)] * scalars
+    in_specs += [pl.BlockSpec(memory_space=pltpu.VMEM)] * (len(operands) - scalars)
     return pl.pallas_call(
         body,
         out_shape=[jax.ShapeDtypeStruct(shape, kind) for shape, kind in outs],
@@ -401,15 +471,6 @@
 
 def season_exchange(value):
     return lax.all_to_all(value, "season", split_axis=0, concat_axis=0, tiled=True)
-
-
-def season_gather(value):
-    apart = 1
-    while apart < SEASONS:
-        pairs = [(s, s ^ apart) for s in range(SEASONS)]
-        value = jnp.concatenate([value, lax.ppermute(value, "season", pairs)], axis=0)
-        apart *= 2
-    return value
 
 
 def on_device(
@@ -436,6 +497,7 @@
     soc_dual,
 ):
     season = lax.axis_index("season").astype(I32).reshape(1)
+    region = lax.axis_index("region").astype(I32).reshape(1)
     pair = lambda v: v.reshape(2, 128)
     short = lambda v: v.reshape(1, BUS)
     link = short(season_link)
@@ -457,25 +519,41 @@
         link,
     )
     limit = pair(line_limit)
-    (sent1,) = call(ends_out, [((REGIONS, 128), F32)], pair(line_to), limit, link_count)
-    got1 = region_exchange(sent1, 1, 1)
-    (rows1,) = call(
-        season_out, [((1, 8, 128), F32)], avail, scarcity, soc, soc_dual, link, turn=True
-    )
-    season1 = season_gather(rows1)
-    flow0, near0, cap, leave = call(
+    (sent1,) = call(
+        ends_out,
+        [((GROUP, 128), F32)],
+        region,
+        season,
+        pair(line_to),
+        limit,
+        link_count,
+        scalars=2,
+    )
+    got1 = lax.all_to_all(
+        sent1.reshape(GROUP, 1, 128),
+        ("region", "season"),
+        0,
+        0,
+        axis_index_groups=coset_groups(),
+        tiled=True,
+    ).reshape(GROUP, 128)
+    (rows1,) = call(season_out, [pack_row], avail, scarcity, soc, soc_dual, link, turn=True)
+    flow0, near0, cap, leave, source = call(
         lines_near,
-        [lines, lines_b, lines, picks],
+        [lines, lines_b, lines, picks, lines],
+        region,
         flow,
         price,
         pair(line_from),
         limit,
         link_count,
+        scalars=1,
         turn=True,
     )
-    got1, season1 = lax.optimization_barrier((got1, season1))
+    (sent_s,) = call(season_with_ends, [seasons], rows1, got1)
+    season1 = season_exchange(sent_s)
     sent2, arrive, came_cap = call(
-        ends_in, [rows_of(WITH_FLOWS), picks, lines], got1, price, flow0, near0
+        ends_in, [rows_of(WITH_FLOWS), picks, lines], season1, source, price, flow0, near0
     )
     got2 = region_exchange(sent2, LINK_CAP, 3)
     disp1, build1, disch1, level1, scarce1, sdual1, balance, rows2, moves = call(
@@ -491,7 +569,7 @@
         soc_dual,
         price,
         season1,
-        scalar=True,
+        scalars=1,
         turn=True,
     )
     price1, flow1, came1, came_far1, sent3 = call(
@@ -534,7 +612,7 @@
         flow1,
         cap,
         leave,
-        scalar=True,
+        scalars=1,
         turn=True,
     )
     return (disp2, build2.reshape(capacity.shape), flow2, disch2, level2, price2, scarce2, sdual2)

time: 109 us -> 106 us (0.972)
  waiting for transfers between devices: 28 us -> 25.6 us
  starting transfers between devices: 33.4 us -> 32.3 us
    all_to_all x0 -> x2, starting transfers between devices: none -> 26.3 us  [the longest x1 16.3 us: on_device(): lax.all_to_all(sent1.reshape(GROUP, 1, 128), ('region', 'season'), 0, 0,...]
    all_to_all x2 -> x1, starting transfers between devices: 20.7 us -> 6.07 us  [region_exchange(): got = lax.all_to_all(cut, 'region', split_axis=0, concat_axis=0, tiled=True)]
    ppermute x3 -> x0, starting transfers between devices: 12.7 us -> none  [season_gather(): lax.ppermute(value, 'season', pairs)]
    all_to_all x0 -> x2, waiting for transfers between devices: none -> 11.3 us  [the longest x1 7.76 us: on_device(): lax.all_to_all(sent1.reshape(GROUP, 1, 128), ('region', 'season'), 0, 0,...]
    all_to_all x2 -> x1, waiting for transfers between devices: 24.8 us -> 14.4 us  [region_exchange(): got = lax.all_to_all(cut, 'region', split_axis=0, concat_axis=0, tiled=True)]
    ppermute x3 -> x0, waiting for transfers between devices: 3.27 us -> none  [season_gather(): lax.ppermute(value, 'season', pairs)]
    unnamed x50 -> x52, local copies, waits for them, and re-layouts: 5.9 us -> 6.44 us
    pallas_call x8 -> x9, Pallas kernels: 6.87 us -> 7.3 us  [call(): pl.pallas_call(body, out_shape=[jax.ShapeDtypeStruct(shape, kind) for sha...]
  transfers between devices with their start and end apart: 5 -> 3, of which waited for: 4 -> 3; matrix products, arithmetic and copies ran while one was open for 0% -> 0% of each run, Pallas kernels for 2% -> 2%
where the time goes in v4:
time: 106 us
  blocking collectives  33.2 us (31%)
  starting transfers between devices  32.3 us (30%)
  waiting for transfers between devices  25.6 us (24%)
  Pallas kernels  7.3 us (7%)
  local copies, waits for them, and re-layouts  6.44 us (6%)
    all_to_all x1, blocking collectives, region_exchange(): got = lax.all_to_all(cut, 'region', split_axis=0, concat_axis=0, tiled=True)  22.2 us
    all_to_all x1, starting transfers between devices, on_device(): lax.all_to_all(sent1.reshape(GROUP, 1, 128), ('region', 'season'), 0, 0,...  16.3 us
    all_to_all x1, waiting for transfers between devices, region_exchange(): got = lax.all_to_all(cut, 'region', split_axis=0, concat_axis=0, tiled=True)  14.4 us
    all_to_all x1, blocking collectives, season_exchange(): lax.all_to_all(value, 'season', split_axis=0, concat_axis=0, tiled=True)  11 us
    all_to_all x1, starting transfers between devices, season_exchange(): lax.all_to_all(value, 'season', split_axis=0, concat_axis=0, tiled=True)  9.94 us
    all_to_all x1, waiting for transfers between devices, on_device(): lax.all_to_all(sent1.reshape(GROUP, 1, 128), ('region', 'season'), 0, 0,...  7.76 us
    pallas_call x9, Pallas kernels, call(): pl.pallas_call(body, out_shape=[jax.ShapeDtypeStruct(shape, kind) for sha...  7.3 us
    unnamed x52, local copies, waits for them, and re-layouts  6.44 us
  transfers between devices with their start and end apart: 3, of which 3 were waited for; matrix products, arithmetic and copies ran while one was open for 0% of the time, Pallas kernels for 2%

profile of v4, /device:TPU:1, one launch (start us, length us, event | category | flops | bytes accessed | tf_op | source)
XLA Modules:
  0.0 105.7 jit_solution(3555996018941233370)
XLA Ops:
  0.6 0.0 copy-start.8
  0.6 0.0 copy-start.16
  0.7 0.7 copy-done.16
  1.3 0.0 copy-start.21
  1.3 0.7 copy-done.21
  2.0 0.0 copy-start.25
  2.0 0.7 copy-done.25
  2.7 0.9 shard_map.261
  3.5 16.3 %all-to-all-start = ((f32[16,1,128]{2,1,0:T(1,128)}), f32[16,1,128]{2,1,0:T(1,128)S(1)}, u32[]{:S(2)}, u32[]{:S(2)}) async-start(f32[16,1,128]{2,1,0:T(1,128)} %bitcast.13), calls=%async_computation | async-start | bytes 16384 | tf_op jit(solution)/shard_map/all_to_all | solution.py:532
  19.9 0.0 copy-start.12
  19.9 0.0 copy-done.8
  19.9 0.6 copy-done.12
  20.5 0.0 copy-start
  20.5 0.8 copy-done
  21.4 0.0 copy-start.3
  21.4 0.9 copy-done.3
  22.3 0.0 copy-start.9
  22.3 0.8 copy-done.9
  23.0 0.0 copy-start.7
  23.0 0.2 shard_map.260.rows
  23.3 7.8 %all-to-all-done = f32[16,1,128]{2,1,0:T(1,128)S(1)} async-done(((f32[16,1,128]{2,1,0:T(1,128)}), f32[16,1,128]{2,1,0:T(1,128)S(1)}, u32[]{:S(2)}, u32[]{:S(2)}) %all-to-all-start) | async-done | bytes 8224 | tf_op jit(solution)/shard_map/all_to_all | solution.py:532
  31.0 0.6 shard_map.262
  31.6 0.0 copy-start.2
  31.6 0.0 copy-start.23
  31.6 9.9 %all-to-all-start.1 = ((f32[8,8,128]{2,1,0:T(8,128)}), f32[8,8,128]{2,1,0:T(8,128)S(1)}, u32[]{:S(2)}, u32[]{:S(2)}) async-start(f32[8,8,128]{2,1,0:T(8,128)} %shard_map.262), calls=%async_computation.1 | async-start | bytes 65536 | tf_op jit(solution)/shard_map/all_to_all | solution.py:473
  41.6 0.0 copy-start.17
  41.6 0.0 copy-start.22
  41.6 0.0 copy-done.7
  41.6 0.0 copy-done.2
  41.6 0.0 copy-done.23
  41.6 0.6 copy-done.17
  42.3 0.0 copy-done.22
  42.3 0.5 shard_map.264
  42.8 3.5 %all-to-all-done.1.got = f32[8,8,128]{2,1,0:T(8,128)S(1)} async-done(((f32[8,8,128]{2,1,0:T(8,128)}), f32[8,8,128]{2,1,0:T(8,128)S(1)}, u32[]{:S(2)}, u32[]{:S(2)}) %all-to-all-start.1) | async-done | bytes 32800 | tf_op jit(solution)/shard_map/all_to_all | solution.py:473
  46.3 1.1 %shard_map.265 = (bf16[768,128]{1,0:T(8,128)(2,1)}, bf16[256,64]{1,0:T(8,128)(2,1)S(1)}, f32[256,128]{1,0:T(8,128)S(1)}) custom-call(f32[8,8,128]{2,1,0:T(8,128)S(1)} %all-to-all-done.1.got, f32[256,128]{1,0:T(8,128)S(1)} %get-tuple-element.48.source, f32[64,128]{1,0:T(8,128)S(1)} %copy-done.2, f32[256,128]{1,0:T(8,128)S(1)} %get-tuple-element.44.flow0, ...), custom_call_target="tpu_custom_call" | custom-call | tf_op jit(solution)/shard_map/pallas_call | solution.py:456
  47.5 0.0 copy-start.11
  47.5 0.0 copy-start.14
  47.5 0.0 copy-start.15
  47.5 0.0 copy-start.19
  47.5 0.0 copy-start.20
  47.5 0.0 copy-start.24
  47.6 6.1 %all-to-all-start.2 = ((bf16[64,3,4,128]{3,2,1,0:T(4,128)(2,1)}), bf16[64,3,4,128]{3,2,1,0:T(4,128)(2,1)S(1)}, u32[]{:S(2)}, u32[]{:S(2)}) async-start(bf16[64,3,4,128]{3,2,1,0:T(4,128)(2,1)} %bitcast.16), calls=%async_computation.2 | async-start | bytes 393216 | tf_op jit(solution)/shard_map/all_to_all | solution.py:468
  53.6 0.0 copy-start.13
  53.6 0.0 copy-start.18
  53.7 0.0 copy-done.1
  53.7 0.0 copy-done.4
  53.7 0.0 copy-done.6
  53.7 0.0 copy-done.10
  53.7 0.0 copy-done.11
  53.7 0.0 copy-done.14
  53.7 0.0 copy-done.15
  53.7 0.0 copy-done.19
  53.7 0.0 copy-done.20
  53.7 0.0 copy-done.24
  53.8 0.6 copy-done.13
  54.3 0.0 copy-done.18
  54.3 1.0 shard_map.263
  55.3 14.4 %all-to-all-done.2 = bf16[64,3,4,128]{3,2,1,0:T(4,128)(2,1)S(1)} async-done(((bf16[64,3,4,128]{3,2,1,0:T(4,128)(2,1)}), bf16[64,3,4,128]{3,2,1,0:T(4,128)(2,1)S(1)}, u32[]{:S(2)}, u32[]{:S(2)}) %all-to-all-start.2) | async-done | bytes 196640 | tf_op jit(solution)/shard_map/all_to_all | solution.py:468
  69.7 0.0 copy-done.5
  69.7 0.9 shard_map.266
  70.6 22.2 %all_to_all.25 = bf16[64,5,2,128]{3,2,1,0:T(2,128)(2,1)S(1)} all-to-all(bf16[64,5,2,128]{3,2,1,0:T(2,128)(2,1)S(1)} %bitcast.25), channel_id=1, replica_groups=mesh['region'=64,'season'=8] {'region'}, dimensions={0} | all-to-all | bytes 327680 | tf_op jit(solution)/shard_map/all_to_all | solution.py:468
  92.8 0.1 shard_map.267
  92.9 11.0 %all_to_all.26.got = f32[8,8,128]{2,1,0:T(8,128)S(1)} all-to-all(f32[8,8,128]{2,1,0:T(8,128)S(1)} %shard_map.267), channel_id=1, replica_groups=mesh['region'=64,'season'=8] {'season'}, dimensions={0} | all-to-all | bytes 65536 | tf_op jit(solution)/shard_map/all_to_all | solution.py:473
  103.9 1.8 %shard_map.268 = (f32[256,128]{1,0:T(8,128)}, f32[2,128]{1,0:T(2,128)}, f32[256,128]{1,0:T(8,128)}, f32[64,128]{1,0:T(8,128)}, f32[64,128]{1,0:T(8,128)}, /*inde...) custom-call(s32[1]{0:T(128)} %bitcast.season, bf16[256,128]{1,0:T(8,128)(2,1)S(1)} %copy-done.1, ...), custom_call_target="tpu_custom_call" | custom-call | tf_op jit(solution)/shard_map/pallas_call | solution.py:456
  (5 shorter events, 0.0 us)
Async XLA Ops:
  0.6 19.2 %copy-start.8 = (f32[64,128]{1,0:T(8,128)S(1)}, f32[64,128]{1,0:T(8,128)}, u32[]{:S(2)}) copy-start(f32[64,128]{1,0:T(8,128)} %level.1) | copy-start | bytes 98308
  0.6 0.7 copy-start.16
  1.3 0.7 copy-start.21
  2.0 0.7 copy-start.25
  3.5 27.5 %all-to-all-start = ((f32[16,1,128]{2,1,0:T(1,128)}), f32[16,1,128]{2,1,0:T(1,128)S(1)}, u32[]{:S(2)}, u32[]{:S(2)}) async-start(f32[16,1,128]{2,1,0:T(1,128)} %bitcast.13), calls=%async_computation | async-start | bytes 16384 | tf_op jit(solution)/shard_map/all_to_all | solution.py:532
  19.9 0.7 copy-start.12
  20.5 0.8 copy-start
  21.4 0.9 copy-start.3
  22.3 0.8 copy-start.9
  23.0 18.6 %copy-start.7 = (f32[256,128]{1,0:T(8,128)S(1)}, f32[256,128]{1,0:T(8,128)}, u32[]{:S(2)}) copy-start(f32[256,128]{1,0:T(8,128)} %flow.1) | copy-start | bytes 393220
  31.6 10.0 %copy-start.2 = (f32[64,128]{1,0:T(8,128)S(1)}, f32[64,128]{1,0:T(8,128)}, u32[]{:S(2)}) copy-start(f32[64,128]{1,0:T(8,128)} %price.7) | copy-start | bytes 98308
  31.6 10.0 %copy-start.23 = (s32[256]{0:T(256)S(1)}, s32[256]{0:T(256)}, u32[]{:S(2)}) copy-start(s32[256]{0:T(256)} %param.26) | copy-start | bytes 3076
  31.6 14.7 %all-to-all-start.1 = ((f32[8,8,128]{2,1,0:T(8,128)}), f32[8,8,128]{2,1,0:T(8,128)S(1)}, u32[]{:S(2)}, u32[]{:S(2)}) async-start(f32[8,8,128]{2,1,0:T(8,128)} %shard_map.262), calls=%async_computation.1 | async-start | bytes 65536 | tf_op jit(solution)/shard_map/all_to_all | solution.py:473
  41.6 0.7 copy-start.17
  41.6 0.7 copy-start.22
  47.5 6.2 %copy-start.1 = (bf16[256,128]{1,0:T(8,128)(2,1)S(1)}, bf16[256,128]{1,0:T(8,128)(2,1)}, u32[]{:S(2)}) copy-start(bf16[256,128]{1,0:T(8,128)(2,1)} %avail.5) | copy-start | bytes 196612
  47.5 6.2 %copy-start.4 = (f32[256,128]{1,0:T(8,128)S(1)}, f32[256,128]{1,0:T(8,128)}, u32[]{:S(2)}) copy-start(f32[256,128]{1,0:T(8,128)} %scarce.1) | copy-start | bytes 393220
  47.5 6.2 %copy-start.6 = (f32[256,128]{1,0:T(8,128)S(1)}, f32[256,128]{1,0:T(8,128)}, u32[]{:S(2)}) copy-start(f32[256,128]{1,0:T(8,128)} %disp.1) | copy-start | bytes 393220
  47.5 6.2 %copy-start.10 = (f32[64,128]{1,0:T(8,128)S(1)}, f32[64,128]{1,0:T(8,128)}, u32[]{:S(2)}) copy-start(f32[64,128]{1,0:T(8,128)} %sdual.1) | copy-start | bytes 98308
  47.5 6.2 %copy-start.11 = (f32[64,128]{1,0:T(8,128)S(1)}, f32[64,128]{1,0:T(8,128)}, u32[]{:S(2)}) copy-start(f32[64,128]{1,0:T(8,128)} %disch.1) | copy-start | bytes 98308
  47.5 6.2 %copy-start.14 = (f32[256]{0:T(256)S(1)}, f32[256]{0:T(256)}, u32[]{:S(2)}) copy-start(f32[256]{0:T(256)} %param.24) | copy-start | bytes 3076
  47.5 6.2 %copy-start.15 = (f32[256]{0:T(256)S(1)}, f32[256]{0:T(256)}, u32[]{:S(2)}) copy-start(f32[256]{0:T(256)} %param.25) | copy-start | bytes 3076
  47.5 6.2 %copy-start.19 = (f32[64]{0:T(128)S(1)}, f32[64]{0:T(128)}, u32[]{:S(2)}) copy-start(f32[64]{0:T(128)} %param.31) | copy-start | bytes 772
  47.5 6.2 %copy-start.20 = (f32[64]{0:T(128)S(1)}, f32[64]{0:T(128)}, u32[]{:S(2)}) copy-start(f32[64]{0:T(128)} %param.32) | copy-start | bytes 772
  47.5 6.2 %copy-start.24 = (f32[256]{0:T(256)S(1)}, f32[256]{0:T(256)}, u32[]{:S(2)}) copy-start(f32[256]{0:T(256)} %param.35) | copy-start | bytes 3076
  47.6 22.1 %all-to-all-start.2 = ((bf16[64,3,4,128]{3,2,1,0:T(4,128)(2,1)}), bf16[64,3,4,128]{3,2,1,0:T(4,128)(2,1)S(1)}, u32[]{:S(2)}, u32[]{:S(2)}) async-start(bf16[64,3,4,128]{3,2,1,0:T(4,128)(2,1)} %bitcast.16), calls=%async_computation.2 | async-start | bytes 393216 | tf_op jit(solution)/shard_map/all_to_all | solution.py:468
  53.6 0.7 copy-start.13
  53.6 0.7 copy-start.18
  54.3 15.4 %copy-start.5 = (f32[64,128]{1,0:T(8,128)S(1)}, f32[64,128]{1,0:T(8,128)}, u32[]{:S(2)}) copy-start(f32[64,128]{1,0:T(8,128)} %demand.3) | copy-start | bytes 98308

commit v5 on v4

--- a/solution.py
+++ b/solution.py
@@ -158,6 +158,17 @@
     return high, offset, jnp.minimum(offset, offset ^ step_of(season))
 
 
+def fetch(sources, held, sems):
+    copies = [
+        pltpu.make_async_copy(source, target, sems.at[at])
+        for at, (source, target) in enumerate(zip(sources, held))
+    ]
+    for copy in copies:
+        copy.start()
+    for copy in copies:
+        copy.wait()
+
+
 def coset_groups():
     def times(a, b):
         product = 0
@@ -182,7 +193,9 @@
     return groups
 
 
-def ends_out(region, season, line_to, line_limit, link_count, sent):
+def ends_out(region, season, *refs):
+    sources, (sent, line_to, line_limit, link_count, sems) = refs[:3], refs[3:]
+    fetch(sources, (line_to, line_limit, link_count), sems)
     _, _, limit = live_limit(line_limit, link_count)
     mine, offset, base = coset_of(season[0], region[0])
     position = mine + 8 * jnp.where(offset == base, 0, 1)
@@ -242,7 +255,9 @@
     return jnp.transpose(held)[0:8]
 
 
-def season_out(avail, scarcity, soc, soc_dual, link, sent, turn):
+def season_out(*refs):
+    sources, (sent, turn, avail, scarcity, soc, soc_dual, link, sems) = refs[:5], refs[5:]
+    fetch(sources, (avail, scarcity, soc, soc_dual, link), sems)
     turn[0:1, 0:BUS] = wide(link[...])
     turned = columns(turn)
     sums = jnp.sum(wide(avail[...]) * wide(narrow(scarcity[...])), axis=1, keepdims=True)
@@ -274,8 +289,8 @@
     pack(narrow(flow0[...]), near0[...], far, sent, WITH_FLOWS)
 
 
-def line_step(flows, near, far, cap, tau):
-    moved = jnp.clip(flows + tau * (far - near), -cap, cap)
+def line_step(flows, push, cap, tau):
+    moved = jnp.clip(flows + tau * push, -cap, cap)
     return moved, extrapolate(moved, flows)
 
 
@@ -285,7 +300,7 @@
     return values[0]
 
 
-def local_step(season, consts, state, price_v, got, turn, tau, sigma):
+def local_step(season, consts, state, price_v, got, turn, tau, sigma, disp_push=None):
     avail, asset_bus, run_cost, build_cost, efficiency, power, energy, link = consts
     disp, build, disch, level, scarce, sdual = state
     before_at = (season + SEASONS - 1) & (SEASONS - 1)
@@ -305,7 +320,6 @@
     turned = columns(turn)
     build_x = long_column(turned, 16)
     cost = long_column(turned, 18)
-    asset_t = onehot_rows(long_column(turned, 20), BUS)
     asset_row = row256(asset_bus)
     asset_onehot = as_bf(iota((BUS, SLOT), 0) == asset_row)
     decay = turned[:BUS, 22:23]
@@ -317,14 +331,16 @@
     after_first, after_link = turned[:BUS, 11:12], turned[BUS:, 11:12]
     price_b = narrow(price_v)
     dual_f = wide(narrow(sdual))
-    grad_dispatch = dot(asset_t, price_b) - wide(narrow(scarce))
+    if disp_push is None:
+        asset_t = onehot_rows(long_column(turned, 20), BUS)
+        disp_push = cost - (dot(asset_t, price_b) - wide(narrow(scarce)))
     grad_charge = wide(price_b) + dual_f
     first = dual_f[:, 0:1]
     after_last = (1.0 - link_c) * first + after_link * after_first
     following = jnp.concatenate([dual_f[:, 1:], after_last], axis=1)
     grad_soc = dual_f - decay * following
     before_grad = before_dual - decay * ((1.0 - before_link) * before_first + link_c * first)
-    disp_new = jnp.maximum(disp - tau * (cost - grad_dispatch), 0.0)
+    disp_new = jnp.maximum(disp - tau * disp_push, 0.0)
     disch_new = jnp.clip(disch + tau * grad_charge, -power_c, power_c)
     level_new = jnp.clip(level + tau * grad_soc, 0.0, energy_c)
     before_new = jnp.clip(before_level + tau * before_grad, 0.0, energy_c)
@@ -386,9 +402,9 @@
     arrive_t = arrive[...]
     came0, came_near, far = unpack(got, WITH_FLOWS)
     came_far = dot(arrive_t, narrow(p0))
-    came_moved, came_x = line_step(came0, came_near, came_far, came_cap[...], step_size)
+    came_moved, came_x = line_step(came0, came_far - came_near, came_cap[...], step_size)
     came1[...] = mean(came_moved, came0)
-    moved, flow_x = line_step(f0, wide(near0[...]), far, cap[...], step_size)
+    moved, flow_x = line_step(f0, far - wide(near0[...]), cap[...], step_size)
     f1 = mean(moved, f0)
     flow1[...] = f1
     whole = balance[...] + dot_t(arrive_t, came_x) - dot_t(leave_t, flow_x)
@@ -421,10 +437,26 @@
         sent[s] = held
 
 
+def pushes(
+    lines_got, price, came_far, leave, asset_bus, run_cost, scarce,
+    push, came_push, disp_push, turn,
+):
+    price_b = narrow(price[...])
+    came_near, far, _ = unpack(lines_got, WITH_MOVES)
+    push[...] = far - dot(leave[...], price_b)
+    came_push[...] = wide(came_far[...]) - came_near
+    turn[0:2, :] = run_cost[...]
+    turn[2:4, :] = wide(asset_bus[...])
+    turned = columns(turn)
+    asset_t = onehot_rows(long_column(turned, 2), BUS)
+    grad = dot(asset_t, price_b) - wide(narrow(scarce[...]))
+    disp_push[...] = long_column(turned, 0) - grad
+
+
 def second_step(
     season, avail, asset_bus, run_cost, build_cost, efficiency, power, energy, link,
-    disp, build, disch, level, scarce, sdual, price, got, lines_got, arrive, came_cap,
-    came_far, came, demand, flow, cap, leave,
+    disp, build, disch, level, scarce, sdual, price, got, push, came_push, disp_push,
+    arrive, came_cap, came, demand, flow, cap, leave,
     disp2, build2, flow2, disch2, level2, price2, scarce2, sdual2, turn,
 ):
     moves = tree([got[s, 4:5] for s in range(SEASONS)])
@@ -435,30 +467,33 @@
     sigma = step_size * weight
     consts = (avail, asset_bus, run_cost, build_cost, efficiency, power, energy, link)
     state = (disp[...], build[...], disch[...], level[...], scarce[...], sdual[...])
-    came_near, far, _ = unpack(lines_got, WITH_MOVES)
-    _, came_x = line_step(came[...], came_near, wide(came_far[...]), came_cap[...], tau)
+    _, came_x = line_step(came[...], came_push[...], came_cap[...], tau)
     f1 = flow[...]
     p1 = price[...]
     leave_t = leave[...]
-    near = dot(leave_t, narrow(p1))
-    moved, flow_x = line_step(f1, near, far, cap[...], tau)
+    moved, flow_x = line_step(f1, push[...], cap[...], tau)
     flow2[...] = mean(moved, f1)
-    local, halves, _ = local_step(season[0], consts, state, p1, got, turn, tau, sigma)
+    local, halves, _ = local_step(season[0], consts, state, p1, got, turn, tau, sigma, disp_push[...])
     whole = local + dot_t(arrive[...], came_x) - dot_t(leave_t, flow_x)
     price2[...] = mean(p1 + sigma * (demand[...] - whole), p1)
     for ref, value in zip((disp2, build2, disch2, level2, scarce2, sdual2), halves):
         ref[...] = value
 
 
-def call(body, outs, *operands, scalars=0, turn=False):
+def call(body, outs, *operands, scalars=0, turn=False, fetched=False):
     in_specs = [pl.BlockSpec(memory_space=pltpu.SMEM)] * scalars
-    in_specs += [pl.BlockSpec(memory_space=pltpu.VMEM)] * (len(operands) - scalars)
+    space = pltpu.HBM if fetched else pltpu.VMEM
+    in_specs += [pl.BlockSpec(memory_space=space)] * (len(operands) - scalars)
+    scratch = [pltpu.VMEM((128, 128), F32)] if turn else []
+    if fetched:
+        scratch += [pltpu.VMEM(v.shape, v.dtype) for v in operands[scalars:]]
+        scratch += [pltpu.SemaphoreType.DMA((len(operands) - scalars,))]
     return pl.pallas_call(
         body,
         out_shape=[jax.ShapeDtypeStruct(shape, kind) for shape, kind in outs],
         in_specs=in_specs,
         out_specs=[pl.BlockSpec(memory_space=pltpu.VMEM)] * len(outs),
-        scratch_shapes=[pltpu.VMEM((128, 128), F32)] if turn else [],
+        scratch_shapes=scratch,
         compiler_params=pltpu.CompilerParams(vmem_limit_bytes=32 * 1024 * 1024),
     )(*operands)
 
@@ -528,6 +563,7 @@
         limit,
         link_count,
         scalars=2,
+        fetched=True,
     )
     got1 = lax.all_to_all(
         sent1.reshape(GROUP, 1, 128),
@@ -537,7 +573,7 @@
         axis_index_groups=coset_groups(),
         tiled=True,
     ).reshape(GROUP, 128)
-    (rows1,) = call(season_out, [pack_row], avail, scarcity, soc, soc_dual, link, turn=True)
+    (rows1,) = call(season_out, [pack_row], avail, scarcity, soc, soc_dual, link, turn=True, fetched=True)
     flow0, near0, cap, leave, source = call(
         lines_near,
         [lines, lines_b, lines, picks, lines],
@@ -590,6 +626,18 @@
     got3 = region_exchange(sent3, 2, 5)
     (rows3,) = call(moves_out, [seasons], got3, rows2)
     season2 = season_exchange(rows3)
+    push, came_push, disp_push = call(
+        pushes,
+        [lines, lines, lines],
+        got3,
+        price1,
+        came_far1,
+        leave,
+        pair(asset_bus),
+        pair(run_cost),
+        scarce1,
+        turn=True,
+    )
     disp2, build2, flow2, disch2, level2, price2, scarce2, sdual2 = call(
         second_step,
         [lines, ((2, 128), F32), lines, buses, buses, buses, lines, buses],
@@ -603,10 +651,11 @@
         sdual1,
         price1,
         season2,
-        got3,
+        push,
+        came_push,
+        disp_push,
         arrive,
         came_cap,
-        came_far1,
         came1,
         demand,
         flow1,

time: 106 us -> 108 us (1.019)
  blocking collectives: 33.2 us -> 22 us
  starting transfers between devices: 32.3 us -> 39.5 us
  waiting for transfers between devices: 25.6 us -> 29.7 us
  Pallas kernels: 7.3 us -> 8.57 us
    all_to_all x1 -> x0, blocking collectives: 11 us -> none  [season_exchange(): lax.all_to_all(value, 'season', split_axis=0, concat_axis=0, tiled=True)]
    all_to_all x1 -> x2, starting transfers between devices: 9.94 us -> 17.1 us  [season_exchange(): lax.all_to_all(value, 'season', split_axis=0, concat_axis=0, tiled=True)]
    all_to_all x1 -> x2, waiting for transfers between devices: 3.52 us -> 7.87 us  [season_exchange(): lax.all_to_all(value, 'season', split_axis=0, concat_axis=0, tiled=True)]
    pallas_call x9 -> x10, Pallas kernels: 7.3 us -> 8.57 us  [call(): pl.pallas_call(body, out_shape=[jax.ShapeDtypeStruct(shape, kind) for sha...]
  transfers between devices with their start and end apart: 3 -> 4, of which waited for: 3 -> 4; matrix products, arithmetic and copies ran while one was open for 0% -> 0% of each run, Pallas kernels for 2% -> 2%
where the time goes in v5:
time: 108 us; the launch traced here: 107 us
  starting transfers between devices  39.5 us (37%)
  waiting for transfers between devices  29.7 us (28%)
  blocking collectives  22 us (20%)
  Pallas kernels  8.57 us (8%)
  local copies, waits for them, and re-layouts  6.44 us (6%)
    all_to_all x1, blocking collectives, region_exchange(): got = lax.all_to_all(cut, 'region', split_axis=0, concat_axis=0, tiled=True)  22 us
    all_to_all x2, starting transfers between devices, season_exchange(): lax.all_to_all(value, 'season', split_axis=0, concat_axis=0, tiled=True)  17.1 us
    all_to_all x1, starting transfers between devices, on_device(): lax.all_to_all(sent1.reshape(GROUP, 1, 128), ('region', 'season'), 0, 0,...  16.3 us
    all_to_all x1, waiting for transfers between devices, region_exchange(): got = lax.all_to_all(cut, 'region', split_axis=0, concat_axis=0, tiled=True)  14.5 us
    pallas_call x10, Pallas kernels, call(): pl.pallas_call(body, out_shape=[jax.ShapeDtypeStruct(shape, kind) for sha...  8.57 us
    all_to_all x2, waiting for transfers between devices, season_exchange(): lax.all_to_all(value, 'season', split_axis=0, concat_axis=0, tiled=True)  7.87 us
    all_to_all x1, waiting for transfers between devices, on_device(): lax.all_to_all(sent1.reshape(GROUP, 1, 128), ('region', 'season'), 0, 0,...  7.38 us
    unnamed x52, local copies, waits for them, and re-layouts  6.44 us
  transfers between devices with their start and end apart: 4, of which 4 were waited for; matrix products, arithmetic and copies ran while one was open for 0% of the time, Pallas kernels for 2%

profile of v5, /device:TPU:1, one launch (start us, length us, event | category | flops | bytes accessed | tf_op | source)
XLA Modules:
  0.0 107.2 jit_solution(361915769885457398)
XLA Ops:
  0.6 0.0 copy-start.8
  0.6 0.0 copy-start.15
  0.7 0.7 copy-done.15
  1.3 0.0 copy-start.21
  1.3 0.7 copy-done.21
  2.0 0.0 copy-start.25
  2.0 0.7 copy-done.25
  2.7 0.9 shard_map.261
  3.6 16.3 %all-to-all-start = ((f32[16,1,128]{2,1,0:T(1,128)}), f32[16,1,128]{2,1,0:T(1,128)S(1)}, u32[]{:S(2)}, u32[]{:S(2)}) async-start(f32[16,1,128]{2,1,0:T(1,128)} %bitcast.13), calls=%async_computation | async-start | bytes 16384 | tf_op jit(solution)/shard_map/all_to_all | solution.py:568
  19.9 0.0 copy-start.14
  19.9 0.0 copy-done.8
  19.9 0.6 copy-done.14
  20.6 0.0 copy-start
  20.6 0.8 copy-done
  21.4 0.0 copy-start.3
  21.4 0.9 copy-done.3
  22.3 0.0 copy-start.9
  22.3 0.8 copy-done.9
  23.1 0.0 copy-start.7
  23.1 0.6 shard_map.260.rows
  23.7 7.4 %all-to-all-done = f32[16,1,128]{2,1,0:T(1,128)S(1)} async-done(((f32[16,1,128]{2,1,0:T(1,128)}), f32[16,1,128]{2,1,0:T(1,128)S(1)}, u32[]{:S(2)}, u32[]{:S(2)}) %all-to-all-start) | async-done | bytes 8224 | tf_op jit(solution)/shard_map/all_to_all | solution.py:568
  31.1 0.6 shard_map.262
  31.7 0.0 copy-start.2
  31.7 0.0 copy-start.23
  31.7 9.9 %all-to-all-start.1 = ((f32[8,8,128]{2,1,0:T(8,128)}), f32[8,8,128]{2,1,0:T(8,128)S(1)}, u32[]{:S(2)}, u32[]{:S(2)}) async-start(f32[8,8,128]{2,1,0:T(8,128)} %shard_map.262), calls=%async_computation.1 | async-start | bytes 65536 | tf_op jit(solution)/shard_map/all_to_all | solution.py:508
  41.6 0.0 copy-done.7
  41.7 0.0 copy-done.2
  41.7 0.0 copy-done.23
  41.7 0.6 copy-done.16
  42.3 0.0 copy-done.22
  42.3 0.5 shard_map.264
  42.9 3.5 %all-to-all-done.1.got = f32[8,8,128]{2,1,0:T(8,128)S(1)} async-done(((f32[8,8,128]{2,1,0:T(8,128)}), f32[8,8,128]{2,1,0:T(8,128)S(1)}, u32[]{:S(2)}, u32[]{:S(2)}) %all-to-all-start.1) | async-done | bytes 32800 | tf_op jit(solution)/shard_map/all_to_all | solution.py:508
  46.4 1.1 %shard_map.265 = (bf16[768,128]{1,0:T(8,128)(2,1)}, bf16[256,64]{1,0:T(8,128)(2,1)S(1)}, f32[256,128]{1,0:T(8,128)S(1)}) custom-call(f32[8,8,128]{2,1,0:T(8,128)S(1)} %all-to-all-done.1.got, f32[256,128]{1,0:T(8,128)S(1)} %get-tuple-element.51.source, f32[64,128]{1,0:T(8,128)S(1)} %copy-done.2, f32[256,128]{1,0:T(8,128)S(1)} %get-tuple-element.47.flow0, ...), custom_call_target="tpu_custom_call" | custom-call | tf_op jit(solution)/shard_map/pallas_call | solution.py:491
  47.5 0.0 copy-start.11
  47.5 0.0 copy-start.13
  47.6 0.0 copy-start.17
  47.6 0.0 copy-start.19
  47.6 0.0 copy-start.20
  47.6 0.0 copy-start.24
  47.6 6.1 %all-to-all-start.2 = ((bf16[64,3,4,128]{3,2,1,0:T(4,128)(2,1)}), bf16[64,3,4,128]{3,2,1,0:T(4,128)(2,1)S(1)}, u32[]{:S(2)}, u32[]{:S(2)}) async-start(bf16[64,3,4,128]{3,2,1,0:T(4,128)(2,1)} %bitcast.16), calls=%async_computation.2 | async-start | bytes 393216 | tf_op jit(solution)/shard_map/all_to_all | solution.py:503
  53.7 0.0 copy-start.12
  53.7 0.0 copy-start.18
  53.7 0.0 copy-done.1
  53.7 0.0 copy-done.4
  53.7 0.0 copy-done.6
  53.7 0.0 copy-done.10
  53.7 0.0 copy-done.11
  53.8 0.0 copy-done.13
  53.8 0.0 copy-done.17
  53.8 0.0 copy-done.19
  53.8 0.0 copy-done.20
  53.8 0.0 copy-done.24
  53.8 0.6 copy-done.12
  54.4 0.0 copy-done.18
  54.4 1.0 shard_map.263
  55.4 14.5 %all-to-all-done.2 = bf16[64,3,4,128]{3,2,1,0:T(4,128)(2,1)S(1)} async-done(((bf16[64,3,4,128]{3,2,1,0:T(4,128)(2,1)}), bf16[64,3,4,128]{3,2,1,0:T(4,128)(2,1)S(1)}, u32[]{:S(2)}, u32[]{:S(2)}) %all-to-all-start.2) | async-done | bytes 196640 | tf_op jit(solution)/shard_map/all_to_all | solution.py:503
  69.9 0.0 copy-done.5
  69.9 0.9 shard_map.266
  70.8 22.0 %all_to_all.25 = bf16[64,5,2,128]{3,2,1,0:T(2,128)(2,1)S(1)} all-to-all(bf16[64,5,2,128]{3,2,1,0:T(2,128)(2,1)S(1)} %bitcast.25), channel_id=1, replica_groups=mesh['region'=64,'season'=8] {'region'}, dimensions={0} | all-to-all | bytes 327680 | tf_op jit(solution)/shard_map/all_to_all | solution.py:503
  92.8 0.8 shard_map.267
  93.6 7.2 %all-to-all-start.4 = ((f32[8,8,128]{2,1,0:T(8,128)}), f32[8,8,128]{2,1,0:T(8,128)S(1)}, u32[]{:S(2)}, u32[]{:S(2)}) async-start(f32[8,8,128]{2,1,0:T(8,128)} %shard_map.267), calls=%async_computation.4 | async-start | bytes 65536 | tf_op jit(solution)/shard_map/all_to_all | solution.py:508
  100.7 0.4 shard_map.268
  101.1 4.3 %all-to-all-done.4.got = f32[8,8,128]{2,1,0:T(8,128)S(1)} async-done(((f32[8,8,128]{2,1,0:T(8,128)}), f32[8,8,128]{2,1,0:T(8,128)S(1)}, u32[]{:S(2)}, u32[]{:S(2)}) %all-to-all-start.4) | async-done | bytes 32800 | tf_op jit(solution)/shard_map/all_to_all | solution.py:508
  105.5 1.7 %shard_map.269 = (f32[256,128]{1,0:T(8,128)}, f32[2,128]{1,0:T(2,128)}, f32[256,128]{1,0:T(8,128)}, f32[64,128]{1,0:T(8,128)}, f32[64,128]{1,0:T(8,128)}, /*inde...) custom-call(s32[1]{0:T(128)} %bitcast.season, bf16[256,128]{1,0:T(8,128)(2,1)S(1)} %copy-done.1, ...), custom_call_target="tpu_custom_call" | custom-call | tf_op jit(solution)/shard_map/pallas_call | solution.py:491
  (7 shorter events, 0.0 us)
Async XLA Ops:
  0.6 19.3 %copy-start.8 = (f32[64,128]{1,0:T(8,128)S(1)}, f32[64,128]{1,0:T(8,128)}, u32[]{:S(2)}) copy-start(f32[64,128]{1,0:T(8,128)} %level.1) | copy-start | bytes 98308
  0.6 0.7 copy-start.15
  1.3 0.7 copy-start.21
  2.0 0.7 copy-start.25
  3.6 27.5 %all-to-all-start = ((f32[16,1,128]{2,1,0:T(1,128)}), f32[16,1,128]{2,1,0:T(1,128)S(1)}, u32[]{:S(2)}, u32[]{:S(2)}) async-start(f32[16,1,128]{2,1,0:T(1,128)} %bitcast.13), calls=%async_computation | async-start | bytes 16384 | tf_op jit(solution)/shard_map/all_to_all | solution.py:568
  19.9 0.7 copy-start.14
  20.6 0.8 copy-start
  21.4 0.9 copy-start.3
  22.3 0.8 copy-start.9
  23.1 18.6 %copy-start.7 = (f32[256,128]{1,0:T(8,128)S(1)}, f32[256,128]{1,0:T(8,128)}, u32[]{:S(2)}) copy-start(f32[256,128]{1,0:T(8,128)} %flow.1) | copy-start | bytes 393220
  31.7 10.0 %copy-start.2 = (f32[64,128]{1,0:T(8,128)S(1)}, f32[64,128]{1,0:T(8,128)}, u32[]{:S(2)}) copy-start(f32[64,128]{1,0:T(8,128)} %price.7) | copy-start | bytes 98308
  31.7 10.0 %copy-start.23 = (s32[256]{0:T(256)S(1)}, s32[256]{0:T(256)}, u32[]{:S(2)}) copy-start(s32[256]{0:T(256)} %param.26) | copy-start | bytes 3076
  31.7 14.7 %all-to-all-start.1 = ((f32[8,8,128]{2,1,0:T(8,128)}), f32[8,8,128]{2,1,0:T(8,128)S(1)}, u32[]{:S(2)}, u32[]{:S(2)}) async-start(f32[8,8,128]{2,1,0:T(8,128)} %shard_map.262), calls=%async_computation.1 | async-start | bytes 65536 | tf_op jit(solution)/shard_map/all_to_all | solution.py:508
  41.6 0.7 copy-start.16
  41.6 0.7 copy-start.22
  47.5 6.2 %copy-start.1 = (bf16[256,128]{1,0:T(8,128)(2,1)S(1)}, bf16[256,128]{1,0:T(8,128)(2,1)}, u32[]{:S(2)}) copy-start(bf16[256,128]{1,0:T(8,128)(2,1)} %avail.3) | copy-start | bytes 196612
  47.5 6.2 %copy-start.4 = (f32[256,128]{1,0:T(8,128)S(1)}, f32[256,128]{1,0:T(8,128)}, u32[]{:S(2)}) copy-start(f32[256,128]{1,0:T(8,128)} %scarce.1) | copy-start | bytes 393220
  47.5 6.2 %copy-start.6 = (f32[256,128]{1,0:T(8,128)S(1)}, f32[256,128]{1,0:T(8,128)}, u32[]{:S(2)}) copy-start(f32[256,128]{1,0:T(8,128)} %disp.1) | copy-start | bytes 393220
  47.5 6.2 %copy-start.10 = (f32[64,128]{1,0:T(8,128)S(1)}, f32[64,128]{1,0:T(8,128)}, u32[]{:S(2)}) copy-start(f32[64,128]{1,0:T(8,128)} %sdual.1) | copy-start | bytes 98308
  47.5 6.2 %copy-start.11 = (f32[64,128]{1,0:T(8,128)S(1)}, f32[64,128]{1,0:T(8,128)}, u32[]{:S(2)}) copy-start(f32[64,128]{1,0:T(8,128)} %disch.1) | copy-start | bytes 98308
  47.5 6.2 %copy-start.13 = (f32[256]{0:T(256)S(1)}, f32[256]{0:T(256)}, u32[]{:S(2)}) copy-start(f32[256]{0:T(256)} %param.24) | copy-start | bytes 3076
  47.6 6.2 %copy-start.17 = (f32[256]{0:T(256)S(1)}, f32[256]{0:T(256)}, u32[]{:S(2)}) copy-start(f32[256]{0:T(256)} %param.25) | copy-start | bytes 3076
  47.6 6.2 %copy-start.19 = (f32[64]{0:T(128)S(1)}, f32[64]{0:T(128)}, u32[]{:S(2)}) copy-start(f32[64]{0:T(128)} %param.31) | copy-start | bytes 772
  47.6 6.2 %copy-start.20 = (f32[64]{0:T(128)S(1)}, f32[64]{0:T(128)}, u32[]{:S(2)}) copy-start(f32[64]{0:T(128)} %param.32) | copy-start | bytes 772
  47.6 6.2 %copy-start.24 = (f32[256]{0:T(256)S(1)}, f32[256]{0:T(256)}, u32[]{:S(2)}) copy-start(f32[256]{0:T(256)} %param.35) | copy-start | bytes 3076
  47.6 22.3 %all-to-all-start.2 = ((bf16[64,3,4,128]{3,2,1,0:T(4,128)(2,1)}), bf16[64,3,4,128]{3,2,1,0:T(4,128)(2,1)S(1)}, u32[]{:S(2)}, u32[]{:S(2)}) async-start(bf16[64,3,4,128]{3,2,1,0:T(4,128)(2,1)} %bitcast.16), calls=%async_computation.2 | async-start | bytes 393216 | tf_op jit(solution)/shard_map/all_to_all | solution.py:503
  53.7 0.7 copy-start.12
  53.7 0.7 copy-start.18
  54.4 15.5 %copy-start.5 = (f32[64,128]{1,0:T(8,128)S(1)}, f32[64,128]{1,0:T(8,128)}, u32[]{:S(2)}) copy-start(f32[64,128]{1,0:T(8,128)} %demand.3) | copy-start | bytes 98308
  93.6 11.9 %all-to-all-start.4 = ((f32[8,8,128]{2,1,0:T(8,128)}), f32[8,8,128]{2,1,0:T(8,128)S(1)}, u32[]{:S(2)}, u32[]{:S(2)}) async-start(f32[8,8,128]{2,1,0:T(8,128)} %shard_map.267), calls=%async_computation.4 | async-start | bytes 65536 | tf_op jit(solution)/shard_map/all_to_all | solution.py:508

commit v6 on v1

--- a/solution.py
+++ b/solution.py
@@ -6,7 +6,6 @@
 from jax.sharding import PartitionSpec as P
 
 LINK_CAP = 4
-PACK = 3 * LINK_CAP
 GROUP = 16
 step_size = 0.2
 F32 = jnp.float32
@@ -14,8 +13,10 @@
 I32 = jnp.int32
 REGIONS, SEASONS = 64, 8
 BUS, SLOT, HOUR = 64, 256, 128
-PACKED = GROUP * PACK
-UNPACKED = 2 * GROUP * LINK_CAP + GROUP
+LINES = GROUP * LINK_CAP
+ROWS_EACH = 2 * LINK_CAP + 2
+PACKED = GROUP * ROWS_EACH
+UNPACKED = 2 * LINES + GROUP
 
 
 def iota(shape, axis):
@@ -63,28 +64,56 @@
     return jnp.concatenate([ref[0:1, :], ref[1:2, :]], axis=1)
 
 
+def flip_bits(value):
+    flipped = value & 0
+    for bit in range(6):
+        flipped = flipped | (((value >> bit) & 1) << (5 - bit))
+    return flipped
+
+
+def region_at(place):
+    return flip_bits(place ^ (place >> 1))
+
+
+def place_of(region):
+    place = flip_bits(region)
+    for shift in (1, 2, 4):
+        place = place ^ (place >> shift)
+    return place
+
+
+def order_out():
+    shape = (SLOT, SLOT)
+    slot = iota((1, SLOT), 1)
+    return as_bf(iota(shape, 0) == LINK_CAP * place_of(slot >> 2) + (slot & 3))
+
+
+def order_in():
+    shape = (SLOT, SLOT)
+    at = iota((1, SLOT), 1)
+    return as_bf(iota(shape, 0) == LINK_CAP * region_at(at >> 2) + (at & 3))
+
+
 def pack_target(packed):
-    q = lax.shift_right_logical(packed * 171, 11)
-    j = packed - PACK * q
+    q = (packed * (262144 // ROWS_EACH + 1)) >> 18
+    j = packed - ROWS_EACH * q
     first = LINK_CAP * q + j
-    second = GROUP * LINK_CAP + LINK_CAP * q + j - LINK_CAP
-    third = 2 * GROUP * LINK_CAP + q
-    return jnp.where(
-        j < LINK_CAP,
-        first,
-        jnp.where(j < 2 * LINK_CAP, second, jnp.where(j == 2 * LINK_CAP, third, -1)),
-    )
+    second = LINES + first - LINK_CAP
+    third = jnp.where(j == 2 * LINK_CAP, 2 * LINES + q, -1)
+    return jnp.where(j < LINK_CAP, first, jnp.where(j < 2 * LINK_CAP, second, third))
 
 
 def pack(first, second, third, out_ref):
+    order = order_out()
+    first = narrow(dot(order, first))
+    second = narrow(dot(order, second))
     shape = (PACKED, UNPACKED)
     place = as_bf(pack_target(iota(shape, 0)) == iota(shape, 1))
-    lines = GROUP * LINK_CAP
     for g in range(REGIONS // GROUP):
         rows = jnp.concatenate(
             [
-                first[g * lines : (g + 1) * lines],
-                second[g * lines : (g + 1) * lines],
+                first[g * LINES : (g + 1) * LINES],
+                second[g * LINES : (g + 1) * LINES],
                 third[g * GROUP : (g + 1) * GROUP],
             ],
             axis=0,
@@ -96,13 +125,13 @@
     shape = (UNPACKED, PACKED)
     place = as_bf(pack_target(iota(shape, 1)) == iota(shape, 0))
     parts = [
-        dot(place, ref[g * PACKED : (g + 1) * PACKED, :]) for g in range(REGIONS // GROUP)
+        narrow(dot(place, ref[g * PACKED : (g + 1) * PACKED, :])) for g in range(REGIONS // GROUP)
     ]
-    lines = GROUP * LINK_CAP
-    first = jnp.concatenate([p[:lines] for p in parts], axis=0)
-    second = jnp.concatenate([p[lines : 2 * lines] for p in parts], axis=0)
-    third = jnp.concatenate([p[2 * lines :] for p in parts], axis=0)
-    return first, second, third
+    order = order_in()
+    first = jnp.concatenate([p[:LINES] for p in parts], axis=0)
+    second = jnp.concatenate([p[LINES : 2 * LINES] for p in parts], axis=0)
+    third = jnp.concatenate([p[2 * LINES :] for p in parts], axis=0)
+    return dot(order, first), dot(order, second), third
 
 
 def columns(ref):
@@ -142,15 +171,18 @@
     leave[...] = leave_t
     high = wide(narrow(limit))
     low = limit - high
+    sending = as_bf(
+        iota((REGIONS, SLOT), 0) == place_of(iota((1, SLOT), 1) >> 2)
+    )
     held = jnp.zeros((REGIONS, 128), F32)
     slot_kind = iota((SLOT, 128), 0) & (LINK_CAP - 1)
     for at, value in enumerate((wide(row256(line_to)), high, low)):
         spots = as_bf(iota((SLOT, 128), 1) == slot_kind + LINK_CAP * at)
-        held = held + dot(spread * narrow(value), spots)
+        held = held + dot(sending * narrow(value), spots)
     pack(narrow(f0), near, narrow(held), sent)
 
 
-def season_block(sums, level, dual_f, link_column, sent, move_row=None):
+def season_block(sums, level, dual_f, link_column):
     lane = iota((128, 128), 1)
     tail = jnp.concatenate([level[:, HOUR - 1 : HOUR], dual_f[:, HOUR - 1 : HOUR]], axis=0)
     head = jnp.concatenate([dual_f[:, 0:1], link_column], axis=0)
@@ -166,23 +198,25 @@
     turn[0:1, 0:BUS] = wide(link[...])
     turned = columns(turn)
     sums = jnp.sum(wide(avail[...]) * wide(narrow(scarcity[...])), axis=1, keepdims=True)
-    rows = season_block(sums, soc[...], wide(narrow(soc_dual[...])), turned[:BUS, 0:1], sent)
+    rows = season_block(sums, soc[...], wide(narrow(soc_dual[...])), turned[:BUS, 0:1])
     for s in range(SEASONS):
         sent[s] = rows
 
 
-def ends_in(got, price, sent, arrive, cap):
+def ends_in(got, price, sent, far, arrive, cap):
     _, _, held = unpack(got)
     shape = (SLOT, REGIONS)
-    spread = as_bf(iota(shape, 1) == lax.shift_right_logical(iota(shape, 0), 2))
-    lines = dot(spread, narrow(held))
+    spread = as_bf(region_at(iota((1, REGIONS), 1)) == iota(shape, 0) >> 2)
+    lines = dot(spread, held)
     lane = iota((SLOT, 128), 1)
     kind = iota((SLOT, 128), 0) & (LINK_CAP - 1)
     ends = jnp.sum(jnp.where(lane == kind, lines, 0.0), axis=1, keepdims=True)
     limits = (lane == kind + LINK_CAP) | (lane == kind + 2 * LINK_CAP)
     limit = jnp.sum(jnp.where(limits, lines, 0.0), axis=1, keepdims=True)
     arrive_t = onehot_rows(ends, BUS)
-    sent[...] = narrow(dot(arrive_t, narrow(price[...])))
+    values = narrow(dot(arrive_t, narrow(price[...])))
+    far[...] = values
+    sent[...] = narrow(dot(order_out(), values))
     arrive[...] = arrive_t
     cap[...] = jnp.broadcast_to(limit, (SLOT, HOUR))
 
@@ -276,7 +310,7 @@
     for ref, value in zip((disp1, build1, disch1, level1, scarce1, sdual1), halves):
         ref[...] = value
     sums = jnp.sum(wide(avail[...]) * wide(narrow(halves[4])), axis=1, keepdims=True)
-    rows[...] = season_block(sums, halves[3], wide(narrow(halves[5])), link_c, None)
+    rows[...] = season_block(sums, halves[3], wide(narrow(halves[5])), link_c)
     primal = (
         square(halves[0], state[0])
         + square(halves[1], state[1]) * (1.0 / SEASONS)
@@ -294,7 +328,8 @@
 ):
     f0 = flow0[...]
     leave_t = leave[...]
-    moved, flow_x = line_step(f0, wide(near0[...]), wide(got[...]), cap[...], step_size)
+    far = dot(order_in(), got[...])
+    moved, flow_x = line_step(f0, wide(near0[...]), far, cap[...], step_size)
     f1 = mean(moved, f0)
     flow1[...] = f1
     p0 = price[...]
@@ -319,10 +354,9 @@
 
 
 def moves_out(got, rows, sent):
-    shape = (8, REGIONS * PACK)
-    at = iota(shape, 1)
-    q = lax.shift_right_logical(at * 21846, 18)
-    mask = as_bf(at - PACK * q == 2 * LINK_CAP)
+    at = iota((8, REGIONS * ROWS_EACH), 1)
+    q = (at * (262144 // ROWS_EACH + 1)) >> 18
+    mask = as_bf(at - ROWS_EACH * q == 2 * LINK_CAP)
     moves = dot(mask, got[...])
     held = jnp.where(iota((8, 128), 0) == 4, moves, rows[...])
     for s in range(SEASONS):
@@ -374,9 +408,10 @@
     )(*operands)
 
 
-def region_exchange(value, per_pair):
-    cut = value.reshape(REGIONS, per_pair, LINK_CAP, HOUR)
-    got = lax.all_to_all(cut, "region", split_axis=0, concat_axis=0, tiled=True)
+def region_exchange(value, rows, per_pair):
+    cut = value.reshape(REGIONS, per_pair, rows, HOUR)
+    members = [[region_at(place) for place in range(REGIONS)]]
+    got = lax.all_to_all(cut, "region", 0, 0, axis_index_groups=members, tiled=True)
     return got.reshape(value.shape)
 
 
@@ -415,7 +450,7 @@
     lines_b = ((SLOT, HOUR), BF16)
     buses = ((BUS, HOUR), F32)
     picks = ((SLOT, BUS), BF16)
-    packed = ((REGIONS * PACK, HOUR), BF16)
+    packed = ((REGIONS * ROWS_EACH, HOUR), BF16)
     seasons = ((SEASONS, 8, 128), F32)
     consts = (
         avail,
@@ -438,11 +473,13 @@
         link_count,
         turn=True,
     )
-    got1 = region_exchange(sent1, 3)
+    got1 = region_exchange(sent1, 2, 5)
     (rows1,) = call(season_out, [seasons], avail, scarcity, soc, soc_dual, link, turn=True)
     season1 = season_exchange(rows1)
-    sent2, arrive, came_cap = call(ends_in, [lines_b, picks, lines], got1, price)
-    got2 = region_exchange(sent2, 1)
+    sent2, came_far0, arrive, came_cap = call(
+        ends_in, [lines_b, lines_b, picks, lines], got1, price
+    )
+    got2 = region_exchange(sent2, LINK_CAP, 1)
     disp1, build1, disch1, level1, scarce1, sdual1, came1, balance, rows2, moves = call(
         first_local,
         [lines, ((2, 128), F32), buses, buses, lines, buses, lines, buses, ((8, 128), F32), ((8, 128), F32)],
@@ -459,7 +496,7 @@
         got1,
         arrive,
         came_cap,
-        sent2,
+        came_far0,
         scalar=True,
         turn=True,
     )
@@ -477,7 +514,7 @@
         balance,
         moves,
     )
-    got3 = region_exchange(sent3, 3)
+    got3 = region_exchange(sent3, 2, 5)
     (rows3,) = call(moves_out, [seasons], got3, rows2)
     season2 = season_exchange(rows3)
     disp2, build2, flow2, disch2, level2, price2, scarce2, sdual2 = call(

time: 106 us -> 104 us (0.981)
  waiting for transfers between devices: 29.5 us -> 28.2 us
    all_to_all x1, blocking collectives: 19.8 us -> 18 us  [region_exchange(): lax.all_to_all(cut, 'region', 0, 0, axis_index_groups=members, tiled=True)]
    all_to_all x1, blocking collectives: 10.9 us -> 12.3 us  [season_exchange(): lax.all_to_all(value, 'season', split_axis=0, concat_axis=0, tiled=True)]
    all_to_all x2, waiting for transfers between devices: 26 us -> 24.9 us  [region_exchange(): lax.all_to_all(cut, 'region', 0, 0, axis_index_groups=members, tiled=True)]
  transfers between devices with their start and end apart: 3 -> 3, of which waited for: 3 -> 3; matrix products, arithmetic and copies ran while one was open for 0% -> 0% of each run, Pallas kernels for 4% -> 3%
where the time goes in v6:
time: 104 us; the launch traced here: 103 us
  starting transfers between devices  32.5 us (31%)
  blocking collectives  30.3 us (29%)
  waiting for transfers between devices  28.2 us (27%)
  Pallas kernels  7.59 us (7%)
  local copies, waits for them, and re-layouts  3.67 us (4%)
    all_to_all x2, starting transfers between devices, region_exchange(): lax.all_to_all(cut, 'region', 0, 0, axis_index_groups=members, tiled=True)  25.6 us
    all_to_all x2, waiting for transfers between devices, region_exchange(): lax.all_to_all(cut, 'region', 0, 0, axis_index_groups=members, tiled=True)  24.9 us
    all_to_all x1, blocking collectives, region_exchange(): lax.all_to_all(cut, 'region', 0, 0, axis_index_groups=members, tiled=True)  18 us
    all_to_all x1, blocking collectives, season_exchange(): lax.all_to_all(value, 'season', split_axis=0, concat_axis=0, tiled=True)  12.3 us
    pallas_call x7, Pallas kernels, call(): pl.pallas_call(body, out_shape=[jax.ShapeDtypeStruct(shape, kind) for sha...  7.59 us
    all_to_all x1, starting transfers between devices, season_exchange(): lax.all_to_all(value, 'season', split_axis=0, concat_axis=0, tiled=True)  6.91 us
    unnamed x44, local copies, waits for them, and re-layouts  3.67 us
    all_to_all x1, waiting for transfers between devices, season_exchange(): lax.all_to_all(value, 'season', split_axis=0, concat_axis=0, tiled=True)  3.31 us
  transfers between devices with their start and end apart: 3, of which 3 were waited for; matrix products, arithmetic and copies ran while one was open for 0% of the time, Pallas kernels for 3%

profile of v6, /device:TPU:1, one launch (start us, length us, event | category | flops | bytes accessed | tf_op | source)
XLA Modules:
  0.0 103.1 jit_solution(2193873153963676380)
XLA Ops:
  0.6 0.0 copy-start.18
  0.6 0.0 copy-start.19
  0.7 0.0 copy-start.17
  0.7 0.0 copy-start.21
  0.7 0.6 copy-done.18
  1.3 0.0 copy-done.19
  1.3 0.0 copy-done.17
  1.3 0.0 copy-done.21
  1.3 0.0 copy-start.2
  1.4 0.8 copy-done.2
  2.1 0.0 copy-start.8
  2.1 0.9 copy-done.8
  3.0 1.5 %shard_map.261 = (bf16[640,128]{1,0:T(8,128)(2,1)}, f32[256,128]{1,0:T(8,128)S(1)}, bf16[256,128]{1,0:T(8,128)(2,1)S(1)}, f32[256,128]{1,0:T(8,128)S(1)}, bf16[256,64]{1,0:T(8,128)(2,1)S(1)}) custom-call(f32[256,128]{1,0:T(8,128)S(1)} %copy-done.8, f32[64,128]{1,0:T(8,128)S(1)} %copy-done.2, s32[2,128]{1,0:T(2,128)S(1)} %bitcast.42, s32[2,128]{1,0:T(2,128)S(1)} %bitcast.43, ...), custom_call_target="tpu_custom_call" | custom-call | tf_op jit(solution)/shard_map/pallas_call | solution.py:401
  4.5 0.0 copy-start
  4.5 0.0 copy-start.1
  4.5 0.0 copy-start.5
  4.5 0.0 copy-start.6
  4.5 19.4 %all-to-all-start.1 = ((bf16[64,5,2,128]{3,2,1,0:T(2,128)(2,1)}), bf16[64,5,2,128]{3,2,1,0:T(2,128)(2,1)S(1)}, u32[]{:S(2)}, u32[]{:S(2)}) async-start(bf16[64,5,2,128]{3,2,1,0:T(2,128)(2,1)} %bitcast.12), calls=%async_computation.1 | async-start | bytes 327680 | tf_op jit(solution)/shard_map/all_to_all | solution.py:414
  24.0 0.0 copy-start.10
  24.0 0.0 copy-done
  24.0 0.0 copy-done.1
  24.0 0.0 copy-done.5
  24.0 0.0 copy-done.6
  24.0 0.6 copy-done.10
  24.6 0.9 shard_map.260
  25.5 0.0 copy-start.3
  25.5 13.7 %all-to-all-done.1 = bf16[64,5,2,128]{3,2,1,0:T(2,128)(2,1)S(1)} async-done(((bf16[64,5,2,128]{3,2,1,0:T(2,128)(2,1)}), bf16[64,5,2,128]{3,2,1,0:T(2,128)(2,1)S(1)}, u32[]{:S(2)}, u32[]{:S(2)}) %all-to-all-start.1) | async-done | bytes 163872 | tf_op jit(solution)/shard_map/all_to_all | solution.py:414
  39.2 6.9 %all-to-all-start = ((f32[8,8,128]{2,1,0:T(8,128)}), f32[8,8,128]{2,1,0:T(8,128)S(1)}, u32[]{:S(2)}, u32[]{:S(2)}) async-start(f32[8,8,128]{2,1,0:T(8,128)} %shard_map.260), calls=%async_computation | async-start | bytes 65536 | tf_op jit(solution)/shard_map/all_to_all | solution.py:419
  46.1 0.0 copy-done.3
  46.1 0.0 copy-start.4
  46.1 1.4 %shard_map.262 = (bf16[256,128]{1,0:T(8,128)(2,1)}, bf16[256,128]{1,0:T(8,128)(2,1)S(1)}, bf16[256,64]{1,0:T(8,128)(2,1)S(1)}, f32[256,128]{1,0:T(8,128)S(1)}) custom-call(bf16[640,128]{1,0:T(8,128)(2,1)S(1)} %bitcast.21, f32[64,128]{1,0:T(8,128)S(1)} %copy-done.3), custom_call_target="tpu_custom_call" | custom-call | tf_op jit(solution)/shard_map/pallas_call | solution.py:401
  47.5 3.3 %all-to-all-done.got = f32[8,8,128]{2,1,0:T(8,128)S(1)} async-done(((f32[8,8,128]{2,1,0:T(8,128)}), f32[8,8,128]{2,1,0:T(8,128)S(1)}, u32[]{:S(2)}, u32[]{:S(2)}) %all-to-all-start) | async-done | bytes 32800 | tf_op jit(solution)/shard_map/all_to_all | solution.py:419
  50.8 0.0 copy-start.9
  50.8 6.2 %all-to-all-start.2 = ((bf16[64,1,4,128]{3,2,1,0:T(4,128)(2,1)}), bf16[64,1,4,128]{3,2,1,0:T(4,128)(2,1)S(1)}, u32[]{:S(2)}, u32[]{:S(2)}) async-start(bf16[64,1,4,128]{3,2,1,0:T(4,128)(2,1)} %bitcast.15), calls=%async_computation.2 | async-start | bytes 131072 | tf_op jit(solution)/shard_map/all_to_all | solution.py:414
  57.0 0.0 copy-start.12
  57.0 0.0 copy-start.13
  57.1 0.0 copy-start.15
  57.1 0.0 copy-start.16
  57.1 0.0 copy-start.20
  57.1 0.0 copy-start.11
  57.1 0.0 copy-start.14
  57.1 0.0 copy-done.4
  57.1 0.0 copy-done.9
  57.1 0.6 copy-done.12
  57.7 0.0 copy-done.13
  57.7 0.0 copy-done.15
  57.7 0.0 copy-done.16
  57.7 0.0 copy-done.20
  57.8 0.0 copy-done.11
  57.8 0.0 copy-done.14
  57.8 0.0 copy-start.7
  57.8 1.0 shard_map.263
  58.8 11.2 %all-to-all-done.2 = bf16[64,1,4,128]{3,2,1,0:T(4,128)(2,1)S(1)} async-done(((bf16[64,1,4,128]{3,2,1,0:T(4,128)(2,1)}), bf16[64,1,4,128]{3,2,1,0:T(4,128)(2,1)S(1)}, u32[]{:S(2)}, u32[]{:S(2)}) %all-to-all-start.2) | async-done | bytes 65568 | tf_op jit(solution)/shard_map/all_to_all | solution.py:414
  70.0 0.0 copy-done.7
  70.0 0.9 shard_map.264
  70.9 18.0 %all_to_all.25 = bf16[64,5,2,128]{3,2,1,0:T(2,128)(2,1)S(1)} all-to-all(bf16[64,5,2,128]{3,2,1,0:T(2,128)(2,1)S(1)} %bitcast.26), channel_id=1, replica_groups={{0,256,384,128,192,448,320,64,96,352,480,224,160,416,288,32,48,304,432,..., dimensions={0} | all-to-all | bytes 327680 | tf_op jit(solution)/shard_map/all_to_all | solution.py:414
  88.9 0.1 shard_map.265
  89.0 12.3 %all_to_all.26.got = f32[8,8,128]{2,1,0:T(8,128)S(1)} all-to-all(f32[8,8,128]{2,1,0:T(8,128)S(1)} %shard_map.265), channel_id=1, replica_groups=mesh['region'=64,'season'=8] {'season'}, dimensions={0} | all-to-all | bytes 65536 | tf_op jit(solution)/shard_map/all_to_all | solution.py:419
  101.3 1.8 %shard_map.266 = (f32[256,128]{1,0:T(8,128)}, f32[2,128]{1,0:T(2,128)}, f32[256,128]{1,0:T(8,128)}, f32[64,128]{1,0:T(8,128)}, f32[64,128]{1,0:T(8,128)}, /*inde...) custom-call(s32[1]{0:T(128)} %bitcast.season, bf16[256,128]{1,0:T(8,128)(2,1)S(1)} %copy-done, ...), custom_call_target="tpu_custom_call" | custom-call | tf_op jit(solution)/shard_map/pallas_call | solution.py:401
Async XLA Ops:
  0.6 0.7 copy-start.18
  0.6 0.7 copy-start.19
  0.7 0.7 copy-start.17
  0.7 0.7 copy-start.21
  1.3 0.8 copy-start.2
  2.1 0.9 copy-start.8
  4.5 19.5 %copy-start = (bf16[256,128]{1,0:T(8,128)(2,1)S(1)}, bf16[256,128]{1,0:T(8,128)(2,1)}, u32[]{:S(2)}) copy-start(bf16[256,128]{1,0:T(8,128)(2,1)} %avail.5) | copy-start | bytes 196612
  4.5 19.5 %copy-start.1 = (f32[256,128]{1,0:T(8,128)S(1)}, f32[256,128]{1,0:T(8,128)}, u32[]{:S(2)}) copy-start(f32[256,128]{1,0:T(8,128)} %scarce.1) | copy-start | bytes 393220
  4.5 19.5 %copy-start.5 = (f32[64,128]{1,0:T(8,128)S(1)}, f32[64,128]{1,0:T(8,128)}, u32[]{:S(2)}) copy-start(f32[64,128]{1,0:T(8,128)} %level.1) | copy-start | bytes 98308
  4.5 19.5 %copy-start.6 = (f32[64,128]{1,0:T(8,128)S(1)}, f32[64,128]{1,0:T(8,128)}, u32[]{:S(2)}) copy-start(f32[64,128]{1,0:T(8,128)} %sdual.1) | copy-start | bytes 98308
  4.5 34.6 %all-to-all-start.1 = ((bf16[64,5,2,128]{3,2,1,0:T(2,128)(2,1)}), bf16[64,5,2,128]{3,2,1,0:T(2,128)(2,1)S(1)}, u32[]{:S(2)}, u32[]{:S(2)}) async-start(bf16[64,5,2,128]{3,2,1,0:T(2,128)(2,1)} %bitcast.12), calls=%async_computation.1 | async-start | bytes 327680 | tf_op jit(solution)/shard_map/all_to_all | solution.py:414
  24.0 0.7 copy-start.10
  25.5 20.6 %copy-start.3 = (f32[64,128]{1,0:T(8,128)S(1)}, f32[64,128]{1,0:T(8,128)}, u32[]{:S(2)}) copy-start(f32[64,128]{1,0:T(8,128)} %price.7) | copy-start | bytes 98308
  39.2 11.6 %all-to-all-start = ((f32[8,8,128]{2,1,0:T(8,128)}), f32[8,8,128]{2,1,0:T(8,128)S(1)}, u32[]{:S(2)}, u32[]{:S(2)}) async-start(f32[8,8,128]{2,1,0:T(8,128)} %shard_map.260), calls=%async_computation | async-start | bytes 65536 | tf_op jit(solution)/shard_map/all_to_all | solution.py:419
  46.1 11.0 %copy-start.4 = (f32[256,128]{1,0:T(8,128)S(1)}, f32[256,128]{1,0:T(8,128)}, u32[]{:S(2)}) copy-start(f32[256,128]{1,0:T(8,128)} %disp.1) | copy-start | bytes 393220
  50.8 6.3 %copy-start.9 = (f32[64,128]{1,0:T(8,128)S(1)}, f32[64,128]{1,0:T(8,128)}, u32[]{:S(2)}) copy-start(f32[64,128]{1,0:T(8,128)} %disch.1) | copy-start | bytes 98308
  50.8 19.2 %all-to-all-start.2 = ((bf16[64,1,4,128]{3,2,1,0:T(4,128)(2,1)}), bf16[64,1,4,128]{3,2,1,0:T(4,128)(2,1)S(1)}, u32[]{:S(2)}, u32[]{:S(2)}) async-start(bf16[64,1,4,128]{3,2,1,0:T(4,128)(2,1)} %bitcast.15), calls=%async_computation.2 | async-start | bytes 131072 | tf_op jit(solution)/shard_map/all_to_all | solution.py:414
  57.0 0.7 copy-start.12
  57.0 0.7 copy-start.13
  57.1 0.7 copy-start.15
  57.1 0.7 copy-start.16
  57.1 0.7 copy-start.20
  57.1 0.7 copy-start.11
  57.1 0.7 copy-start.14
  57.8 12.2 %copy-start.7 = (f32[64,128]{1,0:T(8,128)S(1)}, f32[64,128]{1,0:T(8,128)}, u32[]{:S(2)}) copy-start(f32[64,128]{1,0:T(8,128)} %demand.3) | copy-start | bytes 98308

commit v7 on v3

--- a/solution.py
+++ b/solution.py
@@ -14,8 +14,9 @@
 REGIONS, SEASONS = 64, 8
 BUS, SLOT, HOUR = 64, 256, 128
 LINES = GROUP * LINK_CAP
-WITH_FLOWS = (LINK_CAP, LINK_CAP, LINK_CAP)
-WITH_MOVES = (LINK_CAP, LINK_CAP, 2)
+HALF = 64
+WITH_FLOWS = (LINK_CAP, LINK_CAP, LINK_CAP, 1, 1)
+WITH_MOVES = (LINK_CAP, LINK_CAP, 1, 1)
 
 
 def iota(shape, axis):
@@ -63,48 +64,40 @@
     return jnp.concatenate([ref[0:1, :], ref[1:2, :]], axis=1)
 
 
-def sizes(kinds):
-    return GROUP * sum(kinds), 2 * LINES + GROUP * (LINK_CAP if kinds[2] == LINK_CAP else 1)
-
-
 def pack_target(packed, kinds):
     rows = sum(kinds)
-    q = lax.shift_right_logical(packed * (21846 * 12 // rows + 1), 18)
+    q = (packed * (262144 // rows + 1)) >> 18
     j = packed - rows * q
-    first = LINK_CAP * q + j
-    second = LINES + first - LINK_CAP
-    if kinds[2] == LINK_CAP:
-        third = 2 * LINES + first - 2 * LINK_CAP
-    else:
-        third = jnp.where(j == 2 * LINK_CAP, 2 * LINES + q, -1)
-    return jnp.where(j < LINK_CAP, first, jnp.where(j < 2 * LINK_CAP, second, third))
-
-
-def pack(first, second, third, out_ref, kinds):
-    shape = sizes(kinds)
-    place = as_bf(pack_target(iota(shape, 0), kinds) == iota(shape, 1))
-    thirds = shape[1] - 2 * LINES
+    target = packed * 0 - 1
+    row, held = 0, 0
+    for count in kinds:
+        inside = (j >= row) & (j < row + count)
+        target = jnp.where(inside, held + count * q + j - row, target)
+        row += count
+        held += count * GROUP
+    return target
+
+
+def pack(parts, out_ref, kinds):
+    size = GROUP * sum(kinds)
+    place = as_bf(pack_target(iota((size, size), 0), kinds) == iota((size, size), 1))
     for g in range(REGIONS // GROUP):
         rows = jnp.concatenate(
-            [
-                first[g * LINES : (g + 1) * LINES],
-                second[g * LINES : (g + 1) * LINES],
-                third[g * thirds : (g + 1) * thirds],
-            ],
-            axis=0,
+            [part[g * n * GROUP : (g + 1) * n * GROUP] for part, n in zip(parts, kinds)], axis=0
         )
-        out_ref[g * shape[0] : (g + 1) * shape[0], :] = narrow(dot(place, rows))
+        out_ref[g * size : (g + 1) * size, :] = narrow(dot(place, rows))
 
 
 def unpack(ref, kinds):
-    packed, unpacked = sizes(kinds)
-    shape = (unpacked, packed)
-    place = as_bf(pack_target(iota(shape, 1), kinds) == iota(shape, 0))
-    parts = [dot(place, ref[g * packed : (g + 1) * packed, :]) for g in range(REGIONS // GROUP)]
-    first = jnp.concatenate([p[:LINES] for p in parts], axis=0)
-    second = jnp.concatenate([p[LINES : 2 * LINES] for p in parts], axis=0)
-    third = jnp.concatenate([p[2 * LINES :] for p in parts], axis=0)
-    return first, second, third
+    size = GROUP * sum(kinds)
+    place = as_bf(pack_target(iota((size, size), 1), kinds) == iota((size, size), 0))
+    groups = [dot(place, ref[g * size : (g + 1) * size, :]) for g in range(REGIONS // GROUP)]
+    parts = []
+    held = 0
+    for n in kinds:
+        parts.append(jnp.concatenate([p[held : held + n * GROUP] for p in groups], axis=0))
+        held += n * GROUP
+    return parts
 
 
 def pieces(value):
@@ -138,7 +131,19 @@
     return spread, live, row256(line_limit) * live
 
 
-def ends_out(line_to, line_limit, link_count, sent):
+def season_block(sums, level, dual_f, link_column):
+    lane = iota((HALF, 128), 1)
+    held = jnp.zeros((HALF, 128), F32)
+    eighths = [sums[HALF * n : HALF * (n + 1)] for n in range(4)]
+    eighths += [level[:, HOUR - 1 : HOUR], dual_f[:, HOUR - 1 : HOUR], dual_f[:, 0:1], link_column]
+    for at, eighth in enumerate(eighths):
+        held = jnp.where(lane == at, eighth, held)
+    return jnp.transpose(jnp.concatenate([jnp.zeros((HALF, 128), F32), held], axis=0))[0:8]
+
+
+def ends_out(
+    line_to, line_limit, link_count, avail, scarcity, soc, soc_dual, link, sent, turn
+):
     spread, _, limit = live_limit(line_limit, link_count)
     lane = iota((SLOT, 128), 1)
     kind = iota((SLOT, 128), 0) & (LINK_CAP - 1)
@@ -146,7 +151,15 @@
     spots = as_bf(lane == kind + LINK_CAP)
     for part in pieces(limit):
         held = held + dot(spread * part, spots)
-    sent[...] = held
+    turn[0:1, 0:BUS] = wide(link[...])
+    turned = columns(turn)
+    sums = jnp.sum(wide(avail[...]) * wide(narrow(scarcity[...])), axis=1, keepdims=True)
+    block = season_block(sums, soc[...], wide(narrow(soc_dual[...])), turned[:BUS, 0:1])
+    eighth = iota((REGIONS, 128), 0) >> 3
+    handed = jnp.zeros((REGIONS, 128), F32)
+    for at in range(8):
+        handed = jnp.where(eighth == at, block[at : at + 1], handed)
+    sent[...] = jnp.where(iota((REGIONS, 128), 1) < HALF, held, handed)
 
 
 def lines_near(
@@ -166,25 +179,6 @@
     leave[...] = leave_t
 
 
-def season_block(sums, level, dual_f, link_column):
-    lane = iota((128, 128), 1)
-    tail = jnp.concatenate([level[:, HOUR - 1 : HOUR], dual_f[:, HOUR - 1 : HOUR]], axis=0)
-    head = jnp.concatenate([dual_f[:, 0:1], link_column], axis=0)
-    held = jnp.where(
-        lane == 0,
-        sums[:128],
-        jnp.where(lane == 1, sums[128:], jnp.where(lane == 2, tail, jnp.where(lane == 3, head, 0.0))),
-    )
-    return jnp.transpose(held)[0:8]
-
-
-def season_out(avail, scarcity, soc, soc_dual, link, sent, turn):
-    turn[0:1, 0:BUS] = wide(link[...])
-    turned = columns(turn)
-    sums = jnp.sum(wide(avail[...]) * wide(narrow(scarcity[...])), axis=1, keepdims=True)
-    sent[0] = season_block(sums, soc[...], wide(narrow(soc_dual[...])), turned[:BUS, 0:1])
-
-
 def ends_in(got, price, flow0, near0, sent, arrive, cap):
     shape = (SLOT, REGIONS)
     spread = as_bf(iota(shape, 1) == lax.shift_right_logical(iota(shape, 0), 2))
@@ -198,7 +192,23 @@
     far = narrow(dot(arrive_t, narrow(price[...])))
     arrive[...] = arrive_t
     cap[...] = jnp.broadcast_to(limit, (SLOT, HOUR))
-    pack(narrow(flow0[...]), near0[...], far, sent, WITH_FLOWS)
+    turned = jnp.concatenate([wide(middle)[:, HALF:], wide(middle)[:, :HALF]], axis=1)
+    handed = iota((REGIONS, 128), 1) >= HALF
+    both = narrow(jnp.where(handed, wide(high), turned))
+    rest = narrow(jnp.where(handed, wide(low), 0.0))
+    pack((narrow(flow0[...]), near0[...], far, both, rest), sent, WITH_FLOWS)
+
+
+def season_blocks(region, season, both, rest, got):
+    shape = (REGIONS, REGIONS)
+    row = iota(shape, 0)
+    offset = season + region - (row >> 3)
+    order = as_bf(8 * (row & 7) + (offset & 7) == iota(shape, 1))
+    parts = dot(order, narrow(both))
+    middle = jnp.concatenate([parts[:, HALF:], parts[:, :HALF]], axis=1)
+    value = parts + middle + dot(order, narrow(rest))
+    for s in range(SEASONS):
+        got[s] = value[8 * s : 8 * s + 8]
 
 
 def line_step(flows, near, far, cap, tau):
@@ -212,14 +222,17 @@
     return values[0]
 
 
-def local_step(season, consts, state, price_v, got, turn, tau, sigma, paired):
+def local_step(season, consts, state, price_v, got, turn, tau, sigma):
     avail, asset_bus, run_cost, build_cost, efficiency, power, energy, link = consts
     disp, build, disch, level, scarce, sdual = state
     before_at = (season + SEASONS - 1) & (SEASONS - 1)
     after_at = (season + 1) & (SEASONS - 1)
-    if paired:
-        before_at, after_at = before_at ^ season, after_at ^ season
-    sums = tree([got[s, 0:2] for s in range(SEASONS)])
+    parts = tree([got[s, 0:4] for s in range(SEASONS)])
+    moved = jnp.concatenate([parts[:, HALF:], parts[:, :HALF]], axis=1)
+    left = iota((1, 128), 1) < HALF
+    sums = jnp.concatenate(
+        [jnp.where(left, moved[n : n + 1], parts[n + 1 : n + 2]) for n in (0, 2)], axis=0
+    )
     grad_build = sums * (1.0 / (HOUR * SEASONS))
     build_new = jnp.maximum(build - tau * (build_cost[...] - grad_build), 0.0)
     turn[0:8, :] = got[before_at]
@@ -241,9 +254,9 @@
     power_c = turned[:BUS, 23:24]
     energy_c = turned[:BUS, 24:25]
     link_c = turned[:BUS, 25:26]
-    before_level, before_dual = turned[:BUS, 2:3], turned[BUS:, 2:3]
-    before_first, before_link = turned[:BUS, 3:4], turned[BUS:, 3:4]
-    after_first, after_link = turned[:BUS, 11:12], turned[BUS:, 11:12]
+    before_level, before_dual = turned[HALF:, 4:5], turned[HALF:, 5:6]
+    before_first, before_link = turned[HALF:, 6:7], turned[HALF:, 7:8]
+    after_first, after_link = turned[HALF:, 14:15], turned[HALF:, 15:16]
     price_b = narrow(price_v)
     dual_f = wide(narrow(sdual))
     grad_dispatch = dot(asset_t, price_b) - wide(narrow(scarce))
@@ -279,19 +292,35 @@
     return balance, halves, link_c
 
 
-def first_local(
-    season, avail, asset_bus, run_cost, build_cost, efficiency, power, energy, link,
-    disp, build, disch, level, scarce, sdual, price, got,
-    disp1, build1, disch1, level1, scarce1, sdual1, balance, rows, moves, turn,
+def first_step(
+    region, season, avail, asset_bus, run_cost, build_cost, efficiency, power, energy, link,
+    disp, build, disch, level, scarce, sdual, price, lines_got, arrive, came_cap,
+    demand, flow0, near0, cap, leave,
+    disp1, build1, disch1, level1, scarce1, sdual1, price1, flow1, came1, far1, rows, sent,
+    turn, got,
 ):
+    f0 = flow0[...]
+    p0 = price[...]
+    leave_t = leave[...]
+    arrive_t = arrive[...]
+    came0, came_near, far, both, rest = unpack(lines_got, WITH_FLOWS)
+    season_blocks(region[0], season[0], both, rest, got)
+    came_far = dot(arrive_t, narrow(p0))
+    came_moved, came_x = line_step(came0, came_near, came_far, came_cap[...], step_size)
+    came1[...] = mean(came_moved, came0)
+    moved, flow_x = line_step(f0, wide(near0[...]), far, cap[...], step_size)
+    f1 = mean(moved, f0)
+    flow1[...] = f1
     consts = (avail, asset_bus, run_cost, build_cost, efficiency, power, energy, link)
     state = (disp[...], build[...], disch[...], level[...], scarce[...], sdual[...])
     local, halves, link_c = local_step(
-        season[0], consts, state, price[...], got, turn, step_size, step_size, True
-    )
-    balance[...] = local
+        season[0], consts, state, p0, got, turn, step_size, step_size
+    )
     for ref, value in zip((disp1, build1, disch1, level1, scarce1, sdual1), halves):
         ref[...] = value
+    whole = local + dot_t(arrive_t, came_x) - dot_t(leave_t, flow_x)
+    p1 = mean(p0 + step_size * (demand[...] - whole), p0)
+    price1[...] = p1
     sums = jnp.sum(wide(avail[...]) * wide(narrow(halves[4])), axis=1, keepdims=True)
     rows[...] = season_block(sums, halves[3], wide(narrow(halves[5])), link_c)
     primal = (
@@ -299,34 +328,11 @@
         + square(halves[1], state[1]) * (1.0 / SEASONS)
         + square(halves[2], state[2])
         + square(halves[3], state[3])
-    )
-    dual = square(halves[4], state[4]) + square(halves[5], state[5])
-    lane = iota((8, 128), 1)
-    moves[...] = jnp.where(lane == 0, primal, dual)
-
-
-def price_step(
-    flow0, near0, cap, leave, arrive, came_cap, got, demand, price, balance, moves,
-    price1, flow1, came1, far1, sent,
-):
-    f0 = flow0[...]
-    p0 = price[...]
-    leave_t = leave[...]
-    arrive_t = arrive[...]
-    came0, came_near, far = unpack(got, WITH_FLOWS)
-    came_far = dot(arrive_t, narrow(p0))
-    came_moved, came_x = line_step(came0, came_near, came_far, came_cap[...], step_size)
-    came1[...] = mean(came_moved, came0)
-    moved, flow_x = line_step(f0, wide(near0[...]), far, cap[...], step_size)
-    f1 = mean(moved, f0)
-    flow1[...] = f1
-    whole = balance[...] + dot_t(arrive_t, came_x) - dot_t(leave_t, flow_x)
-    p1 = mean(p0 + step_size * (demand[...] - whole), p0)
-    price1[...] = p1
-    primal = moves[0:1, 0:1] + square(f1, f0)
-    dual = moves[0:1, 1:2] + square(p1, p0)
-    lane = iota((GROUP, 128), 1)
-    held = jnp.zeros((GROUP, 128), F32)
+        + square(f1, f0)
+    )
+    dual = square(halves[4], state[4]) + square(halves[5], state[5]) + square(p1, p0)
+    lane = iota((REGIONS, 128), 1)
+    held = jnp.zeros((REGIONS, 128), F32)
     for at, value in ((0, primal), (3, dual)):
         for step, piece in enumerate(pieces(value)):
             held = jnp.where(lane == at + step, wide(piece), held)
@@ -335,7 +341,7 @@
     near = narrow(dot(leave_t, price_b))
     far = narrow(dot(arrive_t, price_b))
     far1[...] = far
-    pack(near, far, jnp.concatenate([held] * (REGIONS // GROUP), axis=0), sent, WITH_MOVES)
+    pack((near, far, held, jnp.zeros_like(held)), sent, WITH_MOVES)
 
 
 def moves_out(got, rows, sent):
@@ -345,7 +351,8 @@
     q = lax.shift_right_logical(at * (262144 // rows_each + 1), 18)
     mask = as_bf(at - rows_each * q == 2 * LINK_CAP)
     moves = dot(mask, got[...])
-    held = jnp.where(iota((8, 128), 0) == 4, moves, rows[...])
+    spot = (iota((8, 128), 0) == 0) & (iota((8, 128), 1) < HALF)
+    held = jnp.where(spot, moves, rows[...])
     for s in range(SEASONS):
         sent[s] = held
 
@@ -356,7 +363,7 @@
     came_far, came, demand, flow, cap, leave,
     disp2, build2, flow2, disch2, level2, price2, scarce2, sdual2, turn,
 ):
-    moves = tree([got[s, 4:5] for s in range(SEASONS)])
+    moves = tree([got[s, 0:1] for s in range(SEASONS)])
     primal = moves[:, 0:1] + moves[:, 1:2] + moves[:, 2:3]
     dual = moves[:, 3:4] + moves[:, 4:5] + moves[:, 5:6]
     weight = jnp.sqrt(jnp.sqrt((dual + 1e-06) / (primal + 1e-06)))
@@ -364,7 +371,7 @@
     sigma = step_size * weight
     consts = (avail, asset_bus, run_cost, build_cost, efficiency, power, energy, link)
     state = (disp[...], build[...], disch[...], level[...], scarce[...], sdual[...])
-    came_near, far, _ = unpack(lines_got, WITH_MOVES)
+    came_near, far, _, _ = unpack(lines_got, WITH_MOVES)
     _, came_x = line_step(came[...], came_near, wide(came_far[...]), came_cap[...], tau)
     f1 = flow[...]
     p1 = price[...]
@@ -372,25 +379,39 @@
     near = dot(leave_t, narrow(p1))
     moved, flow_x = line_step(f1, near, far, cap[...], tau)
     flow2[...] = mean(moved, f1)
-    local, halves, _ = local_step(season[0], consts, state, p1, got, turn, tau, sigma, False)
+    local, halves, _ = local_step(season[0], consts, state, p1, got, turn, tau, sigma)
     whole = local + dot_t(arrive[...], came_x) - dot_t(leave_t, flow_x)
     price2[...] = mean(p1 + sigma * (demand[...] - whole), p1)
     for ref, value in zip((disp2, build2, disch2, level2, scarce2, sdual2), halves):
         ref[...] = value
 
 
-def call(body, outs, *operands, scalar=False, turn=False):
-    in_specs = [pl.BlockSpec(memory_space=pltpu.VMEM)] * len(operands)
-    if scalar:
-        in_specs[0] = pl.BlockSpec(memory_space=pltpu.SMEM)
+def call(body, outs, *operands, scalars=0, scratch=()):
+    in_specs = [pl.BlockSpec(memory_space=pltpu.SMEM)] * scalars
+    in_specs += [pl.BlockSpec(memory_space=pltpu.VMEM)] * (len(operands) - scalars)
     return pl.pallas_call(
         body,
         out_shape=[jax.ShapeDtypeStruct(shape, kind) for shape, kind in outs],
         in_specs=in_specs,
         out_specs=[pl.BlockSpec(memory_space=pltpu.VMEM)] * len(outs),
-        scratch_shapes=[pltpu.VMEM((128, 128), F32)] if turn else [],
+        scratch_shapes=[pltpu.VMEM(shape, F32) for shape in scratch],
         compiler_params=pltpu.CompilerParams(vmem_limit_bytes=32 * 1024 * 1024),
     )(*operands)
+
+
+def mixed_exchange(value):
+    members = [
+        [SEASONS * r + (g + r) % SEASONS for r in range(REGIONS)] for g in range(SEASONS)
+    ]
+    got = lax.all_to_all(
+        value.reshape(REGIONS, 1, 128),
+        ("region", "season"),
+        0,
+        0,
+        axis_index_groups=members,
+        tiled=True,
+    )
+    return got.reshape(value.shape)
 
 
 def region_exchange(value, rows, per_pair):
@@ -401,15 +422,6 @@
 
 def season_exchange(value):
     return lax.all_to_all(value, "season", split_axis=0, concat_axis=0, tiled=True)
-
-
-def season_gather(value):
-    apart = 1
-    while apart < SEASONS:
-        pairs = [(s, s ^ apart) for s in range(SEASONS)]
-        value = jnp.concatenate([value, lax.ppermute(value, "season", pairs)], axis=0)
-        apart *= 2
-    return value
 
 
 def on_device(
@@ -436,6 +448,7 @@
     soc_dual,
 ):
     season = lax.axis_index("season").astype(I32).reshape(1)
+    region = lax.axis_index("region").astype(I32).reshape(1)
     pair = lambda v: v.reshape(2, 128)
     short = lambda v: v.reshape(1, BUS)
     link = short(season_link)
@@ -457,12 +470,21 @@
         link,
     )
     limit = pair(line_limit)
-    (sent1,) = call(ends_out, [((REGIONS, 128), F32)], pair(line_to), limit, link_count)
-    got1 = region_exchange(sent1, 1, 1)
-    (rows1,) = call(
-        season_out, [((1, 8, 128), F32)], avail, scarcity, soc, soc_dual, link, turn=True
-    )
-    season1 = season_gather(rows1)
+    turn = (128, 128)
+    (sent1,) = call(
+        ends_out,
+        [((REGIONS, 128), F32)],
+        pair(line_to),
+        limit,
+        link_count,
+        avail,
+        scarcity,
+        soc,
+        soc_dual,
+        link,
+        scratch=[turn],
+    )
+    got1 = mixed_exchange(sent1)
     flow0, near0, cap, leave = call(
         lines_near,
         [lines, lines_b, lines, picks],
@@ -471,16 +493,42 @@
         pair(line_from),
         limit,
         link_count,
-        turn=True,
-    )
-    got1, season1 = lax.optimization_barrier((got1, season1))
+        scratch=[turn],
+    )
     sent2, arrive, came_cap = call(
         ends_in, [rows_of(WITH_FLOWS), picks, lines], got1, price, flow0, near0
     )
-    got2 = region_exchange(sent2, LINK_CAP, 3)
-    disp1, build1, disch1, level1, scarce1, sdual1, balance, rows2, moves = call(
-        first_local,
-        [lines, ((2, 128), F32), buses, buses, lines, buses, buses, pack_row, pack_row],
+    got2 = region_exchange(sent2, 2, 7)
+    (
+        disp1,
+        build1,
+        disch1,
+        level1,
+        scarce1,
+        sdual1,
+        price1,
+        flow1,
+        came1,
+        came_far1,
+        rows2,
+        sent3,
+    ) = call(
+        first_step,
+        [
+            lines,
+            ((2, 128), F32),
+            buses,
+            buses,
+            lines,
+            buses,
+            buses,
+            lines,
+            lines,
+            lines_b,
+            pack_row,
+            rows_of(WITH_MOVES),
+        ],
+        region,
         season,
         *consts,
         dispatch,
@@ -490,24 +538,16 @@
         scarcity,
         soc_dual,
         price,
-        season1,
-        scalar=True,
-        turn=True,
-    )
-    price1, flow1, came1, came_far1, sent3 = call(
-        price_step,
-        [buses, lines, lines, lines_b, rows_of(WITH_MOVES)],
+        got2,
+        arrive,
+        came_cap,
+        demand,
         flow0,
         near0,
         cap,
         leave,
-        arrive,
-        came_cap,
-        got2,
-        demand,
-        price,
-        balance,
-        moves,
+        scalars=2,
+        scratch=[turn, (SEASONS, 8, 128)],
     )
     got3 = region_exchange(sent3, 2, 5)
     (rows3,) = call(moves_out, [seasons], got3, rows2)
@@ -534,8 +574,8 @@
         flow1,
         cap,
         leave,
-        scalar=True,
-        turn=True,
+        scalars=1,
+        scratch=[turn],
     )
     return (disp2, build2.reshape(capacity.shape), flow2, disch2, level2, price2, scarce2, sdual2)
 

time: 109 us -> 104 us (0.954)
  starting transfers between devices: 33.4 us -> 27.2 us
  waiting for transfers between devices: 28 us -> 30.1 us
    all_to_all x0 -> x1, starting transfers between devices: none -> 21.1 us  [mixed_exchange(): lax.all_to_all(value.reshape(REGIONS, 1, 128), ('region', 'season'), 0, 0...]
    all_to_all x2 -> x1, starting transfers between devices: 20.7 us -> 6.08 us  [region_exchange(): got = lax.all_to_all(cut, 'region', split_axis=0, concat_axis=0, tiled=True)]
    ppermute x3 -> x0, starting transfers between devices: 12.7 us -> none  [season_gather(): lax.ppermute(value, 'season', pairs)]
    all_to_all x0 -> x1, waiting for transfers between devices: none -> 12.4 us  [mixed_exchange(): lax.all_to_all(value.reshape(REGIONS, 1, 128), ('region', 'season'), 0, 0...]
    all_to_all x2 -> x1, waiting for transfers between devices: 24.8 us -> 17.6 us  [region_exchange(): got = lax.all_to_all(cut, 'region', split_axis=0, concat_axis=0, tiled=True)]
    ppermute x3 -> x0, waiting for transfers between devices: 3.27 us -> none  [season_gather(): lax.ppermute(value, 'season', pairs)]
    pallas_call x8 -> x6, Pallas kernels: 6.87 us -> 6.69 us  [call(): pl.pallas_call(body, out_shape=[jax.ShapeDtypeStruct(shape, kind) for sha...]
  transfers between devices with their start and end apart: 5 -> 2, of which waited for: 4 -> 2; matrix products, arithmetic and copies ran while one was open for 0% -> 0% of each run, Pallas kernels for 2% -> 0%
where the time goes in v7:
time: 104 us
  blocking collectives  33.7 us (32%)
  waiting for transfers between devices  30.1 us (29%)
  starting transfers between devices  27.2 us (26%)
  Pallas kernels  6.69 us (6%)
  local copies, waits for them, and re-layouts  5.31 us (5%)
    all_to_all x1, blocking collectives, region_exchange(): got = lax.all_to_all(cut, 'region', split_axis=0, concat_axis=0, tiled=True)  22 us
    all_to_all x1, starting transfers between devices, mixed_exchange(): lax.all_to_all(value.reshape(REGIONS, 1, 128), ('region', 'season'), 0, 0...  21.1 us
    all_to_all x1, waiting for transfers between devices, region_exchange(): got = lax.all_to_all(cut, 'region', split_axis=0, concat_axis=0, tiled=True)  17.6 us
    all_to_all x1, waiting for transfers between devices, mixed_exchange(): lax.all_to_all(value.reshape(REGIONS, 1, 128), ('region', 'season'), 0, 0...  12.4 us
    all_to_all x1, blocking collectives, season_exchange(): lax.all_to_all(value, 'season', split_axis=0, concat_axis=0, tiled=True)  11.7 us
    pallas_call x6, Pallas kernels, call(): pl.pallas_call(body, out_shape=[jax.ShapeDtypeStruct(shape, kind) for sha...  6.69 us
    all_to_all x1, starting transfers between devices, region_exchange(): got = lax.all_to_all(cut, 'region', split_axis=0, concat_axis=0, tiled=True)  6.08 us
    unnamed x50, local copies, waits for them, and re-layouts  5.31 us
  transfers between devices with their start and end apart: 2, of which 2 were waited for; matrix products, arithmetic and copies ran while one was open for 0% of the time, Pallas kernels for 0%

profile of v7, /device:TPU:1, one launch (start us, length us, event | category | flops | bytes accessed | tf_op | source)
XLA Modules:
  0.0 103.8 jit_solution(3375762763390397542)
XLA Ops:
  0.6 0.0 copy-start.21
  0.6 0.0 copy-start.22
  0.7 0.0 copy-start.13
  0.7 0.0 copy-start.14
  0.7 0.6 copy-done.21
  1.3 0.0 copy-done.22
  1.3 0.0 copy-done.13
  1.3 0.0 copy-done.14
  1.4 0.0 copy-start
  1.4 0.8 copy-done
  2.2 0.0 copy-start.2
  2.2 0.9 copy-done.2
  3.1 0.0 copy-start.6
  3.1 0.8 copy-done.6
  3.9 0.0 copy-start.8
  3.9 0.8 copy-done.8
  4.6 0.0 copy-start.11
  4.6 1.0 shard_map.260
  5.6 0.0 copy-start.4
  5.6 21.1 %all-to-all-start = ((f32[64,1,128]{2,1,0:T(1,128)}), f32[64,1,128]{2,1,0:T(1,128)S(1)}, u32[]{:S(2)}, u32[]{:S(2)}) async-start(f32[64,1,128]{2,1,0:T(1,128)} %bitcast.13), calls=%async_computation | async-start | bytes 65536 | tf_op jit(solution)/shard_map/all_to_all | solution.py:406
  26.7 0.0 copy-start.23
  26.7 0.0 copy-done.11
  26.7 0.0 copy-done.4
  26.7 0.7 copy-done.23
  27.4 0.5 shard_map.261
  27.9 12.4 %all-to-all-done = f32[64,1,128]{2,1,0:T(1,128)S(1)} async-done(((f32[64,1,128]{2,1,0:T(1,128)}), f32[64,1,128]{2,1,0:T(1,128)S(1)}, u32[]{:S(2)}, u32[]{:S(2)}) %all-to-all-start) | async-done | bytes 32800 | tf_op jit(solution)/shard_map/all_to_all | solution.py:406
  40.3 1.4 %shard_map.262 = (bf16[896,128]{1,0:T(8,128)(2,1)}, bf16[256,64]{1,0:T(8,128)(2,1)S(1)}, f32[256,128]{1,0:T(8,128)S(1)}) custom-call(f32[64,128]{1,0:T(8,128)S(1)} %bitcast.26, f32[64,128]{1,0:T(8,128)S(1)} %copy-done.4, f32[256,128]{1,0:T(8,128)S(1)} %get-tuple-element.35.flow0, bf16[256,128]{1,0:T(8,128)(2,1)S(1)} %get-tuple-element.36.near0), custom_call_target="tpu_custom_call" | custom-call | tf_op jit(solution)/shard_map/pallas_call | solution.py:392
  41.7 0.0 copy-start.1
  41.7 0.0 copy-start.3
  41.7 0.0 copy-start.5
  41.7 0.0 copy-start.9
  41.7 0.0 copy-start.10
  41.7 0.0 copy-start.12
  41.7 6.1 %all-to-all-start.1 = ((bf16[64,7,2,128]{3,2,1,0:T(2,128)(2,1)}), bf16[64,7,2,128]{3,2,1,0:T(2,128)(2,1)S(1)}, u32[]{:S(2)}, u32[]{:S(2)}) async-start(bf16[64,7,2,128]{3,2,1,0:T(2,128)(2,1)} %bitcast.16), calls=%async_computation.1 | async-start | bytes 458752 | tf_op jit(solution)/shard_map/all_to_all | solution.py:419
  47.8 0.0 copy-start.7
  47.8 17.6 %all-to-all-done.1 = bf16[64,7,2,128]{3,2,1,0:T(2,128)(2,1)S(1)} async-done(((bf16[64,7,2,128]{3,2,1,0:T(2,128)(2,1)}), bf16[64,7,2,128]{3,2,1,0:T(2,128)(2,1)S(1)}, u32[]{:S(2)}, u32[]{:S(2)}) %all-to-all-start.1) | async-done | bytes 229408 | tf_op jit(solution)/shard_map/all_to_all | solution.py:419
  65.5 0.0 copy-start.16
  65.5 0.0 copy-start.17
  65.5 0.0 copy-start.19
  65.5 0.0 copy-start.20
  65.5 0.0 copy-start.24
  65.5 0.0 copy-start.15
  65.5 0.0 copy-start.18
  65.5 0.0 copy-done.1
  65.5 0.0 copy-done.3
  65.5 0.0 copy-done.5
  65.5 0.0 copy-done.9
  65.6 0.0 copy-done.10
  65.6 0.0 copy-done.12
  65.6 0.0 copy-done.7
  65.6 0.6 copy-done.16
  66.2 0.0 copy-done.17
  66.2 0.0 copy-done.19
  66.2 0.0 copy-done.20
  66.2 0.0 copy-done.24
  66.2 0.0 copy-done.15
  66.2 0.0 copy-done.18
  66.2 1.8 %shard_map.263 = (f32[256,128]{1,0:T(8,128)S(1)}, f32[2,128]{1,0:T(2,128)S(1)}, f32[64,128]{1,0:T(8,128)S(1)}, f32[64,128]{1,0:T(8,128)S(1)}, f32[256,128]{1,0:T...) custom-call(s32[1]{0:T(128)} %bitcast.8.region, ...), custom_call_target="tpu_custom_call" | custom-call | tf_op jit(solution)/shard_map/pallas_call | solution.py:392
  68.1 22.0 %all_to_all.20 = bf16[64,5,2,128]{3,2,1,0:T(2,128)(2,1)S(1)} all-to-all(bf16[64,5,2,128]{3,2,1,0:T(2,128)(2,1)S(1)} %bitcast.25), channel_id=1, replica_groups=mesh['region'=64,'season'=8] {'region'}, dimensions={0} | all-to-all | bytes 327680 | tf_op jit(solution)/shard_map/all_to_all | solution.py:419
  90.0 0.1 shard_map.264
  90.2 11.7 %all_to_all.21.got = f32[8,8,128]{2,1,0:T(8,128)S(1)} all-to-all(f32[8,8,128]{2,1,0:T(8,128)S(1)} %shard_map.264), channel_id=1, replica_groups=mesh['region'=64,'season'=8] {'season'}, dimensions={0} | all-to-all | bytes 65536 | tf_op jit(solution)/shard_map/all_to_all | solution.py:424
  101.9 1.9 %shard_map.265 = (f32[256,128]{1,0:T(8,128)}, f32[2,128]{1,0:T(2,128)}, f32[256,128]{1,0:T(8,128)}, f32[64,128]{1,0:T(8,128)}, f32[64,128]{1,0:T(8,128)}, /*inde...) custom-call(s32[1]{0:T(128)} %bitcast.season, bf16[256,128]{1,0:T(8,128)(2,1)S(1)} %copy-done.1, ...), custom_call_target="tpu_custom_call" | custom-call | tf_op jit(solution)/shard_map/pallas_call | solution.py:392
Async XLA Ops:
  0.6 0.7 copy-start.21
  0.6 0.7 copy-start.22
  0.7 0.7 copy-start.13
  0.7 0.7 copy-start.14
  1.4 0.8 copy-start
  2.2 0.9 copy-start.2
  3.1 0.8 copy-start.6
  3.9 0.8 copy-start.8
  4.6 22.1 %copy-start.11 = (f32[256,128]{1,0:T(8,128)S(1)}, f32[256,128]{1,0:T(8,128)}, u32[]{:S(2)}) copy-start(f32[256,128]{1,0:T(8,128)} %flow.1) | copy-start | bytes 393220
  5.6 21.1 %copy-start.4 = (f32[64,128]{1,0:T(8,128)S(1)}, f32[64,128]{1,0:T(8,128)}, u32[]{:S(2)}) copy-start(f32[64,128]{1,0:T(8,128)} %price.5) | copy-start | bytes 98308
  5.6 34.7 %all-to-all-start = ((f32[64,1,128]{2,1,0:T(1,128)}), f32[64,1,128]{2,1,0:T(1,128)S(1)}, u32[]{:S(2)}, u32[]{:S(2)}) async-start(f32[64,1,128]{2,1,0:T(1,128)} %bitcast.13), calls=%async_computation | async-start | bytes 65536 | tf_op jit(solution)/shard_map/all_to_all | solution.py:406
  26.7 0.7 copy-start.23
  41.7 23.8 %copy-start.1 = (bf16[256,128]{1,0:T(8,128)(2,1)S(1)}, bf16[256,128]{1,0:T(8,128)(2,1)}, u32[]{:S(2)}) copy-start(bf16[256,128]{1,0:T(8,128)(2,1)} %avail.5) | copy-start | bytes 196612
  41.7 23.8 %copy-start.3 = (f32[256,128]{1,0:T(8,128)S(1)}, f32[256,128]{1,0:T(8,128)}, u32[]{:S(2)}) copy-start(f32[256,128]{1,0:T(8,128)} %scarce.1) | copy-start | bytes 393220
  41.7 23.9 %copy-start.5 = (f32[256,128]{1,0:T(8,128)S(1)}, f32[256,128]{1,0:T(8,128)}, u32[]{:S(2)}) copy-start(f32[256,128]{1,0:T(8,128)} %disp.1) | copy-start | bytes 393220
  41.7 23.9 %copy-start.9 = (f32[64,128]{1,0:T(8,128)S(1)}, f32[64,128]{1,0:T(8,128)}, u32[]{:S(2)}) copy-start(f32[64,128]{1,0:T(8,128)} %sdual.1) | copy-start | bytes 98308
  41.7 23.9 %copy-start.10 = (f32[64,128]{1,0:T(8,128)S(1)}, f32[64,128]{1,0:T(8,128)}, u32[]{:S(2)}) copy-start(f32[64,128]{1,0:T(8,128)} %demand.3) | copy-start | bytes 98308
  41.7 23.9 %copy-start.12 = (f32[64,128]{1,0:T(8,128)S(1)}, f32[64,128]{1,0:T(8,128)}, u32[]{:S(2)}) copy-start(f32[64,128]{1,0:T(8,128)} %disch.1) | copy-start | bytes 98308
  41.7 23.8 %all-to-all-start.1 = ((bf16[64,7,2,128]{3,2,1,0:T(2,128)(2,1)}), bf16[64,7,2,128]{3,2,1,0:T(2,128)(2,1)S(1)}, u32[]{:S(2)}, u32[]{:S(2)}) async-start(bf16[64,7,2,128]{3,2,1,0:T(2,128)(2,1)} %bitcast.16), calls=%async_computation.1 | async-start | bytes 458752 | tf_op jit(solution)/shard_map/all_to_all | solution.py:419
  47.8 17.8 %copy-start.7 = (f32[64,128]{1,0:T(8,128)S(1)}, f32[64,128]{1,0:T(8,128)}, u32[]{:S(2)}) copy-start(f32[64,128]{1,0:T(8,128)} %level.1) | copy-start | bytes 98308
  65.5 0.7 copy-start.16
  65.5 0.7 copy-start.17
  65.5 0.7 copy-start.19
  65.5 0.7 copy-start.20
  65.5 0.7 copy-start.24
  65.5 0.7 copy-start.15
  65.5 0.7 copy-start.18

commit v8 on v6

--- a/solution.py
+++ b/solution.py
@@ -64,36 +64,6 @@
     return jnp.concatenate([ref[0:1, :], ref[1:2, :]], axis=1)
 
 
-def flip_bits(value):
-    flipped = value & 0
-    for bit in range(6):
-        flipped = flipped | (((value >> bit) & 1) << (5 - bit))
-    return flipped
-
-
-def region_at(place):
-    return flip_bits(place ^ (place >> 1))
-
-
-def place_of(region):
-    place = flip_bits(region)
-    for shift in (1, 2, 4):
-        place = place ^ (place >> shift)
-    return place
-
-
-def order_out():
-    shape = (SLOT, SLOT)
-    slot = iota((1, SLOT), 1)
-    return as_bf(iota(shape, 0) == LINK_CAP * place_of(slot >> 2) + (slot & 3))
-
-
-def order_in():
-    shape = (SLOT, SLOT)
-    at = iota((1, SLOT), 1)
-    return as_bf(iota(shape, 0) == LINK_CAP * region_at(at >> 2) + (at & 3))
-
-
 def pack_target(packed):
     q = (packed * (262144 // ROWS_EACH + 1)) >> 18
     j = packed - ROWS_EACH * q
@@ -104,9 +74,6 @@
 
 
 def pack(first, second, third, out_ref):
-    order = order_out()
-    first = narrow(dot(order, first))
-    second = narrow(dot(order, second))
     shape = (PACKED, UNPACKED)
     place = as_bf(pack_target(iota(shape, 0)) == iota(shape, 1))
     for g in range(REGIONS // GROUP):
@@ -125,13 +92,12 @@
     shape = (UNPACKED, PACKED)
     place = as_bf(pack_target(iota(shape, 1)) == iota(shape, 0))
     parts = [
-        narrow(dot(place, ref[g * PACKED : (g + 1) * PACKED, :])) for g in range(REGIONS // GROUP)
+        dot(place, ref[g * PACKED : (g + 1) * PACKED, :]) for g in range(REGIONS // GROUP)
     ]
-    order = order_in()
     first = jnp.concatenate([p[:LINES] for p in parts], axis=0)
     second = jnp.concatenate([p[LINES : 2 * LINES] for p in parts], axis=0)
     third = jnp.concatenate([p[2 * LINES :] for p in parts], axis=0)
-    return dot(order, first), dot(order, second), third
+    return first, second, third
 
 
 def columns(ref):
@@ -171,14 +137,11 @@
     leave[...] = leave_t
     high = wide(narrow(limit))
     low = limit - high
-    sending = as_bf(
-        iota((REGIONS, SLOT), 0) == place_of(iota((1, SLOT), 1) >> 2)
-    )
     held = jnp.zeros((REGIONS, 128), F32)
     slot_kind = iota((SLOT, 128), 0) & (LINK_CAP - 1)
     for at, value in enumerate((wide(row256(line_to)), high, low)):
         spots = as_bf(iota((SLOT, 128), 1) == slot_kind + LINK_CAP * at)
-        held = held + dot(sending * narrow(value), spots)
+        held = held + dot(spread * narrow(value), spots)
     pack(narrow(f0), near, narrow(held), sent)
 
 
@@ -194,29 +157,31 @@
     return jnp.transpose(held)[0:8]
 
 
-def season_out(avail, scarcity, soc, soc_dual, link, sent, turn):
+def season_out(season, avail, scarcity, soc, soc_dual, link, sent, turn):
     turn[0:1, 0:BUS] = wide(link[...])
     turned = columns(turn)
     sums = jnp.sum(wide(avail[...]) * wide(narrow(scarcity[...])), axis=1, keepdims=True)
     rows = season_block(sums, soc[...], wide(narrow(soc_dual[...])), turned[:BUS, 0:1])
-    for s in range(SEASONS):
-        sent[s] = rows
-
-
-def ends_in(got, price, sent, far, arrive, cap):
+    row = iota((8, 128), 0)
+    sent[0:8] = jnp.where(row < 2, rows, 0.0)
+    for half in range(2):
+        own = season[0] - 4 * half
+        halo = jnp.where((row & 1) == 0, rows[2:3], rows[3:4])
+        sent[8 + 8 * half : 16 + 8 * half] = jnp.where((row >> 1) == own, halo, 0.0)
+
+
+def ends_in(got, price, sent, arrive, cap):
     _, _, held = unpack(got)
     shape = (SLOT, REGIONS)
-    spread = as_bf(region_at(iota((1, REGIONS), 1)) == iota(shape, 0) >> 2)
-    lines = dot(spread, held)
+    spread = as_bf(iota(shape, 1) == iota(shape, 0) >> 2)
+    lines = dot(spread, narrow(held))
     lane = iota((SLOT, 128), 1)
     kind = iota((SLOT, 128), 0) & (LINK_CAP - 1)
     ends = jnp.sum(jnp.where(lane == kind, lines, 0.0), axis=1, keepdims=True)
     limits = (lane == kind + LINK_CAP) | (lane == kind + 2 * LINK_CAP)
     limit = jnp.sum(jnp.where(limits, lines, 0.0), axis=1, keepdims=True)
     arrive_t = onehot_rows(ends, BUS)
-    values = narrow(dot(arrive_t, narrow(price[...])))
-    far[...] = values
-    sent[...] = narrow(dot(order_out(), values))
+    sent[...] = narrow(dot(arrive_t, narrow(price[...])))
     arrive[...] = arrive_t
     cap[...] = jnp.broadcast_to(limit, (SLOT, HOUR))
 
@@ -226,18 +191,26 @@
     return moved, extrapolate(moved, flows)
 
 
-def local_step(season, consts, state, price_v, got, turn, tau, sigma):
+def halo_of(got, season):
+    rows = got[8:10]
+    for s in range(1, SEASONS):
+        rows = jnp.where(season == s, got[8 + 2 * s : 10 + 2 * s], rows)
+    return rows
+
+
+def tree(values):
+    while len(values) > 1:
+        values = [values[i] + values[i + 1] for i in range(0, len(values), 2)]
+    return values[0]
+
+
+def local_step(sums, before, after, consts, state, price_v, turn, tau, sigma):
     avail, asset_bus, run_cost, build_cost, efficiency, power, energy, link = consts
     disp, build, disch, level, scarce, sdual = state
-    before_at = (season + SEASONS - 1) & (SEASONS - 1)
-    after_at = (season + 1) & (SEASONS - 1)
-    sums = got[0, 0:2]
-    for s in range(1, SEASONS):
-        sums = sums + got[s, 0:2]
     grad_build = sums * (1.0 / (HOUR * SEASONS))
     build_new = jnp.maximum(build - tau * (build_cost[...] - grad_build), 0.0)
-    turn[0:8, :] = got[before_at]
-    turn[8:16, :] = got[after_at]
+    turn[2:4, :] = before
+    turn[10:12, :] = after
     turn[16:18, :] = wide(extrapolate(build_new, build))
     turn[18:20, :] = run_cost[...]
     turn[20:22, :] = wide(asset_bus[...])
@@ -303,8 +276,10 @@
     came0, near, _ = unpack(lines_got)
     moved, came_x = line_step(came0, near, wide(far[...]), cap[...], step_size)
     came1[...] = mean(moved, came0)
+    before = halo_of(got, (season[0] + SEASONS - 1) & (SEASONS - 1))
+    after = halo_of(got, (season[0] + 1) & (SEASONS - 1))
     local, halves, link_c = local_step(
-        season[0], consts, state, price[...], got, turn, step_size, step_size
+        got[0:2], before, after, consts, state, price[...], turn, step_size, step_size
     )
     balance[...] = local + dot_t(arrive[...], came_x)
     for ref, value in zip((disp1, build1, disch1, level1, scarce1, sdual1), halves):
@@ -328,8 +303,7 @@
 ):
     f0 = flow0[...]
     leave_t = leave[...]
-    far = dot(order_in(), got[...])
-    moved, flow_x = line_step(f0, wide(near0[...]), far, cap[...], step_size)
+    moved, flow_x = line_step(f0, wide(near0[...]), wide(got[...]), cap[...], step_size)
     f1 = mean(moved, f0)
     flow1[...] = f1
     p0 = price[...]
@@ -369,9 +343,7 @@
     came_far, came, demand, flow, cap, leave,
     disp2, build2, flow2, disch2, level2, price2, scarce2, sdual2, turn,
 ):
-    moves = got[0, 4:5]
-    for s in range(1, SEASONS):
-        moves = moves + got[s, 4:5]
+    moves = tree([got[s, 4:5] for s in range(SEASONS)])
     primal = moves[:, 0:1] + moves[:, 1:2] + moves[:, 2:3]
     dual = moves[:, 3:4] + moves[:, 4:5] + moves[:, 5:6]
     weight = jnp.sqrt(jnp.sqrt((dual + 1e-06) / (primal + 1e-06)))
@@ -387,7 +359,12 @@
     near = dot(leave_t, narrow(p1))
     moved, flow_x = line_step(f1, near, far, cap[...], tau)
     flow2[...] = mean(moved, f1)
-    local, halves, _ = local_step(season[0], consts, state, p1, got, turn, tau, sigma)
+    sums = tree([got[s, 0:2] for s in range(SEASONS)])
+    before = got[(season[0] + SEASONS - 1) & (SEASONS - 1), 2:4]
+    after = got[(season[0] + 1) & (SEASONS - 1), 2:4]
+    local, halves, _ = local_step(
+        sums, before, after, consts, state, p1, turn, tau, sigma
+    )
     whole = local + dot_t(arrive[...], came_x) - dot_t(leave_t, flow_x)
     price2[...] = mean(p1 + sigma * (demand[...] - whole), p1)
     for ref, value in zip((disp2, build2, disch2, level2, scarce2, sdual2), halves):
@@ -410,8 +387,7 @@
 
 def region_exchange(value, rows, per_pair):
     cut = value.reshape(REGIONS, per_pair, rows, HOUR)
-    members = [[region_at(place) for place in range(REGIONS)]]
-    got = lax.all_to_all(cut, "region", 0, 0, axis_index_groups=members, tiled=True)
+    got = lax.all_to_all(cut, "region", split_axis=0, concat_axis=0, tiled=True)
     return got.reshape(value.shape)
 
 
@@ -474,11 +450,21 @@
         turn=True,
     )
     got1 = region_exchange(sent1, 2, 5)
-    (rows1,) = call(season_out, [seasons], avail, scarcity, soc, soc_dual, link, turn=True)
-    season1 = season_exchange(rows1)
-    sent2, came_far0, arrive, came_cap = call(
-        ends_in, [lines_b, lines_b, picks, lines], got1, price
-    )
+    (rows1,) = call(
+        season_out,
+        [((24, 128), F32)],
+        season,
+        avail,
+        scarcity,
+        soc,
+        soc_dual,
+        link,
+        scalar=True,
+        turn=True,
+    )
+    season1 = lax.psum(rows1, "season")
+    got1, season1 = lax.optimization_barrier((got1, season1))
+    sent2, arrive, came_cap = call(ends_in, [lines_b, picks, lines], got1, price)
     got2 = region_exchange(sent2, LINK_CAP, 1)
     disp1, build1, disch1, level1, scarce1, sdual1, came1, balance, rows2, moves = call(
         first_local,
@@ -496,7 +482,7 @@
         got1,
         arrive,
         came_cap,
-        came_far0,
+        sent2,
         scalar=True,
         turn=True,
     )

time: 104 us -> 113 us (1.087)
  blocking collectives: 30.3 us -> 55.4 us
  waiting for transfers between devices: 28.2 us -> 10.7 us
  starting transfers between devices: 32.5 us -> 33.8 us
    psum x0 -> x1, blocking collectives: none -> 23.3 us  [on_device(): season1 = lax.psum(rows1, 'season')]
    all_to_all x3 -> x2, waiting for transfers between devices: 28.2 us -> 10.7 us  [region_exchange(): got = lax.all_to_all(cut, 'region', split_axis=0, concat_axis=0, tiled=True)]
    all_to_all x1, blocking collectives: 12.3 us -> 13.6 us  [season_exchange(): lax.all_to_all(value, 'season', split_axis=0, concat_axis=0, tiled=True)]
    all_to_all x3 -> x2, starting transfers between devices: 32.5 us -> 33.8 us  [region_exchange(): got = lax.all_to_all(cut, 'region', split_axis=0, concat_axis=0, tiled=True)]
  transfers between devices with their start and end apart: 3 -> 2, of which waited for: 3 -> 1; matrix products, arithmetic and copies ran while one was open for 0% -> 0% of each run, Pallas kernels for 3% -> 2%
where the time goes in v8:
time: 113 us; the launch traced here: 112 us
  blocking collectives  55.4 us (49%)
  starting transfers between devices  33.8 us (30%)
  waiting for transfers between devices  10.7 us (9%)
  Pallas kernels  7.53 us (7%)
  local copies, waits for them, and re-layouts  3.67 us (3%)
    all_to_all x2, starting transfers between devices, region_exchange(): got = lax.all_to_all(cut, 'region', split_axis=0, concat_axis=0, tiled=True)  33.8 us
    psum x1, blocking collectives, on_device(): season1 = lax.psum(rows1, 'season')  23.3 us
    all_to_all x1, blocking collectives, region_exchange(): got = lax.all_to_all(cut, 'region', split_axis=0, concat_axis=0, tiled=True)  18.5 us
    all_to_all x1, blocking collectives, season_exchange(): lax.all_to_all(value, 'season', split_axis=0, concat_axis=0, tiled=True)  13.6 us
    all_to_all x2, waiting for transfers between devices, region_exchange(): got = lax.all_to_all(cut, 'region', split_axis=0, concat_axis=0, tiled=True)  10.7 us
    pallas_call x7, Pallas kernels, call(): pl.pallas_call(body, out_shape=[jax.ShapeDtypeStruct(shape, kind) for sha...  7.53 us
    unnamed x44, local copies, waits for them, and re-layouts  3.67 us
  transfers between devices with their start and end apart: 2, of which 1 were waited for; matrix products, arithmetic and copies ran while one was open for 0% of the time, Pallas kernels for 2%

profile of v8, /device:TPU:1, one launch (start us, length us, event | category | flops | bytes accessed | tf_op | source)
XLA Modules:
  0.0 112.0 jit_solution(7485728814701990806)
XLA Ops:
  0.6 0.0 copy-start.18
  0.6 0.0 copy-start.19
  0.7 0.0 copy-start.17
  0.7 0.0 copy-start.21
  0.7 0.6 copy-done.18
  1.3 0.0 copy-done.19
  1.3 0.0 copy-done.17
  1.3 0.0 copy-done.21
  1.3 0.0 copy-start.2
  1.4 0.8 copy-done.2
  2.1 0.0 copy-start.8
  2.1 0.9 copy-done.8
  3.0 1.4 %shard_map.260 = (bf16[640,128]{1,0:T(8,128)(2,1)}, f32[256,128]{1,0:T(8,128)S(1)}, bf16[256,128]{1,0:T(8,128)(2,1)S(1)}, f32[256,128]{1,0:T(8,128)S(1)}, bf16[256,64]{1,0:T(8,128)(2,1)S(1)}) custom-call(f32[256,128]{1,0:T(8,128)S(1)} %copy-done.8, f32[64,128]{1,0:T(8,128)S(1)} %copy-done.2, s32[2,128]{1,0:T(2,128)S(1)} %bitcast.42, s32[2,128]{1,0:T(2,128)S(1)} %bitcast.43, ...), custom_call_target="tpu_custom_call" | custom-call | tf_op jit(solution)/shard_map/pallas_call | solution.py:378
  4.4 0.0 copy-start
  4.4 0.0 copy-start.1
  4.4 0.0 copy-start.5
  4.4 0.0 copy-start.6
  4.4 19.4 %all-to-all-start = ((bf16[64,5,2,128]{3,2,1,0:T(2,128)(2,1)}), bf16[64,5,2,128]{3,2,1,0:T(2,128)(2,1)S(1)}, u32[]{:S(2)}, u32[]{:S(2)}) async-start(bf16[64,5,2,128]{3,2,1,0:T(2,128)(2,1)} %bitcast.12), calls=%async_computation | async-start | bytes 327680 | tf_op jit(solution)/shard_map/all_to_all | solution.py:390
  23.8 0.0 copy-start.10
  23.9 0.0 copy-done
  23.9 0.0 copy-done.1
  23.9 0.0 copy-done.5
  23.9 0.0 copy-done.6
  23.9 0.6 copy-done.10
  24.5 0.0 copy-start.3
  24.5 0.2 shard_map.261
  24.8 23.3 %psum.7.got = f32[24,128]{1,0:T(8,128)S(1)} all-reduce(f32[24,128]{1,0:T(8,128)S(1)} %shard_map.261), channel_id=1, replica_groups=mesh['region'=64,'season'=8] {'season'}, use_global_device_ids=true, to_apply=%region_0.0 | all-reduce | flops 3072 | bytes 24576 | tf_op jit(solution)/shard_map/psum | solution.py:465
  48.1 0.0 all-to-all-done
  48.1 0.0 copy-done.3
  48.1 0.0 copy-start.4
  48.1 1.2 %shard_map.262 = (bf16[256,128]{1,0:T(8,128)(2,1)}, bf16[256,64]{1,0:T(8,128)(2,1)S(1)}, f32[256,128]{1,0:T(8,128)S(1)}) custom-call(bf16[640,128]{1,0:T(8,128)(2,1)S(1)} %bitcast.23, f32[64,128]{1,0:T(8,128)S(1)} %copy-done.3), custom_call_target="tpu_custom_call" | custom-call | tf_op jit(solution)/shard_map/pallas_call | solution.py:378
  49.3 0.0 copy-start.9
  49.3 14.4 %all-to-all-start.1 = ((bf16[64,1,4,128]{3,2,1,0:T(4,128)(2,1)}), bf16[64,1,4,128]{3,2,1,0:T(4,128)(2,1)S(1)}, u32[]{:S(2)}, u32[]{:S(2)}) async-start(bf16[64,1,4,128]{3,2,1,0:T(4,128)(2,1)} %bitcast.15), calls=%async_computation.1 | async-start | bytes 131072 | tf_op jit(solution)/shard_map/all_to_all | solution.py:390
  63.7 0.0 copy-start.12
  63.7 0.0 copy-start.13
  63.7 0.0 copy-start.15
  63.8 0.0 copy-start.16
  63.8 0.0 copy-start.20
  63.8 0.0 copy-start.11
  63.8 0.0 copy-start.14
  63.8 0.0 copy-done.4
  63.8 0.0 copy-done.9
  63.8 0.6 copy-done.12
  64.4 0.0 copy-done.13
  64.4 0.0 copy-done.15
  64.4 0.0 copy-done.16
  64.4 0.0 copy-done.20
  64.5 0.0 copy-done.11
  64.5 0.0 copy-done.14
  64.5 0.0 copy-start.7
  64.5 2.1 %shard_map.263 = (f32[256,128]{1,0:T(8,128)S(1)}, f32[2,128]{1,0:T(2,128)S(1)}, f32[64,128]{1,0:T(8,128)S(1)}, f32[64,128]{1,0:T(8,128)S(1)}, f32[256,128]{1,0:T...) custom-call(s32[1]{0:T(128)} %bitcast.season, ...), custom_call_target="tpu_custom_call" | custom-call | tf_op jit(solution)/shard_map/pallas_call | solution.py:378
  66.6 10.7 %all-to-all-done.1 = bf16[64,1,4,128]{3,2,1,0:T(4,128)(2,1)S(1)} async-done(((bf16[64,1,4,128]{3,2,1,0:T(4,128)(2,1)}), bf16[64,1,4,128]{3,2,1,0:T(4,128)(2,1)S(1)}, u32[]{:S(2)}, u32[]{:S(2)}) %all-to-all-start.1) | async-done | bytes 65568 | tf_op jit(solution)/shard_map/all_to_all | solution.py:390
  77.2 0.0 copy-done.7
  77.2 0.6 shard_map.264
  77.9 18.5 %all_to_all.20 = bf16[64,5,2,128]{3,2,1,0:T(2,128)(2,1)S(1)} all-to-all(bf16[64,5,2,128]{3,2,1,0:T(2,128)(2,1)S(1)} %bitcast.26), channel_id=1, replica_groups=mesh['region'=64,'season'=8] {'region'}, dimensions={0} | all-to-all | bytes 327680 | tf_op jit(solution)/shard_map/all_to_all | solution.py:390
  96.4 0.1 shard_map.265
  96.5 13.6 %all_to_all.21.got = f32[8,8,128]{2,1,0:T(8,128)S(1)} all-to-all(f32[8,8,128]{2,1,0:T(8,128)S(1)} %shard_map.265), channel_id=1, replica_groups=mesh['region'=64,'season'=8] {'season'}, dimensions={0} | all-to-all | bytes 65536 | tf_op jit(solution)/shard_map/all_to_all | solution.py:395
  110.1 1.8 %shard_map.266 = (f32[256,128]{1,0:T(8,128)}, f32[2,128]{1,0:T(2,128)}, f32[256,128]{1,0:T(8,128)}, f32[64,128]{1,0:T(8,128)}, f32[64,128]{1,0:T(8,128)}, /*inde...) custom-call(s32[1]{0:T(128)} %bitcast.season, bf16[256,128]{1,0:T(8,128)(2,1)S(1)} %copy-done, ...), custom_call_target="tpu_custom_call" | custom-call | tf_op jit(solution)/shard_map/pallas_call | solution.py:378
Async XLA Ops:
  0.6 0.7 copy-start.18
  0.6 0.7 copy-start.19
  0.7 0.7 copy-start.17
  0.7 0.7 copy-start.21
  1.3 0.8 copy-start.2
  2.1 0.9 copy-start.8
  4.4 19.5 %copy-start = (bf16[256,128]{1,0:T(8,128)(2,1)S(1)}, bf16[256,128]{1,0:T(8,128)(2,1)}, u32[]{:S(2)}) copy-start(bf16[256,128]{1,0:T(8,128)(2,1)} %avail.5) | copy-start | bytes 196612
  4.4 19.5 %copy-start.1 = (f32[256,128]{1,0:T(8,128)S(1)}, f32[256,128]{1,0:T(8,128)}, u32[]{:S(2)}) copy-start(f32[256,128]{1,0:T(8,128)} %scarce.1) | copy-start | bytes 393220
  4.4 19.5 %copy-start.5 = (f32[64,128]{1,0:T(8,128)S(1)}, f32[64,128]{1,0:T(8,128)}, u32[]{:S(2)}) copy-start(f32[64,128]{1,0:T(8,128)} %level.1) | copy-start | bytes 98308
  4.4 19.5 %copy-start.6 = (f32[64,128]{1,0:T(8,128)S(1)}, f32[64,128]{1,0:T(8,128)}, u32[]{:S(2)}) copy-start(f32[64,128]{1,0:T(8,128)} %sdual.1) | copy-start | bytes 98308
  4.4 43.7 %all-to-all-start = ((bf16[64,5,2,128]{3,2,1,0:T(2,128)(2,1)}), bf16[64,5,2,128]{3,2,1,0:T(2,128)(2,1)S(1)}, u32[]{:S(2)}, u32[]{:S(2)}) async-start(bf16[64,5,2,128]{3,2,1,0:T(2,128)(2,1)} %bitcast.12), calls=%async_computation | async-start | bytes 327680 | tf_op jit(solution)/shard_map/all_to_all | solution.py:390
  23.8 0.7 copy-start.10
  24.5 23.6 %copy-start.3 = (f32[64,128]{1,0:T(8,128)S(1)}, f32[64,128]{1,0:T(8,128)}, u32[]{:S(2)}) copy-start(f32[64,128]{1,0:T(8,128)} %price.7) | copy-start | bytes 98308
  48.1 15.7 %copy-start.4 = (f32[256,128]{1,0:T(8,128)S(1)}, f32[256,128]{1,0:T(8,128)}, u32[]{:S(2)}) copy-start(f32[256,128]{1,0:T(8,128)} %disp.1) | copy-start | bytes 393220
  49.3 14.5 %copy-start.9 = (f32[64,128]{1,0:T(8,128)S(1)}, f32[64,128]{1,0:T(8,128)}, u32[]{:S(2)}) copy-start(f32[64,128]{1,0:T(8,128)} %disch.1) | copy-start | bytes 98308
  49.3 27.9 %all-to-all-start.1 = ((bf16[64,1,4,128]{3,2,1,0:T(4,128)(2,1)}), bf16[64,1,4,128]{3,2,1,0:T(4,128)(2,1)S(1)}, u32[]{:S(2)}, u32[]{:S(2)}) async-start(bf16[64,1,4,128]{3,2,1,0:T(4,128)(2,1)} %bitcast.15), calls=%async_computation.1 | async-start | bytes 131072 | tf_op jit(solution)/shard_map/all_to_all | solution.py:390
  63.7 0.7 copy-start.12
  63.7 0.7 copy-start.13
  63.7 0.7 copy-start.15
  63.8 0.7 copy-start.16
  63.8 0.7 copy-start.20
  63.8 0.7 copy-start.11
  63.8 0.7 copy-start.14
  64.5 12.8 %copy-start.7 = (f32[64,128]{1,0:T(8,128)S(1)}, f32[64,128]{1,0:T(8,128)}, u32[]{:S(2)}) copy-start(f32[64,128]{1,0:T(8,128)} %demand.3) | copy-start | bytes 98308

commit v9 on v8

--- a/solution.py
+++ b/solution.py
@@ -157,17 +157,13 @@
     return jnp.transpose(held)[0:8]
 
 
-def season_out(season, avail, scarcity, soc, soc_dual, link, sent, turn):
+def season_out(avail, scarcity, soc, soc_dual, link, sent, halo, turn):
     turn[0:1, 0:BUS] = wide(link[...])
     turned = columns(turn)
     sums = jnp.sum(wide(avail[...]) * wide(narrow(scarcity[...])), axis=1, keepdims=True)
     rows = season_block(sums, soc[...], wide(narrow(soc_dual[...])), turned[:BUS, 0:1])
-    row = iota((8, 128), 0)
-    sent[0:8] = jnp.where(row < 2, rows, 0.0)
-    for half in range(2):
-        own = season[0] - 4 * half
-        halo = jnp.where((row & 1) == 0, rows[2:3], rows[3:4])
-        sent[8 + 8 * half : 16 + 8 * half] = jnp.where((row >> 1) == own, halo, 0.0)
+    sent[...] = rows[0:2]
+    halo[...] = rows[2:4]
 
 
 def ends_in(got, price, sent, arrive, cap):
@@ -189,13 +185,6 @@
 def line_step(flows, near, far, cap, tau):
     moved = jnp.clip(flows + tau * (far - near), -cap, cap)
     return moved, extrapolate(moved, flows)
-
-
-def halo_of(got, season):
-    rows = got[8:10]
-    for s in range(1, SEASONS):
-        rows = jnp.where(season == s, got[8 + 2 * s : 10 + 2 * s], rows)
-    return rows
 
 
 def tree(values):
@@ -267,8 +256,9 @@
 
 
 def first_local(
-    season, avail, asset_bus, run_cost, build_cost, efficiency, power, energy, link,
-    disp, build, disch, level, scarce, sdual, price, got, lines_got, arrive, cap, far,
+    avail, asset_bus, run_cost, build_cost, efficiency, power, energy, link,
+    disp, build, disch, level, scarce, sdual, price, sums, before, after,
+    lines_got, arrive, cap, far,
     disp1, build1, disch1, level1, scarce1, sdual1, came1, balance, rows, moves, turn,
 ):
     consts = (avail, asset_bus, run_cost, build_cost, efficiency, power, energy, link)
@@ -276,10 +266,8 @@
     came0, near, _ = unpack(lines_got)
     moved, came_x = line_step(came0, near, wide(far[...]), cap[...], step_size)
     came1[...] = mean(moved, came0)
-    before = halo_of(got, (season[0] + SEASONS - 1) & (SEASONS - 1))
-    after = halo_of(got, (season[0] + 1) & (SEASONS - 1))
     local, halves, link_c = local_step(
-        got[0:2], before, after, consts, state, price[...], turn, step_size, step_size
+        sums[...], before[...], after[...], consts, state, price[...], turn, step_size, step_size
     )
     balance[...] = local + dot_t(arrive[...], came_x)
     for ref, value in zip((disp1, build1, disch1, level1, scarce1, sdual1), halves):
@@ -389,6 +377,11 @@
     cut = value.reshape(REGIONS, per_pair, rows, HOUR)
     got = lax.all_to_all(cut, "region", split_axis=0, concat_axis=0, tiled=True)
     return got.reshape(value.shape)
+
+
+def season_pass(value, steps):
+    pairs = [(s, (s + steps) % SEASONS) for s in range(SEASONS)]
+    return lax.ppermute(value, "season", pairs)
 
 
 def season_exchange(value):
@@ -450,26 +443,25 @@
         turn=True,
     )
     got1 = region_exchange(sent1, 2, 5)
-    (rows1,) = call(
+    sums0, halo0 = call(
         season_out,
-        [((24, 128), F32)],
-        season,
+        [((2, 128), F32), ((2, 128), F32)],
         avail,
         scarcity,
         soc,
         soc_dual,
         link,
-        scalar=True,
         turn=True,
     )
-    season1 = lax.psum(rows1, "season")
-    got1, season1 = lax.optimization_barrier((got1, season1))
+    sums1 = lax.psum(sums0, "season")
+    before1 = season_pass(halo0, 1)
+    after1 = season_pass(halo0, SEASONS - 1)
+    got1, sums1 = lax.optimization_barrier((got1, sums1))
     sent2, arrive, came_cap = call(ends_in, [lines_b, picks, lines], got1, price)
     got2 = region_exchange(sent2, LINK_CAP, 1)
     disp1, build1, disch1, level1, scarce1, sdual1, came1, balance, rows2, moves = call(
         first_local,
         [lines, ((2, 128), F32), buses, buses, lines, buses, lines, buses, ((8, 128), F32), ((8, 128), F32)],
-        season,
         *consts,
         dispatch,
         pair(capacity),
@@ -478,12 +470,13 @@
         scarcity,
         soc_dual,
         price,
-        season1,
+        sums1,
+        before1,
+        after1,
         got1,
         arrive,
         came_cap,
         sent2,
-        scalar=True,
         turn=True,
     )
     price1, flow1, came_far1, sent3 = call(

time: 113 us -> 106 us (0.938)
  blocking collectives: 55.4 us -> 35.2 us
  starting transfers between devices: 33.8 us -> 43.6 us
  waiting for transfers between devices: 10.7 us -> 13.7 us
    all_to_all x1 -> x0, blocking collectives: 13.6 us -> none  [season_exchange(): lax.all_to_all(value, 'season', split_axis=0, concat_axis=0, tiled=True)]
    psum x1, blocking collectives: 23.3 us -> 13 us  [on_device(): sums1 = lax.psum(sums0, 'season')]
    all_to_all x0 -> x1, starting transfers between devices: none -> 7.76 us  [season_exchange(): lax.all_to_all(value, 'season', split_axis=0, concat_axis=0, tiled=True)]
    all_to_all x0 -> x1, waiting for transfers between devices: none -> 4.74 us  [season_exchange(): lax.all_to_all(value, 'season', split_axis=0, concat_axis=0, tiled=True)]
    all_to_all x1, blocking collectives: 18.5 us -> 22.2 us  [region_exchange(): got = lax.all_to_all(cut, 'region', split_axis=0, concat_axis=0, tiled=True)]
    ppermute x0 -> x2, starting transfers between devices: none -> 2.86 us  [season_pass(): return lax.ppermute(value, 'season', pairs)]
    all_to_all x2, waiting for transfers between devices: 10.7 us -> 7.86 us  [region_exchange(): got = lax.all_to_all(cut, 'region', split_axis=0, concat_axis=0, tiled=True)]
    ppermute x0 -> x2, waiting for transfers between devices: none -> 1.14 us  [season_pass(): return lax.ppermute(value, 'season', pairs)]
  transfers between devices with their start and end apart: 2 -> 5, of which waited for: 1 -> 5; matrix products, arithmetic and copies ran while one was open for 0% -> 0% of each run, Pallas kernels for 2% -> 2%
where the time goes in v9:
time: 106 us; the launch traced here: 105 us
  starting transfers between devices  43.6 us (41%)
  blocking collectives  35.2 us (33%)
  waiting for transfers between devices  13.7 us (13%)
  Pallas kernels  8.13 us (8%)
  local copies, waits for them, and re-layouts  3.69 us (3%)
    all_to_all x2, starting transfers between devices, region_exchange(): got = lax.all_to_all(cut, 'region', split_axis=0, concat_axis=0, tiled=True)  32.9 us
    all_to_all x1, blocking collectives, region_exchange(): got = lax.all_to_all(cut, 'region', split_axis=0, concat_axis=0, tiled=True)  22.2 us
    psum x1, blocking collectives, on_device(): sums1 = lax.psum(sums0, 'season')  13 us
    pallas_call x7, Pallas kernels, call(): pl.pallas_call(body, out_shape=[jax.ShapeDtypeStruct(shape, kind) for sha...  8.13 us
    all_to_all x2, waiting for transfers between devices, region_exchange(): got = lax.all_to_all(cut, 'region', split_axis=0, concat_axis=0, tiled=True)  7.86 us
    all_to_all x1, starting transfers between devices, season_exchange(): lax.all_to_all(value, 'season', split_axis=0, concat_axis=0, tiled=True)  7.76 us
    all_to_all x1, waiting for transfers between devices, season_exchange(): lax.all_to_all(value, 'season', split_axis=0, concat_axis=0, tiled=True)  4.74 us
    unnamed x44, local copies, waits for them, and re-layouts  3.69 us
  transfers between devices with their start and end apart: 5, of which 5 were waited for; matrix products, arithmetic and copies ran while one was open for 0% of the time, Pallas kernels for 2%

profile of v9, /device:TPU:1, one launch (start us, length us, event | category | flops | bytes accessed | tf_op | source)
XLA Modules:
  0.0 105.1 jit_solution(7347025035517021485)
XLA Ops:
  0.6 0.0 copy-start.18
  0.6 0.0 copy-start.19
  0.7 0.0 copy-start.17
  0.7 0.0 copy-start.21
  0.7 0.6 copy-done.18
  1.3 0.0 copy-done.19
  1.3 0.0 copy-done.17
  1.3 0.0 copy-done.21
  1.3 0.0 copy-start.1
  1.4 0.8 copy-done.1
  2.1 0.0 copy-start.5
  2.1 0.9 copy-done.5
  3.0 1.4 %shard_map.260 = (bf16[640,128]{1,0:T(8,128)(2,1)}, f32[256,128]{1,0:T(8,128)S(1)}, bf16[256,128]{1,0:T(8,128)(2,1)S(1)}, f32[256,128]{1,0:T(8,128)S(1)}, bf16[256,64]{1,0:T(8,128)(2,1)S(1)}) custom-call(f32[256,128]{1,0:T(8,128)S(1)} %copy-done.5, f32[64,128]{1,0:T(8,128)S(1)} %copy-done.1, s32[2,128]{1,0:T(2,128)S(1)} %bitcast.42, s32[2,128]{1,0:T(2,128)S(1)} %bitcast.43, ...), custom_call_target="tpu_custom_call" | custom-call | tf_op jit(solution)/shard_map/pallas_call | solution.py:366
  4.4 0.0 copy-start
  4.4 0.0 copy-start.3
  4.4 0.0 copy-start.7
  4.4 0.0 copy-start.8
  4.4 19.4 %all-to-all-start = ((bf16[64,5,2,128]{3,2,1,0:T(2,128)(2,1)}), bf16[64,5,2,128]{3,2,1,0:T(2,128)(2,1)S(1)}, u32[]{:S(2)}, u32[]{:S(2)}) async-start(bf16[64,5,2,128]{3,2,1,0:T(2,128)(2,1)} %bitcast.12), calls=%async_computation | async-start | bytes 327680 | tf_op jit(solution)/shard_map/all_to_all | solution.py:378
  23.8 0.0 copy-start.10
  23.8 0.0 copy-done
  23.9 0.0 copy-done.3
  23.9 0.0 copy-done.7
  23.9 0.0 copy-done.8
  23.9 0.6 copy-done.10
  24.5 0.0 copy-start.2
  24.5 0.2 shard_map.261
  24.7 13.0 %psum.7.sums = f32[2,128]{1,0:T(2,128)S(1)} all-reduce(f32[2,128]{1,0:T(2,128)S(1)} %get-tuple-element.43), channel_id=1, replica_groups=mesh['region'=64,'season'=8] {'season'}, use_global_device_ids=true, to_apply=%region_0.0 | all-reduce | flops 256 | bytes 2048 | tf_op jit(solution)/shard_map/psum | solution.py:456
  37.8 1.2 %all-to-all-done = bf16[64,5,2,128]{3,2,1,0:T(2,128)(2,1)S(1)} async-done(((bf16[64,5,2,128]{3,2,1,0:T(2,128)(2,1)}), bf16[64,5,2,128]{3,2,1,0:T(2,128)(2,1)S(1)}, u32[]{:S(2)}, u32[]{:S(2)}) %all-to-all-start) | async-done | bytes 163872 | tf_op jit(solution)/shard_map/all_to_all | solution.py:378
  38.9 0.0 copy-done.2
  38.9 0.0 copy-start.6
  38.9 1.2 %shard_map.262 = (bf16[256,128]{1,0:T(8,128)(2,1)}, bf16[256,64]{1,0:T(8,128)(2,1)S(1)}, f32[256,128]{1,0:T(8,128)S(1)}) custom-call(bf16[640,128]{1,0:T(8,128)(2,1)S(1)} %bitcast.23, f32[64,128]{1,0:T(8,128)S(1)} %copy-done.2), custom_call_target="tpu_custom_call" | custom-call | tf_op jit(solution)/shard_map/pallas_call | solution.py:366
  40.1 0.0 copy-start.9
  40.1 13.5 %all-to-all-start.1 = ((bf16[64,1,4,128]{3,2,1,0:T(4,128)(2,1)}), bf16[64,1,4,128]{3,2,1,0:T(4,128)(2,1)S(1)}, u32[]{:S(2)}, u32[]{:S(2)}) async-start(bf16[64,1,4,128]{3,2,1,0:T(4,128)(2,1)} %bitcast.15), calls=%async_computation.1 | async-start | bytes 131072 | tf_op jit(solution)/shard_map/all_to_all | solution.py:378
  53.7 2.9 %collective-permute-start.1 = (f32[2,128]{1,0:T(2,128)S(1)}, f32[2,128]{1,0:T(2,128)S(1)}, u32[]{:S(2)}, u32[]{:S(2)}) collective-permute-start(f32[2,128]{1,0:T(2,128)S(1)} %get-tuple-element.45), channel_id=1, source_target_pairs={{0,7},{1,0},{2,1},{3,2},{4,3},{5,4},{6,5},{7,6},{8,15},{9,8},{10,9... | collective-permute-start | bytes 3080 | tf_op jit(solution)/shard_map/ppermute | solution.py:384
  56.5 0.0 collective-permute-start
  56.5 0.8 collective-permute-done.1.after
  57.3 0.3 collective-permute-done.before
  57.7 0.0 copy-start.12
  57.7 0.0 copy-start.13
  57.7 0.0 copy-start.15
  57.7 0.0 copy-start.16
  57.7 0.0 copy-start.20
  57.7 0.0 copy-start.11
  57.7 0.0 copy-start.14
  57.7 0.0 copy-done.6
  57.7 0.0 copy-done.9
  57.7 0.6 copy-done.12
  58.3 0.0 copy-done.13
  58.4 0.0 copy-done.15
  58.4 0.0 copy-done.16
  58.4 0.0 copy-done.20
  58.4 0.0 copy-done.11
  58.4 0.0 copy-done.14
  58.4 0.0 copy-start.4
  58.4 2.1 %shard_map.263 = (f32[256,128]{1,0:T(8,128)S(1)}, f32[2,128]{1,0:T(2,128)S(1)}, f32[64,128]{1,0:T(8,128)S(1)}, f32[64,128]{1,0:T(8,128)S(1)}, f32[256,128]{1,0:T...) custom-call(bf16[256,128]{1,0:T(8,128)(2,1)S(1)} %copy-done, ...), custom_call_target="tpu_custom_call" | custom-call | tf_op jit(solution)/shard_map/pallas_call | solution.py:366
  60.5 6.7 %all-to-all-done.1 = bf16[64,1,4,128]{3,2,1,0:T(4,128)(2,1)S(1)} async-done(((bf16[64,1,4,128]{3,2,1,0:T(4,128)(2,1)}), bf16[64,1,4,128]{3,2,1,0:T(4,128)(2,1)S(1)}, u32[]{:S(2)}, u32[]{:S(2)}) %all-to-all-start.1) | async-done | bytes 65568 | tf_op jit(solution)/shard_map/all_to_all | solution.py:378
  67.2 0.0 copy-done.4
  67.2 0.6 shard_map.264
  67.8 22.2 %all_to_all.20 = bf16[64,5,2,128]{3,2,1,0:T(2,128)(2,1)S(1)} all-to-all(bf16[64,5,2,128]{3,2,1,0:T(2,128)(2,1)S(1)} %bitcast.26), channel_id=1, replica_groups=mesh['region'=64,'season'=8] {'region'}, dimensions={0} | all-to-all | bytes 327680 | tf_op jit(solution)/shard_map/all_to_all | solution.py:378
  90.0 0.8 shard_map.265
  90.7 7.8 %all-to-all-start.3 = ((f32[8,8,128]{2,1,0:T(8,128)}), f32[8,8,128]{2,1,0:T(8,128)S(1)}, u32[]{:S(2)}, u32[]{:S(2)}) async-start(f32[8,8,128]{2,1,0:T(8,128)} %shard_map.265), calls=%async_computation.3 | async-start | bytes 65536 | tf_op jit(solution)/shard_map/all_to_all | solution.py:388
  98.5 4.7 %all-to-all-done.3.got = f32[8,8,128]{2,1,0:T(8,128)S(1)} async-done(((f32[8,8,128]{2,1,0:T(8,128)}), f32[8,8,128]{2,1,0:T(8,128)S(1)}, u32[]{:S(2)}, u32[]{:S(2)}) %all-to-all-start.3) | async-done | bytes 32800 | tf_op jit(solution)/shard_map/all_to_all | solution.py:388
  103.2 1.8 %shard_map.266 = (f32[256,128]{1,0:T(8,128)}, f32[2,128]{1,0:T(2,128)}, f32[256,128]{1,0:T(8,128)}, f32[64,128]{1,0:T(8,128)}, f32[64,128]{1,0:T(8,128)}, /*inde...) custom-call(s32[1]{0:T(128)} %bitcast.season, bf16[256,128]{1,0:T(8,128)(2,1)S(1)} %copy-done, ...), custom_call_target="tpu_custom_call" | custom-call | tf_op jit(solution)/shard_map/pallas_call | solution.py:366
Async XLA Ops:
  0.6 0.7 copy-start.18
  0.6 0.7 copy-start.19
  0.7 0.7 copy-start.17
  0.7 0.7 copy-start.21
  1.3 0.8 copy-start.1
  2.1 0.9 copy-start.5
  4.4 19.5 %copy-start = (bf16[256,128]{1,0:T(8,128)(2,1)S(1)}, bf16[256,128]{1,0:T(8,128)(2,1)}, u32[]{:S(2)}) copy-start(bf16[256,128]{1,0:T(8,128)(2,1)} %avail.5) | copy-start | bytes 196612
  4.4 19.5 %copy-start.3 = (f32[256,128]{1,0:T(8,128)S(1)}, f32[256,128]{1,0:T(8,128)}, u32[]{:S(2)}) copy-start(f32[256,128]{1,0:T(8,128)} %scarce.1) | copy-start | bytes 393220
  4.4 19.5 %copy-start.7 = (f32[64,128]{1,0:T(8,128)S(1)}, f32[64,128]{1,0:T(8,128)}, u32[]{:S(2)}) copy-start(f32[64,128]{1,0:T(8,128)} %level.1) | copy-start | bytes 98308
  4.4 19.5 %copy-start.8 = (f32[64,128]{1,0:T(8,128)S(1)}, f32[64,128]{1,0:T(8,128)}, u32[]{:S(2)}) copy-start(f32[64,128]{1,0:T(8,128)} %sdual.1) | copy-start | bytes 98308
  4.4 34.5 %all-to-all-start = ((bf16[64,5,2,128]{3,2,1,0:T(2,128)(2,1)}), bf16[64,5,2,128]{3,2,1,0:T(2,128)(2,1)S(1)}, u32[]{:S(2)}, u32[]{:S(2)}) async-start(bf16[64,5,2,128]{3,2,1,0:T(2,128)(2,1)} %bitcast.12), calls=%async_computation | async-start | bytes 327680 | tf_op jit(solution)/shard_map/all_to_all | solution.py:378
  23.8 0.7 copy-start.10
  24.5 14.4 %copy-start.2 = (f32[64,128]{1,0:T(8,128)S(1)}, f32[64,128]{1,0:T(8,128)}, u32[]{:S(2)}) copy-start(f32[64,128]{1,0:T(8,128)} %price.7) | copy-start | bytes 98308
  38.9 18.8 %copy-start.6 = (f32[256,128]{1,0:T(8,128)S(1)}, f32[256,128]{1,0:T(8,128)}, u32[]{:S(2)}) copy-start(f32[256,128]{1,0:T(8,128)} %disp.1) | copy-start | bytes 393220
  40.1 17.6 %copy-start.9 = (f32[64,128]{1,0:T(8,128)S(1)}, f32[64,128]{1,0:T(8,128)}, u32[]{:S(2)}) copy-start(f32[64,128]{1,0:T(8,128)} %disch.1) | copy-start | bytes 98308
  40.1 27.0 %all-to-all-start.1 = ((bf16[64,1,4,128]{3,2,1,0:T(4,128)(2,1)}), bf16[64,1,4,128]{3,2,1,0:T(4,128)(2,1)S(1)}, u32[]{:S(2)}, u32[]{:S(2)}) async-start(bf16[64,1,4,128]{3,2,1,0:T(4,128)(2,1)} %bitcast.15), calls=%async_computation.1 | async-start | bytes 131072 | tf_op jit(solution)/shard_map/all_to_all | solution.py:378
  53.7 3.7 %collective-permute-start.1 = (f32[2,128]{1,0:T(2,128)S(1)}, f32[2,128]{1,0:T(2,128)S(1)}, u32[]{:S(2)}, u32[]{:S(2)}) collective-permute-start(f32[2,128]{1,0:T(2,128)S(1)} %get-tuple-element.45), channel_id=1, source_target_pairs={{0,7},{1,0},{2,1},{3,2},{4,3},{5,4},{6,5},{7,6},{8,15},{9,8},{10,9... | collective-permute-start | bytes 3080 | tf_op jit(solution)/shard_map/ppermute | solution.py:384
  56.5 1.1 %collective-permute-start = (f32[2,128]{1,0:T(2,128)S(1)}, f32[2,128]{1,0:T(2,128)S(1)}, u32[]{:S(2)}, u32[]{:S(2)}) collective-permute-start(f32[2,128]{1,0:T(2,128)S(1)} %get-tuple-element.45), channel_id=1, source_target_pairs={{0,1},{1,2},{2,3},{3,4},{4,5},{5,6},{6,7},{7,0},{8,9},{9,10},{10,1... | collective-permute-start | bytes 3080 | tf_op jit(solution)/shard_map/ppermute | solution.py:384
  57.7 0.7 copy-start.12
  57.7 0.7 copy-start.13
  57.7 0.7 copy-start.15
  57.7 0.7 copy-start.16
  57.7 0.7 copy-start.20
  57.7 0.7 copy-start.11
  57.7 0.7 copy-start.14
  58.4 8.8 %copy-start.4 = (f32[64,128]{1,0:T(8,128)S(1)}, f32[64,128]{1,0:T(8,128)}, u32[]{:S(2)}) copy-start(f32[64,128]{1,0:T(8,128)} %demand.3) | copy-start | bytes 98308
  90.7 12.5 %all-to-all-start.3 = ((f32[8,8,128]{2,1,0:T(8,128)}), f32[8,8,128]{2,1,0:T(8,128)S(1)}, u32[]{:S(2)}, u32[]{:S(2)}) async-start(f32[8,8,128]{2,1,0:T(8,128)} %shard_map.265), calls=%async_computation.3 | async-start | bytes 65536 | tf_op jit(solution)/shard_map/all_to_all | solution.py:388

commit v10 on v8

--- a/solution.py
+++ b/solution.py
@@ -100,6 +100,17 @@
     return first, second, third
 
 
+def fetch(sources, held, sems):
+    copies = [
+        pltpu.make_async_copy(source, target, sems.at[at])
+        for at, (source, target) in enumerate(zip(sources, held))
+    ]
+    for copy in copies:
+        copy.start()
+    for copy in copies:
+        copy.wait()
+
+
 def columns(ref):
     return jnp.transpose(ref[...])
 
@@ -112,10 +123,10 @@
     return as_bf(column == wide(iota((SLOT, count), 1)))
 
 
-def lines_out(
-    flow, price, line_from, line_to, line_limit, link_count,
-    sent, flow0, near0, cap, leave, turn,
-):
+def lines_out(*refs):
+    sent, flow0, near0, cap, leave, turn = refs[6:12]
+    flow, price, line_from, line_to, line_limit, link_count, sems = refs[12:]
+    fetch(refs[:6], refs[12:18], sems)
     lane = iota((1, SLOT), 1)
     spread = as_bf(iota((REGIONS, SLOT), 0) == lax.shift_right_logical(iota((REGIONS, SLOT), 1), 2))
     counts = jnp.broadcast_to(narrow(wide(link_count[...])), (8, REGIONS))
@@ -157,17 +168,15 @@
     return jnp.transpose(held)[0:8]
 
 
-def season_out(season, avail, scarcity, soc, soc_dual, link, sent, turn):
+def season_out(*refs):
+    sent, turn, avail, scarcity, soc, soc_dual, link, sems = refs[5:]
+    fetch(refs[:5], refs[7:12], sems)
     turn[0:1, 0:BUS] = wide(link[...])
     turned = columns(turn)
     sums = jnp.sum(wide(avail[...]) * wide(narrow(scarcity[...])), axis=1, keepdims=True)
     rows = season_block(sums, soc[...], wide(narrow(soc_dual[...])), turned[:BUS, 0:1])
-    row = iota((8, 128), 0)
-    sent[0:8] = jnp.where(row < 2, rows, 0.0)
-    for half in range(2):
-        own = season[0] - 4 * half
-        halo = jnp.where((row & 1) == 0, rows[2:3], rows[3:4])
-        sent[8 + 8 * half : 16 + 8 * half] = jnp.where((row >> 1) == own, halo, 0.0)
+    for s in range(SEASONS):
+        sent[s] = rows
 
 
 def ends_in(got, price, sent, arrive, cap):
@@ -191,17 +200,17 @@
     return moved, extrapolate(moved, flows)
 
 
-def halo_of(got, season):
-    rows = got[8:10]
-    for s in range(1, SEASONS):
-        rows = jnp.where(season == s, got[8 + 2 * s : 10 + 2 * s], rows)
-    return rows
-
-
 def tree(values):
     while len(values) > 1:
         values = [values[i] + values[i + 1] for i in range(0, len(values), 2)]
     return values[0]
+
+
+def season_parts(got, season):
+    sums = tree([got[s, 0:2] for s in range(SEASONS)])
+    before = got[(season + SEASONS - 1) & (SEASONS - 1), 2:4]
+    after = got[(season + 1) & (SEASONS - 1), 2:4]
+    return sums, before, after
 
 
 def local_step(sums, before, after, consts, state, price_v, turn, tau, sigma):
@@ -276,10 +285,9 @@
     came0, near, _ = unpack(lines_got)
     moved, came_x = line_step(came0, near, wide(far[...]), cap[...], step_size)
     came1[...] = mean(moved, came0)
-    before = halo_of(got, (season[0] + SEASONS - 1) & (SEASONS - 1))
-    after = halo_of(got, (season[0] + 1) & (SEASONS - 1))
+    sums, before, after = season_parts(got, season[0])
     local, halves, link_c = local_step(
-        got[0:2], before, after, consts, state, price[...], turn, step_size, step_size
+        sums, before, after, consts, state, price[...], turn, step_size, step_size
     )
     balance[...] = local + dot_t(arrive[...], came_x)
     for ref, value in zip((disp1, build1, disch1, level1, scarce1, sdual1), halves):
@@ -359,9 +367,7 @@
     near = dot(leave_t, narrow(p1))
     moved, flow_x = line_step(f1, near, far, cap[...], tau)
     flow2[...] = mean(moved, f1)
-    sums = tree([got[s, 0:2] for s in range(SEASONS)])
-    before = got[(season[0] + SEASONS - 1) & (SEASONS - 1), 2:4]
-    after = got[(season[0] + 1) & (SEASONS - 1), 2:4]
+    sums, before, after = season_parts(got, season[0])
     local, halves, _ = local_step(
         sums, before, after, consts, state, p1, turn, tau, sigma
     )
@@ -371,8 +377,14 @@
         ref[...] = value
 
 
-def call(body, outs, *operands, scalar=False, turn=False):
-    in_specs = [pl.BlockSpec(memory_space=pltpu.VMEM)] * len(operands)
+def call(body, outs, *operands, scalar=False, turn=False, fetched=False):
+    space = pltpu.HBM if fetched else pltpu.VMEM
+    in_specs = [pl.BlockSpec(memory_space=space)] * len(operands)
+    scratch = [pltpu.VMEM((128, 128), F32)] if turn else []
+    if fetched:
+        operands = [pltpu.with_memory_space_constraint(v, pltpu.HBM) for v in operands]
+        scratch += [pltpu.VMEM(v.shape, v.dtype) for v in operands]
+        scratch += [pltpu.SemaphoreType.DMA((len(operands),))]
     if scalar:
         in_specs[0] = pl.BlockSpec(memory_space=pltpu.SMEM)
     return pl.pallas_call(
@@ -380,7 +392,7 @@
         out_shape=[jax.ShapeDtypeStruct(shape, kind) for shape, kind in outs],
         in_specs=in_specs,
         out_specs=[pl.BlockSpec(memory_space=pltpu.VMEM)] * len(outs),
-        scratch_shapes=[pltpu.VMEM((128, 128), F32)] if turn else [],
+        scratch_shapes=scratch,
         compiler_params=pltpu.CompilerParams(vmem_limit_bytes=32 * 1024 * 1024),
     )(*operands)
 
@@ -448,22 +460,11 @@
         pair(line_limit),
         link_count,
         turn=True,
+        fetched=True,
     )
     got1 = region_exchange(sent1, 2, 5)
-    (rows1,) = call(
-        season_out,
-        [((24, 128), F32)],
-        season,
-        avail,
-        scarcity,
-        soc,
-        soc_dual,
-        link,
-        scalar=True,
-        turn=True,
-    )
-    season1 = lax.psum(rows1, "season")
-    got1, season1 = lax.optimization_barrier((got1, season1))
+    (rows1,) = call(season_out, [seasons], avail, scarcity, soc, soc_dual, link, turn=True, fetched=True)
+    season1 = season_exchange(rows1)
     sent2, arrive, came_cap = call(ends_in, [lines_b, picks, lines], got1, price)
     got2 = region_exchange(sent2, LINK_CAP, 1)
     disp1, build1, disch1, level1, scarce1, sdual1, came1, balance, rows2, moves = call(

time: 113 us -> 102 us (0.903)
  blocking collectives: 55.4 us -> 29.7 us
  waiting for transfers between devices: 10.7 us -> 27.4 us
  local copies, waits for them, and re-layouts: 3.67 us -> 0.7 us
  Pallas kernels: 7.53 us -> 10.1 us
    psum x1 -> x0, blocking collectives: 23.3 us -> none  [on_device(): season1 = lax.psum(rows1, 'season')]
    all_to_all x2, waiting for transfers between devices: 10.7 us -> 23.9 us  [region_exchange(): got = lax.all_to_all(cut, 'region', split_axis=0, concat_axis=0, tiled=True)]
    all_to_all x2, starting transfers between devices: 33.8 us -> 25.5 us  [region_exchange(): got = lax.all_to_all(cut, 'region', split_axis=0, concat_axis=0, tiled=True)]
    all_to_all x0 -> x1, starting transfers between devices: none -> 7.27 us  [season_exchange(): lax.all_to_all(value, 'season', split_axis=0, concat_axis=0, tiled=True)]
    all_to_all x0 -> x1, waiting for transfers between devices: none -> 3.5 us  [season_exchange(): lax.all_to_all(value, 'season', split_axis=0, concat_axis=0, tiled=True)]
    unnamed x44 -> x32, local copies, waits for them, and re-layouts: 3.67 us -> 0.7 us
    pallas_call x7, Pallas kernels: 7.53 us -> 10.1 us  [call(): pl.pallas_call(body, out_shape=[jax.ShapeDtypeStruct(shape, kind) for sha...]
    all_to_all x1, blocking collectives: 13.6 us -> 11.2 us  [season_exchange(): lax.all_to_all(value, 'season', split_axis=0, concat_axis=0, tiled=True)]
  transfers between devices with their start and end apart: 2 -> 3, of which waited for: 1 -> 3; matrix products, arithmetic and copies ran while one was open for 0% -> 0% of each run, Pallas kernels for 2% -> 5%
where the time goes in v10:
time: 102 us; the launch traced here: 101 us
  starting transfers between devices  32.7 us (32%)
  blocking collectives  29.7 us (29%)
  waiting for transfers between devices  27.4 us (27%)
  Pallas kernels  10.1 us (10%)
    all_to_all x2, starting transfers between devices, region_exchange(): got = lax.all_to_all(cut, 'region', split_axis=0, concat_axis=0, tiled=True)  25.5 us
    all_to_all x2, waiting for transfers between devices, region_exchange(): got = lax.all_to_all(cut, 'region', split_axis=0, concat_axis=0, tiled=True)  23.9 us
    all_to_all x1, blocking collectives, region_exchange(): got = lax.all_to_all(cut, 'region', split_axis=0, concat_axis=0, tiled=True)  18.5 us
    all_to_all x1, blocking collectives, season_exchange(): lax.all_to_all(value, 'season', split_axis=0, concat_axis=0, tiled=True)  11.2 us
    pallas_call x7, Pallas kernels, call(): pl.pallas_call(body, out_shape=[jax.ShapeDtypeStruct(shape, kind) for sha...  10.1 us
    all_to_all x1, starting transfers between devices, season_exchange(): lax.all_to_all(value, 'season', split_axis=0, concat_axis=0, tiled=True)  7.27 us
    all_to_all x1, waiting for transfers between devices, season_exchange(): lax.all_to_all(value, 'season', split_axis=0, concat_axis=0, tiled=True)  3.5 us
  transfers between devices with their start and end apart: 3, of which 3 were waited for; matrix products, arithmetic and copies ran while one was open for 0% of the time, Pallas kernels for 5%

profile of v10, /device:TPU:1, one launch (start us, length us, event | category | flops | bytes accessed | tf_op | source)
XLA Modules:
  0.0 101.5 jit_solution(7035320132487989745)
XLA Ops:
  0.6 2.4 %shard_map.261 = (bf16[640,128]{1,0:T(8,128)(2,1)}, f32[256,128]{1,0:T(8,128)S(1)}, bf16[256,128]{1,0:T(8,128)(2,1)S(1)}, f32[256,128]{1,0:T(8,128)S(1)}, bf16[256,64]{1,0:T(8,128)(2,1)S(1)}) custom-call(f32[256,128]{1,0:T(8,128)} %refs_0_.3, f32[64,128]{1,0:T(8,128)} %price.5, s32[2,128]{1,0:T(2,128)} %bitcast.43, s32[2,128]{1,0:T(2,128)} %bitcast.44, ...), custom_call_target="tpu_custom_call" | custom-call | tf_op jit(solution)/shard_map/pallas_call | solution.py:390
  3.0 19.3 %all-to-all-start.1 = ((bf16[64,5,2,128]{3,2,1,0:T(2,128)(2,1)}), bf16[64,5,2,128]{3,2,1,0:T(2,128)(2,1)S(1)}, u32[]{:S(2)}, u32[]{:S(2)}) async-start(bf16[64,5,2,128]{3,2,1,0:T(2,128)(2,1)} %bitcast.12), calls=%async_computation.1 | async-start | bytes 327680 | tf_op jit(solution)/shard_map/all_to_all | solution.py:402
  22.3 0.0 copy-start.5
  22.3 0.0 copy-start.7
  22.3 1.9 %shard_map.260 = f32[8,8,128]{2,1,0:T(8,128)} custom-call(bf16[256,128]{1,0:T(8,128)(2,1)} %avail.3, f32[256,128]{1,0:T(8,128)} %scarce.1, f32[64,128]{1,0:T(8,128)} %level.1, f32[64,128]{1,0:T(8,128)} %sdual.1, s32[1,64]{1,0:T(1,128)} %bitcast.27), custom_call_target="tpu_custom_call" | custom-call | tf_op jit(solution)/shard_map/pallas_call | solution.py:390
  24.2 0.0 copy-start.2
  24.2 13.2 %all-to-all-done.1 = bf16[64,5,2,128]{3,2,1,0:T(2,128)(2,1)S(1)} async-done(((bf16[64,5,2,128]{3,2,1,0:T(2,128)(2,1)}), bf16[64,5,2,128]{3,2,1,0:T(2,128)(2,1)S(1)}, u32[]{:S(2)}, u32[]{:S(2)}) %all-to-all-start.1) | async-done | bytes 163872 | tf_op jit(solution)/shard_map/all_to_all | solution.py:402
  37.4 0.0 copy-start.4
  37.4 7.3 %all-to-all-start = ((f32[8,8,128]{2,1,0:T(8,128)}), f32[8,8,128]{2,1,0:T(8,128)S(1)}, u32[]{:S(2)}, u32[]{:S(2)}) async-start(f32[8,8,128]{2,1,0:T(8,128)} %shard_map.260), calls=%async_computation | async-start | bytes 65536 | tf_op jit(solution)/shard_map/all_to_all | solution.py:407
  44.7 0.0 copy-done.2
  44.7 0.0 copy-start.1
  44.7 0.0 copy-start.3
  44.7 1.2 %shard_map.262 = (bf16[256,128]{1,0:T(8,128)(2,1)}, bf16[256,64]{1,0:T(8,128)(2,1)S(1)}, f32[256,128]{1,0:T(8,128)S(1)}) custom-call(bf16[640,128]{1,0:T(8,128)(2,1)S(1)} %bitcast.21, f32[64,128]{1,0:T(8,128)S(1)} %copy-done.2), custom_call_target="tpu_custom_call" | custom-call | tf_op jit(solution)/shard_map/pallas_call | solution.py:390
  45.9 3.5 %all-to-all-done.got = f32[8,8,128]{2,1,0:T(8,128)S(1)} async-done(((f32[8,8,128]{2,1,0:T(8,128)}), f32[8,8,128]{2,1,0:T(8,128)S(1)}, u32[]{:S(2)}, u32[]{:S(2)}) %all-to-all-start) | async-done | bytes 32800 | tf_op jit(solution)/shard_map/all_to_all | solution.py:407
  49.4 0.0 copy-start
  49.4 6.2 %all-to-all-start.2 = ((bf16[64,1,4,128]{3,2,1,0:T(4,128)(2,1)}), bf16[64,1,4,128]{3,2,1,0:T(4,128)(2,1)S(1)}, u32[]{:S(2)}, u32[]{:S(2)}) async-start(bf16[64,1,4,128]{3,2,1,0:T(4,128)(2,1)} %bitcast.15), calls=%async_computation.2 | async-start | bytes 131072 | tf_op jit(solution)/shard_map/all_to_all | solution.py:402
  55.6 0.0 copy-start.10
  55.6 0.0 copy-start.11
  55.6 0.0 copy-start.12
  55.6 0.0 copy-start.13
  55.6 0.0 copy-start.14
  55.6 0.0 copy-start.15
  55.6 0.0 copy-start.8
  55.7 0.0 copy-start.9
  55.7 0.0 copy-done.5
  55.7 0.0 copy-done.7
  55.7 0.0 copy-done.4
  55.7 0.0 copy-done.1
  55.7 0.0 copy-done.3
  55.7 0.0 copy-done
  55.7 0.5 copy-done.10
  56.3 0.0 copy-done.11
  56.3 0.0 copy-done.12
  56.3 0.0 copy-done.13
  56.3 0.0 copy-done.14
  56.3 0.0 copy-done.15
  56.3 0.0 copy-done.8
  56.3 0.0 copy-done.9
  56.4 0.0 copy-start.6
  56.4 2.0 %shard_map.263 = (f32[256,128]{1,0:T(8,128)S(1)}, f32[2,128]{1,0:T(2,128)S(1)}, f32[64,128]{1,0:T(8,128)S(1)}, f32[64,128]{1,0:T(8,128)S(1)}, f32[256,128]{1,0:T...) custom-call(s32[1]{0:T(128)} %bitcast.season, ...), custom_call_target="tpu_custom_call" | custom-call | tf_op jit(solution)/shard_map/pallas_call | solution.py:390
  58.4 10.7 %all-to-all-done.2 = bf16[64,1,4,128]{3,2,1,0:T(4,128)(2,1)S(1)} async-done(((bf16[64,1,4,128]{3,2,1,0:T(4,128)(2,1)}), bf16[64,1,4,128]{3,2,1,0:T(4,128)(2,1)S(1)}, u32[]{:S(2)}, u32[]{:S(2)}) %all-to-all-start.2) | async-done | bytes 65568 | tf_op jit(solution)/shard_map/all_to_all | solution.py:402
  69.1 0.0 copy-done.6
  69.1 0.6 shard_map.264
  69.7 18.5 %all_to_all.25 = bf16[64,5,2,128]{3,2,1,0:T(2,128)(2,1)S(1)} all-to-all(bf16[64,5,2,128]{3,2,1,0:T(2,128)(2,1)S(1)} %bitcast.26), channel_id=1, replica_groups=mesh['region'=64,'season'=8] {'region'}, dimensions={0} | all-to-all | bytes 327680 | tf_op jit(solution)/shard_map/all_to_all | solution.py:402
  88.3 0.1 shard_map.265
  88.4 11.2 %all_to_all.26.got = f32[8,8,128]{2,1,0:T(8,128)S(1)} all-to-all(f32[8,8,128]{2,1,0:T(8,128)S(1)} %shard_map.265), channel_id=1, replica_groups=mesh['region'=64,'season'=8] {'season'}, dimensions={0} | all-to-all | bytes 65536 | tf_op jit(solution)/shard_map/all_to_all | solution.py:407
  99.6 1.8 %shard_map.266 = (f32[256,128]{1,0:T(8,128)}, f32[2,128]{1,0:T(2,128)}, f32[256,128]{1,0:T(8,128)}, f32[64,128]{1,0:T(8,128)}, f32[64,128]{1,0:T(8,128)}, /*inde...) custom-call(s32[1]{0:T(128)} %bitcast.season, bf16[256,128]{1,0:T(8,128)(2,1)S(1)} %copy-done, ...), custom_call_target="tpu_custom_call" | custom-call | tf_op jit(solution)/shard_map/pallas_call | solution.py:390
Async XLA Ops:
  3.0 34.4 %all-to-all-start.1 = ((bf16[64,5,2,128]{3,2,1,0:T(2,128)(2,1)}), bf16[64,5,2,128]{3,2,1,0:T(2,128)(2,1)S(1)}, u32[]{:S(2)}, u32[]{:S(2)}) async-start(bf16[64,5,2,128]{3,2,1,0:T(2,128)(2,1)} %bitcast.12), calls=%async_computation.1 | async-start | bytes 327680 | tf_op jit(solution)/shard_map/all_to_all | solution.py:402
  22.3 33.4 %copy-start.5 = (f32[64,128]{1,0:T(8,128)S(1)}, f32[64,128]{1,0:T(8,128)}, u32[]{:S(2)}) copy-start(f32[64,128]{1,0:T(8,128)} %sdual.1) | copy-start | bytes 98308
  22.3 33.4 %copy-start.7 = (f32[64,128]{1,0:T(8,128)S(1)}, f32[64,128]{1,0:T(8,128)}, u32[]{:S(2)}) copy-start(f32[64,128]{1,0:T(8,128)} %disch.1) | copy-start | bytes 98308
  24.2 20.5 %copy-start.2 = (f32[64,128]{1,0:T(8,128)S(1)}, f32[64,128]{1,0:T(8,128)}, u32[]{:S(2)}) copy-start(f32[64,128]{1,0:T(8,128)} %price.5) | copy-start | bytes 98308
  37.4 18.3 %copy-start.4 = (f32[64,128]{1,0:T(8,128)S(1)}, f32[64,128]{1,0:T(8,128)}, u32[]{:S(2)}) copy-start(f32[64,128]{1,0:T(8,128)} %level.1) | copy-start | bytes 98308
  37.4 12.0 %all-to-all-start = ((f32[8,8,128]{2,1,0:T(8,128)}), f32[8,8,128]{2,1,0:T(8,128)S(1)}, u32[]{:S(2)}, u32[]{:S(2)}) async-start(f32[8,8,128]{2,1,0:T(8,128)} %shard_map.260), calls=%async_computation | async-start | bytes 65536 | tf_op jit(solution)/shard_map/all_to_all | solution.py:407
  44.7 11.0 %copy-start.1 = (f32[256,128]{1,0:T(8,128)S(1)}, f32[256,128]{1,0:T(8,128)}, u32[]{:S(2)}) copy-start(f32[256,128]{1,0:T(8,128)} %scarce.1) | copy-start | bytes 393220
  44.7 11.0 %copy-start.3 = (f32[256,128]{1,0:T(8,128)S(1)}, f32[256,128]{1,0:T(8,128)}, u32[]{:S(2)}) copy-start(f32[256,128]{1,0:T(8,128)} %disp.1) | copy-start | bytes 393220
  49.4 6.3 %copy-start = (bf16[256,128]{1,0:T(8,128)(2,1)S(1)}, bf16[256,128]{1,0:T(8,128)(2,1)}, u32[]{:S(2)}) copy-start(bf16[256,128]{1,0:T(8,128)(2,1)} %avail.3) | copy-start | bytes 196612
  49.4 19.7 %all-to-all-start.2 = ((bf16[64,1,4,128]{3,2,1,0:T(4,128)(2,1)}), bf16[64,1,4,128]{3,2,1,0:T(4,128)(2,1)S(1)}, u32[]{:S(2)}, u32[]{:S(2)}) async-start(bf16[64,1,4,128]{3,2,1,0:T(4,128)(2,1)} %bitcast.15), calls=%async_computation.2 | async-start | bytes 131072 | tf_op jit(solution)/shard_map/all_to_all | solution.py:402
  55.6 0.7 copy-start.10
  55.6 0.7 copy-start.11
  55.6 0.7 copy-start.12
  55.6 0.7 copy-start.13
  55.6 0.7 copy-start.14
  55.6 0.7 copy-start.15
  55.6 0.7 copy-start.8
  55.7 0.7 copy-start.9
  56.4 12.7 %copy-start.6 = (f32[64,128]{1,0:T(8,128)S(1)}, f32[64,128]{1,0:T(8,128)}, u32[]{:S(2)}) copy-start(f32[64,128]{1,0:T(8,128)} %demand.3) | copy-start | bytes 98308

commit v11 on v10

--- a/solution.py
+++ b/solution.py
@@ -100,15 +100,19 @@
     return first, second, third
 
 
-def fetch(sources, held, sems):
+def start_copies(sources, held, sems):
     copies = [
         pltpu.make_async_copy(source, target, sems.at[at])
         for at, (source, target) in enumerate(zip(sources, held))
     ]
     for copy in copies:
         copy.start()
-    for copy in copies:
-        copy.wait()
+    return [copy.wait for copy in copies]
+
+
+def fetch(sources, held, sems):
+    for wait in start_copies(sources, held, sems):
+        wait()
 
 
 def columns(ref):
@@ -126,7 +130,9 @@
 def lines_out(*refs):
     sent, flow0, near0, cap, leave, turn = refs[6:12]
     flow, price, line_from, line_to, line_limit, link_count, sems = refs[12:]
-    fetch(refs[:6], refs[12:18], sems)
+    waits = start_copies(refs[:6], refs[12:18], sems)
+    for wait in waits[2:]:
+        wait()
     lane = iota((1, SLOT), 1)
     spread = as_bf(iota((REGIONS, SLOT), 0) == lax.shift_right_logical(iota((REGIONS, SLOT), 1), 2))
     counts = jnp.broadcast_to(narrow(wide(link_count[...])), (8, REGIONS))
@@ -140,10 +146,6 @@
     turn[5:6, :] = limit[:, 128:]
     turned = columns(turn)
     leave_t = onehot_rows(long_column(turned, 0), BUS)
-    f0 = flow[...] * long_column(turned, 2)
-    near = narrow(dot(leave_t, narrow(price[...])))
-    flow0[...] = f0
-    near0[...] = near
     cap[...] = jnp.broadcast_to(long_column(turned, 4), (SLOT, HOUR))
     leave[...] = leave_t
     high = wide(narrow(limit))
@@ -153,6 +155,12 @@
     for at, value in enumerate((wide(row256(line_to)), high, low)):
         spots = as_bf(iota((SLOT, 128), 1) == slot_kind + LINK_CAP * at)
         held = held + dot(spread * narrow(value), spots)
+    waits[1]()
+    near = narrow(dot(leave_t, narrow(price[...])))
+    near0[...] = near
+    waits[0]()
+    f0 = flow[...] * long_column(turned, 2)
+    flow0[...] = f0
     pack(narrow(f0), near, narrow(held), sent)
 
 
@@ -275,23 +283,37 @@
     return balance, halves, link_c
 
 
-def first_local(
+def first_step(
     season, avail, asset_bus, run_cost, build_cost, efficiency, power, energy, link,
-    disp, build, disch, level, scarce, sdual, price, got, lines_got, arrive, cap, far,
-    disp1, build1, disch1, level1, scarce1, sdual1, came1, balance, rows, moves, turn,
+    disp, build, disch, level, scarce, sdual, price, seasons_got, lines_got, arrive, came_cap,
+    came_far, got, demand, flow0, near0, cap, leave,
+    disp1, build1, disch1, level1, scarce1, sdual1, price1, flow1, came1, far1, rows, sent, turn,
 ):
+    f0 = flow0[...]
+    p0 = price[...]
+    leave_t = leave[...]
+    arrive_t = arrive[...]
+    came0, came_near, _ = unpack(lines_got)
+    came_moved, came_x = line_step(came0, came_near, wide(came_far[...]), came_cap[...], step_size)
+    came1[...] = mean(came_moved, came0)
+    moved, flow_x = line_step(f0, wide(near0[...]), wide(got[...]), cap[...], step_size)
+    f1 = mean(moved, f0)
+    flow1[...] = f1
     consts = (avail, asset_bus, run_cost, build_cost, efficiency, power, energy, link)
     state = (disp[...], build[...], disch[...], level[...], scarce[...], sdual[...])
-    came0, near, _ = unpack(lines_got)
-    moved, came_x = line_step(came0, near, wide(far[...]), cap[...], step_size)
-    came1[...] = mean(moved, came0)
-    sums, before, after = season_parts(got, season[0])
+    sums, before, after = season_parts(seasons_got, season[0])
     local, halves, link_c = local_step(
-        sums, before, after, consts, state, price[...], turn, step_size, step_size
-    )
-    balance[...] = local + dot_t(arrive[...], came_x)
+        sums, before, after, consts, state, p0, turn, step_size, step_size
+    )
     for ref, value in zip((disp1, build1, disch1, level1, scarce1, sdual1), halves):
         ref[...] = value
+    whole = local + dot_t(arrive_t, came_x) - dot_t(leave_t, flow_x)
+    p1 = mean(p0 + step_size * (demand[...] - whole), p0)
+    price1[...] = p1
+    price_b = narrow(p1)
+    near = narrow(dot(leave_t, price_b))
+    far = narrow(dot(arrive_t, price_b))
+    far1[...] = far
     sums = jnp.sum(wide(avail[...]) * wide(narrow(halves[4])), axis=1, keepdims=True)
     rows[...] = season_block(sums, halves[3], wide(narrow(halves[5])), link_c)
     primal = (
@@ -299,27 +321,9 @@
         + square(halves[1], state[1]) * (1.0 / SEASONS)
         + square(halves[2], state[2])
         + square(halves[3], state[3])
-    )
-    dual = square(halves[4], state[4]) + square(halves[5], state[5])
-    lane = iota((8, 128), 1)
-    moves[...] = jnp.where(lane == 0, primal, dual)
-
-
-def price_step(
-    flow0, near0, cap, leave, arrive, got, demand, price, balance, moves,
-    price1, flow1, far0, sent,
-):
-    f0 = flow0[...]
-    leave_t = leave[...]
-    moved, flow_x = line_step(f0, wide(near0[...]), wide(got[...]), cap[...], step_size)
-    f1 = mean(moved, f0)
-    flow1[...] = f1
-    p0 = price[...]
-    whole = balance[...] - dot_t(leave_t, flow_x)
-    p1 = mean(p0 + step_size * (demand[...] - whole), p0)
-    price1[...] = p1
-    primal = moves[0:1, 0:1] + square(f1, f0)
-    dual = moves[0:1, 1:2] + square(p1, p0)
+        + square(f1, f0)
+    )
+    dual = square(halves[4], state[4]) + square(halves[5], state[5]) + square(p1, p0)
     lane = iota((GROUP, 128), 1)
     held = jnp.zeros((GROUP, 128), F32)
     for at, value in ((0, primal), (3, dual)):
@@ -328,10 +332,6 @@
             held = jnp.where(lane == at + step, piece, held)
             value = value - piece
     held = narrow(held)
-    price_b = narrow(p1)
-    near = narrow(dot(leave_t, price_b))
-    far = narrow(dot(arrive[...], price_b))
-    far0[...] = far
     pack(near, far, jnp.concatenate([held] * (REGIONS // GROUP), axis=0), sent)
 
 
@@ -467,9 +467,35 @@
     season1 = season_exchange(rows1)
     sent2, arrive, came_cap = call(ends_in, [lines_b, picks, lines], got1, price)
     got2 = region_exchange(sent2, LINK_CAP, 1)
-    disp1, build1, disch1, level1, scarce1, sdual1, came1, balance, rows2, moves = call(
-        first_local,
-        [lines, ((2, 128), F32), buses, buses, lines, buses, lines, buses, ((8, 128), F32), ((8, 128), F32)],
+    (
+        disp1,
+        build1,
+        disch1,
+        level1,
+        scarce1,
+        sdual1,
+        price1,
+        flow1,
+        came1,
+        came_far1,
+        rows2,
+        sent3,
+    ) = call(
+        first_step,
+        [
+            lines,
+            ((2, 128), F32),
+            buses,
+            buses,
+            lines,
+            buses,
+            buses,
+            lines,
+            lines,
+            lines_b,
+            ((8, 128), F32),
+            packed,
+        ],
         season,
         *consts,
         dispatch,
@@ -484,22 +510,14 @@
         arrive,
         came_cap,
         sent2,
-        scalar=True,
-        turn=True,
-    )
-    price1, flow1, came_far1, sent3 = call(
-        price_step,
-        [buses, lines, lines_b, packed],
+        got2,
+        demand,
         flow0,
         near0,
         cap,
         leave,
-        arrive,
-        got2,
-        demand,
-        price,
-        balance,
-        moves,
+        scalar=True,
+        turn=True,
     )
     got3 = region_exchange(sent3, 2, 5)
     (rows3,) = call(moves_out, [seasons], got3, rows2)

time: 102 us -> 104 us (1.020)
  waiting for transfers between devices: 27.4 us -> 30.2 us
    all_to_all x2, waiting for transfers between devices: 23.9 us -> 26.7 us  [region_exchange(): got = lax.all_to_all(cut, 'region', split_axis=0, concat_axis=0, tiled=True)]
    pallas_call x7 -> x6, Pallas kernels: 10.1 us -> 9.58 us  [call(): pl.pallas_call(body, out_shape=[jax.ShapeDtypeStruct(shape, kind) for sha...]
  transfers between devices with their start and end apart: 3 -> 3, of which waited for: 3 -> 3; matrix products, arithmetic and copies ran while one was open for 0% -> 0% of each run, Pallas kernels for 5% -> 3%
where the time goes in v11:
time: 104 us
  starting transfers between devices  32.7 us (31%)
  waiting for transfers between devices  30.2 us (29%)
  blocking collectives  29.7 us (29%)
  Pallas kernels  9.58 us (9%)
    all_to_all x2, waiting for transfers between devices, region_exchange(): got = lax.all_to_all(cut, 'region', split_axis=0, concat_axis=0, tiled=True)  26.7 us
    all_to_all x2, starting transfers between devices, region_exchange(): got = lax.all_to_all(cut, 'region', split_axis=0, concat_axis=0, tiled=True)  25.5 us
    all_to_all x1, blocking collectives, region_exchange(): got = lax.all_to_all(cut, 'region', split_axis=0, concat_axis=0, tiled=True)  18.5 us
    all_to_all x1, blocking collectives, season_exchange(): lax.all_to_all(value, 'season', split_axis=0, concat_axis=0, tiled=True)  11.2 us
    pallas_call x6, Pallas kernels, call(): pl.pallas_call(body, out_shape=[jax.ShapeDtypeStruct(shape, kind) for sha...  9.58 us
    all_to_all x1, starting transfers between devices, season_exchange(): lax.all_to_all(value, 'season', split_axis=0, concat_axis=0, tiled=True)  7.27 us
    all_to_all x1, waiting for transfers between devices, season_exchange(): lax.all_to_all(value, 'season', split_axis=0, concat_axis=0, tiled=True)  3.5 us
  transfers between devices with their start and end apart: 3, of which 3 were waited for; matrix products, arithmetic and copies ran while one was open for 0% of the time, Pallas kernels for 3%

profile of v11, /device:TPU:1, one launch (start us, length us, event | category | flops | bytes accessed | tf_op | source)
XLA Modules:
  0.0 103.7 jit_solution(18145401840709632004)
XLA Ops:
  0.6 2.4 %shard_map.261 = (bf16[640,128]{1,0:T(8,128)(2,1)}, f32[256,128]{1,0:T(8,128)S(1)}, bf16[256,128]{1,0:T(8,128)(2,1)S(1)}, f32[256,128]{1,0:T(8,128)S(1)}, bf16[256,64]{1,0:T(8,128)(2,1)S(1)}) custom-call(f32[256,128]{1,0:T(8,128)} %refs_0_.3, f32[64,128]{1,0:T(8,128)} %price.3, s32[2,128]{1,0:T(2,128)} %bitcast.43, s32[2,128]{1,0:T(2,128)} %bitcast.44, ...), custom_call_target="tpu_custom_call" | custom-call | tf_op jit(solution)/shard_map/pallas_call | solution.py:390
  3.0 19.3 %all-to-all-start.1 = ((bf16[64,5,2,128]{3,2,1,0:T(2,128)(2,1)}), bf16[64,5,2,128]{3,2,1,0:T(2,128)(2,1)S(1)}, u32[]{:S(2)}, u32[]{:S(2)}) async-start(bf16[64,5,2,128]{3,2,1,0:T(2,128)(2,1)} %bitcast.12), calls=%async_computation.1 | async-start | bytes 327680 | tf_op jit(solution)/shard_map/all_to_all | solution.py:402
  22.3 0.0 copy-start.6
  22.4 0.0 copy-start.7
  22.4 1.9 %shard_map.260 = f32[8,8,128]{2,1,0:T(8,128)} custom-call(bf16[256,128]{1,0:T(8,128)(2,1)} %avail.3, f32[256,128]{1,0:T(8,128)} %scarce.1, f32[64,128]{1,0:T(8,128)} %level.1, f32[64,128]{1,0:T(8,128)} %sdual.1, s32[1,64]{1,0:T(1,128)} %bitcast.27), custom_call_target="tpu_custom_call" | custom-call | tf_op jit(solution)/shard_map/pallas_call | solution.py:390
  24.2 0.0 copy-start.2
  24.3 13.2 %all-to-all-done.1 = bf16[64,5,2,128]{3,2,1,0:T(2,128)(2,1)S(1)} async-done(((bf16[64,5,2,128]{3,2,1,0:T(2,128)(2,1)}), bf16[64,5,2,128]{3,2,1,0:T(2,128)(2,1)S(1)}, u32[]{:S(2)}, u32[]{:S(2)}) %all-to-all-start.1) | async-done | bytes 163872 | tf_op jit(solution)/shard_map/all_to_all | solution.py:402
  37.4 0.0 copy-start.5
  37.4 0.0 copy-start.15
  37.4 7.3 %all-to-all-start = ((f32[8,8,128]{2,1,0:T(8,128)}), f32[8,8,128]{2,1,0:T(8,128)S(1)}, u32[]{:S(2)}, u32[]{:S(2)}) async-start(f32[8,8,128]{2,1,0:T(8,128)} %shard_map.260), calls=%async_computation | async-start | bytes 65536 | tf_op jit(solution)/shard_map/all_to_all | solution.py:407
  44.7 0.0 copy-done.2
  44.7 0.0 copy-start.1
  44.7 0.0 copy-start.3
  44.7 1.2 %shard_map.262 = (bf16[256,128]{1,0:T(8,128)(2,1)}, bf16[256,64]{1,0:T(8,128)(2,1)S(1)}, f32[256,128]{1,0:T(8,128)S(1)}) custom-call(bf16[640,128]{1,0:T(8,128)(2,1)S(1)} %bitcast.21, f32[64,128]{1,0:T(8,128)S(1)} %copy-done.2), custom_call_target="tpu_custom_call" | custom-call | tf_op jit(solution)/shard_map/pallas_call | solution.py:390
  45.9 3.5 %all-to-all-done.seasons_got = f32[8,8,128]{2,1,0:T(8,128)S(1)} async-done(((f32[8,8,128]{2,1,0:T(8,128)}), f32[8,8,128]{2,1,0:T(8,128)S(1)}, u32[]{:S(2)}, u32[]{:S(2)}) %all-to-all-start) | async-done | bytes 32800 | tf_op jit(solution)/shard_map/all_to_all | solution.py:407
  49.4 0.0 copy-start
  49.4 0.0 copy-start.10
  49.4 0.0 copy-start.11
  49.4 0.0 copy-start.13
  49.4 0.0 copy-start.14
  49.5 6.2 %all-to-all-start.2 = ((bf16[64,1,4,128]{3,2,1,0:T(4,128)(2,1)}), bf16[64,1,4,128]{3,2,1,0:T(4,128)(2,1)S(1)}, u32[]{:S(2)}, u32[]{:S(2)}) async-start(bf16[64,1,4,128]{3,2,1,0:T(4,128)(2,1)} %bitcast.15), calls=%async_computation.2 | async-start | bytes 131072 | tf_op jit(solution)/shard_map/all_to_all | solution.py:402
  55.6 0.0 copy-start.4
  55.7 13.5 %all-to-all-done.2 = bf16[64,1,4,128]{3,2,1,0:T(4,128)(2,1)S(1)} async-done(((bf16[64,1,4,128]{3,2,1,0:T(4,128)(2,1)}), bf16[64,1,4,128]{3,2,1,0:T(4,128)(2,1)S(1)}, u32[]{:S(2)}, u32[]{:S(2)}) %all-to-all-start.2) | async-done | bytes 65568 | tf_op jit(solution)/shard_map/all_to_all | solution.py:402
  69.2 0.0 copy-start.12
  69.2 0.0 copy-start.8
  69.2 0.0 copy-start.9
  69.2 0.0 copy-done.6
  69.2 0.0 copy-done.7
  69.2 0.0 copy-done.5
  69.2 0.0 copy-done.15
  69.2 0.0 copy-done.1
  69.2 0.0 copy-done.3
  69.2 0.0 copy-done
  69.2 0.0 copy-done.10
  69.3 0.0 copy-done.11
  69.3 0.0 copy-done.13
  69.3 0.0 copy-done.14
  69.3 0.0 copy-done.4
  69.3 0.5 copy-done.12
  69.8 0.0 copy-done.8
  69.8 0.0 copy-done.9
  69.9 2.1 %shard_map.263 = (f32[256,128]{1,0:T(8,128)S(1)}, f32[2,128]{1,0:T(2,128)S(1)}, f32[64,128]{1,0:T(8,128)S(1)}, f32[64,128]{1,0:T(8,128)S(1)}, f32[256,128]{1,0:T...) custom-call(s32[1]{0:T(128)} %bitcast.season, ...), custom_call_target="tpu_custom_call" | custom-call | tf_op jit(solution)/shard_map/pallas_call | solution.py:390
  72.0 18.5 %all_to_all.25 = bf16[64,5,2,128]{3,2,1,0:T(2,128)(2,1)S(1)} all-to-all(bf16[64,5,2,128]{3,2,1,0:T(2,128)(2,1)S(1)} %bitcast.26), channel_id=1, replica_groups=mesh['region'=64,'season'=8] {'region'}, dimensions={0} | all-to-all | bytes 327680 | tf_op jit(solution)/shard_map/all_to_all | solution.py:402
  90.5 0.1 shard_map.264
  90.7 11.2 %all_to_all.26.got = f32[8,8,128]{2,1,0:T(8,128)S(1)} all-to-all(f32[8,8,128]{2,1,0:T(8,128)S(1)} %shard_map.264), channel_id=1, replica_groups=mesh['region'=64,'season'=8] {'season'}, dimensions={0} | all-to-all | bytes 65536 | tf_op jit(solution)/shard_map/all_to_all | solution.py:407
  101.9 1.9 %shard_map.265 = (f32[256,128]{1,0:T(8,128)}, f32[2,128]{1,0:T(2,128)}, f32[256,128]{1,0:T(8,128)}, f32[64,128]{1,0:T(8,128)}, f32[64,128]{1,0:T(8,128)}, /*inde...) custom-call(s32[1]{0:T(128)} %bitcast.season, bf16[256,128]{1,0:T(8,128)(2,1)S(1)} %copy-done, ...), custom_call_target="tpu_custom_call" | custom-call | tf_op jit(solution)/shard_map/pallas_call | solution.py:390
Async XLA Ops:
  3.0 34.4 %all-to-all-start.1 = ((bf16[64,5,2,128]{3,2,1,0:T(2,128)(2,1)}), bf16[64,5,2,128]{3,2,1,0:T(2,128)(2,1)S(1)}, u32[]{:S(2)}, u32[]{:S(2)}) async-start(bf16[64,5,2,128]{3,2,1,0:T(2,128)(2,1)} %bitcast.12), calls=%async_computation.1 | async-start | bytes 327680 | tf_op jit(solution)/shard_map/all_to_all | solution.py:402
  22.3 46.8 %copy-start.6 = (f32[64,128]{1,0:T(8,128)S(1)}, f32[64,128]{1,0:T(8,128)}, u32[]{:S(2)}) copy-start(f32[64,128]{1,0:T(8,128)} %demand.3) | copy-start | bytes 98308
  22.4 46.8 %copy-start.7 = (f32[64,128]{1,0:T(8,128)S(1)}, f32[64,128]{1,0:T(8,128)}, u32[]{:S(2)}) copy-start(f32[64,128]{1,0:T(8,128)} %disch.1) | copy-start | bytes 98308
  24.2 20.5 %copy-start.2 = (f32[64,128]{1,0:T(8,128)S(1)}, f32[64,128]{1,0:T(8,128)}, u32[]{:S(2)}) copy-start(f32[64,128]{1,0:T(8,128)} %price.3) | copy-start | bytes 98308
  37.4 31.8 %copy-start.5 = (f32[64,128]{1,0:T(8,128)S(1)}, f32[64,128]{1,0:T(8,128)}, u32[]{:S(2)}) copy-start(f32[64,128]{1,0:T(8,128)} %sdual.1) | copy-start | bytes 98308
  37.4 31.8 %copy-start.15 = (f32[256]{0:T(256)S(1)}, f32[256]{0:T(256)}, u32[]{:S(2)}) copy-start(f32[256]{0:T(256)} %param.35) | copy-start | bytes 3076
  37.4 12.0 %all-to-all-start = ((f32[8,8,128]{2,1,0:T(8,128)}), f32[8,8,128]{2,1,0:T(8,128)S(1)}, u32[]{:S(2)}, u32[]{:S(2)}) async-start(f32[8,8,128]{2,1,0:T(8,128)} %shard_map.260), calls=%async_computation | async-start | bytes 65536 | tf_op jit(solution)/shard_map/all_to_all | solution.py:407
  44.7 24.5 %copy-start.1 = (f32[256,128]{1,0:T(8,128)S(1)}, f32[256,128]{1,0:T(8,128)}, u32[]{:S(2)}) copy-start(f32[256,128]{1,0:T(8,128)} %scarce.1) | copy-start | bytes 393220
  44.7 24.5 %copy-start.3 = (f32[256,128]{1,0:T(8,128)S(1)}, f32[256,128]{1,0:T(8,128)}, u32[]{:S(2)}) copy-start(f32[256,128]{1,0:T(8,128)} %disp.1) | copy-start | bytes 393220
  49.4 19.8 %copy-start = (bf16[256,128]{1,0:T(8,128)(2,1)S(1)}, bf16[256,128]{1,0:T(8,128)(2,1)}, u32[]{:S(2)}) copy-start(bf16[256,128]{1,0:T(8,128)(2,1)} %avail.3) | copy-start | bytes 196612
  49.4 19.8 %copy-start.10 = (f32[256]{0:T(256)S(1)}, f32[256]{0:T(256)}, u32[]{:S(2)}) copy-start(f32[256]{0:T(256)} %param.24) | copy-start | bytes 3076
  49.4 19.8 %copy-start.11 = (f32[256]{0:T(256)S(1)}, f32[256]{0:T(256)}, u32[]{:S(2)}) copy-start(f32[256]{0:T(256)} %param.25) | copy-start | bytes 3076
  49.4 19.8 %copy-start.13 = (f32[64]{0:T(128)S(1)}, f32[64]{0:T(128)}, u32[]{:S(2)}) copy-start(f32[64]{0:T(128)} %param.31) | copy-start | bytes 772
  49.4 19.8 %copy-start.14 = (f32[64]{0:T(128)S(1)}, f32[64]{0:T(128)}, u32[]{:S(2)}) copy-start(f32[64]{0:T(128)} %param.32) | copy-start | bytes 772
  49.5 19.7 %all-to-all-start.2 = ((bf16[64,1,4,128]{3,2,1,0:T(4,128)(2,1)}), bf16[64,1,4,128]{3,2,1,0:T(4,128)(2,1)S(1)}, u32[]{:S(2)}, u32[]{:S(2)}) async-start(bf16[64,1,4,128]{3,2,1,0:T(4,128)(2,1)} %bitcast.15), calls=%async_computation.2 | async-start | bytes 131072 | tf_op jit(solution)/shard_map/all_to_all | solution.py:402
  55.6 13.6 %copy-start.4 = (f32[64,128]{1,0:T(8,128)S(1)}, f32[64,128]{1,0:T(8,128)}, u32[]{:S(2)}) copy-start(f32[64,128]{1,0:T(8,128)} %level.1) | copy-start | bytes 98308
  69.2 0.7 copy-start.12
  69.2 0.7 copy-start.8
  69.2 0.7 copy-start.9

commit v12 on v10

--- a/solution.py
+++ b/solution.py
@@ -73,7 +73,7 @@
     return jnp.where(j < LINK_CAP, first, jnp.where(j < 2 * LINK_CAP, second, third))
 
 
-def pack(first, second, third, out_ref):
+def pack(first, second, third, out_ref, packed_group=None):
     shape = (PACKED, UNPACKED)
     place = as_bf(pack_target(iota(shape, 0)) == iota(shape, 1))
     for g in range(REGIONS // GROUP):
@@ -86,6 +86,8 @@
             axis=0,
         )
         out_ref[g * PACKED : (g + 1) * PACKED, :] = narrow(dot(place, rows))
+        if packed_group is not None:
+            packed_group(g)
 
 
 def unpack(ref):
@@ -125,7 +127,7 @@
 
 def lines_out(*refs):
     sent, flow0, near0, cap, leave, turn = refs[6:12]
-    flow, price, line_from, line_to, line_limit, link_count, sems = refs[12:]
+    flow, price, line_from, line_to, line_limit, link_count, sems, held_out, out_sems = refs[12:]
     fetch(refs[:6], refs[12:18], sems)
     lane = iota((1, SLOT), 1)
     spread = as_bf(iota((REGIONS, SLOT), 0) == lax.shift_right_logical(iota((REGIONS, SLOT), 1), 2))
@@ -153,7 +155,17 @@
     for at, value in enumerate((wide(row256(line_to)), high, low)):
         spots = as_bf(iota((SLOT, 128), 1) == slot_kind + LINK_CAP * at)
         held = held + dot(spread * narrow(value), spots)
-    pack(narrow(f0), near, narrow(held), sent)
+    copies = []
+
+    def send(g):
+        rows = pl.ds(g * PACKED, PACKED)
+        copy = pltpu.make_async_copy(held_out.at[rows], sent.at[rows], out_sems.at[g])
+        copy.start()
+        copies.append(copy)
+
+    pack(narrow(f0), near, narrow(held), held_out, send)
+    for copy in copies:
+        copy.wait()
 
 
 def season_block(sums, level, dual_f, link_column):
@@ -179,7 +191,7 @@
         sent[s] = rows
 
 
-def ends_in(got, price, sent, arrive, cap):
+def ends_in(got, price, sent, far, arrive, cap):
     _, _, held = unpack(got)
     shape = (SLOT, REGIONS)
     spread = as_bf(iota(shape, 1) == iota(shape, 0) >> 2)
@@ -190,7 +202,9 @@
     limits = (lane == kind + LINK_CAP) | (lane == kind + 2 * LINK_CAP)
     limit = jnp.sum(jnp.where(limits, lines, 0.0), axis=1, keepdims=True)
     arrive_t = onehot_rows(ends, BUS)
-    sent[...] = narrow(dot(arrive_t, narrow(price[...])))
+    values = narrow(dot(arrive_t, narrow(price[...])))
+    sent[...] = values
+    far[...] = values
     arrive[...] = arrive_t
     cap[...] = jnp.broadcast_to(limit, (SLOT, HOUR))
 
@@ -349,8 +363,17 @@
     season, avail, asset_bus, run_cost, build_cost, efficiency, power, energy, link,
     disp, build, disch, level, scarce, sdual, price, got, lines_got, arrive, came_cap,
     came_far, came, demand, flow, cap, leave,
-    disp2, build2, flow2, disch2, level2, price2, scarce2, sdual2, turn,
+    *refs,
 ):
+    outs, turn, held, sems = refs[:8], refs[8], refs[9:17], refs[17]
+    copies = []
+
+    def give(at, value):
+        held[at][...] = value
+        copy = pltpu.make_async_copy(held[at], outs[at], sems.at[at])
+        copy.start()
+        copies.append(copy)
+
     moves = tree([got[s, 4:5] for s in range(SEASONS)])
     primal = moves[:, 0:1] + moves[:, 1:2] + moves[:, 2:3]
     dual = moves[:, 3:4] + moves[:, 4:5] + moves[:, 5:6]
@@ -366,32 +389,39 @@
     leave_t = leave[...]
     near = dot(leave_t, narrow(p1))
     moved, flow_x = line_step(f1, near, far, cap[...], tau)
-    flow2[...] = mean(moved, f1)
+    give(2, mean(moved, f1))
     sums, before, after = season_parts(got, season[0])
     local, halves, _ = local_step(
         sums, before, after, consts, state, p1, turn, tau, sigma
     )
     whole = local + dot_t(arrive[...], came_x) - dot_t(leave_t, flow_x)
-    price2[...] = mean(p1 + sigma * (demand[...] - whole), p1)
-    for ref, value in zip((disp2, build2, disch2, level2, scarce2, sdual2), halves):
-        ref[...] = value
-
-
-def call(body, outs, *operands, scalar=False, turn=False, fetched=False):
+    for at, value in zip((0, 1, 3, 4, 6, 7), halves):
+        give(at, value)
+    give(5, mean(p1 + sigma * (demand[...] - whole), p1))
+    for copy in copies:
+        copy.wait()
+
+
+def call(body, outs, *operands, scalar=False, turn=False, fetched=False, streamed=0):
     space = pltpu.HBM if fetched else pltpu.VMEM
     in_specs = [pl.BlockSpec(memory_space=space)] * len(operands)
+    out_specs = [pl.BlockSpec(memory_space=pltpu.HBM)] * streamed
+    out_specs += [pl.BlockSpec(memory_space=pltpu.VMEM)] * (len(outs) - streamed)
     scratch = [pltpu.VMEM((128, 128), F32)] if turn else []
     if fetched:
         operands = [pltpu.with_memory_space_constraint(v, pltpu.HBM) for v in operands]
         scratch += [pltpu.VMEM(v.shape, v.dtype) for v in operands]
         scratch += [pltpu.SemaphoreType.DMA((len(operands),))]
+    if streamed:
+        scratch += [pltpu.VMEM(shape, kind) for shape, kind in outs[:streamed]]
+        scratch += [pltpu.SemaphoreType.DMA((8,))]
     if scalar:
         in_specs[0] = pl.BlockSpec(memory_space=pltpu.SMEM)
     return pl.pallas_call(
         body,
         out_shape=[jax.ShapeDtypeStruct(shape, kind) for shape, kind in outs],
         in_specs=in_specs,
-        out_specs=[pl.BlockSpec(memory_space=pltpu.VMEM)] * len(outs),
+        out_specs=out_specs,
         scratch_shapes=scratch,
         compiler_params=pltpu.CompilerParams(vmem_limit_bytes=32 * 1024 * 1024),
     )(*operands)
@@ -461,11 +491,14 @@
         link_count,
         turn=True,
         fetched=True,
+        streamed=1,
     )
     got1 = region_exchange(sent1, 2, 5)
     (rows1,) = call(season_out, [seasons], avail, scarcity, soc, soc_dual, link, turn=True, fetched=True)
     season1 = season_exchange(rows1)
-    sent2, arrive, came_cap = call(ends_in, [lines_b, picks, lines], got1, price)
+    sent2, came_far0, arrive, came_cap = call(
+        ends_in, [lines_b, lines_b, picks, lines], got1, price
+    )
     got2 = region_exchange(sent2, LINK_CAP, 1)
     disp1, build1, disch1, level1, scarce1, sdual1, came1, balance, rows2, moves = call(
         first_local,
@@ -483,7 +516,7 @@
         got1,
         arrive,
         came_cap,
-        sent2,
+        came_far0,
         scalar=True,
         turn=True,
     )
@@ -528,6 +561,7 @@
         leave,
         scalar=True,
         turn=True,
+        streamed=8,
     )
     return (disp2, build2.reshape(capacity.shape), flow2, disch2, level2, price2, scarce2, sdual2)
 

time: 102 us -> 102 us (level)
  waiting for transfers between devices: 27.4 us -> 28.7 us
    all_to_all x2, waiting for transfers between devices: 23.9 us -> 25.3 us  [region_exchange(): got = lax.all_to_all(cut, 'region', split_axis=0, concat_axis=0, tiled=True)]
  transfers between devices with their start and end apart: 3 -> 3, of which waited for: 3 -> 3; matrix products, arithmetic and copies ran while one was open for 0% -> 0% of each run, Pallas kernels for 5% -> 4%
where the time goes in v12:
time: 102 us
  starting transfers between devices  32.7 us (32%)
  blocking collectives  29.8 us (29%)
  waiting for transfers between devices  28.7 us (28%)
  Pallas kernels  9.36 us (9%)
    all_to_all x2, starting transfers between devices, region_exchange(): got = lax.all_to_all(cut, 'region', split_axis=0, concat_axis=0, tiled=True)  25.5 us
    all_to_all x2, waiting for transfers between devices, region_exchange(): got = lax.all_to_all(cut, 'region', split_axis=0, concat_axis=0, tiled=True)  25.3 us
    all_to_all x1, blocking collectives, region_exchange(): got = lax.all_to_all(cut, 'region', split_axis=0, concat_axis=0, tiled=True)  18.5 us
    all_to_all x1, blocking collectives, season_exchange(): lax.all_to_all(value, 'season', split_axis=0, concat_axis=0, tiled=True)  11.2 us
    pallas_call x7, Pallas kernels, call(): pl.pallas_call(body, out_shape=[jax.ShapeDtypeStruct(shape, kind) for sha...  9.36 us
    all_to_all x1, starting transfers between devices, season_exchange(): lax.all_to_all(value, 'season', split_axis=0, concat_axis=0, tiled=True)  7.27 us
    all_to_all x1, waiting for transfers between devices, season_exchange(): lax.all_to_all(value, 'season', split_axis=0, concat_axis=0, tiled=True)  3.48 us
  transfers between devices with their start and end apart: 3, of which 3 were waited for; matrix products, arithmetic and copies ran while one was open for 0% of the time, Pallas kernels for 4%

profile of v12, /device:TPU:1, one launch (start us, length us, event | category | flops | bytes accessed | tf_op | source)
XLA Modules:
  0.0 101.6 jit_solution(6488855583502568228)
XLA Ops:
  0.6 2.4 %shard_map.261 = (bf16[640,128]{1,0:T(8,128)(2,1)}, f32[256,128]{1,0:T(8,128)S(1)}, bf16[256,128]{1,0:T(8,128)(2,1)S(1)}, f32[256,128]{1,0:T(8,128)S(1)}, bf16[256,64]{1,0:T(8,128)(2,1)S(1)}) custom-call(f32[256,128]{1,0:T(8,128)} %refs_0_.3, f32[64,128]{1,0:T(8,128)} %price.5, s32[2,128]{1,0:T(2,128)} %bitcast.43, s32[2,128]{1,0:T(2,128)} %bitcast.44, ...), custom_call_target="tpu_custom_call" | custom-call | tf_op jit(solution)/shard_map/pallas_call | solution.py:420
  3.0 19.3 %all-to-all-start.1 = ((bf16[64,5,2,128]{3,2,1,0:T(2,128)(2,1)}), bf16[64,5,2,128]{3,2,1,0:T(2,128)(2,1)S(1)}, u32[]{:S(2)}, u32[]{:S(2)}) async-start(bf16[64,5,2,128]{3,2,1,0:T(2,128)(2,1)} %bitcast.12), calls=%async_computation.1 | async-start | bytes 327680 | tf_op jit(solution)/shard_map/all_to_all | solution.py:432
  22.3 0.0 copy-start.7
  22.3 0.0 copy-start.8
  22.4 0.0 copy-start.9
  22.4 0.0 copy-start.10
  22.4 0.0 copy-start.11
  22.4 0.0 copy-start.12
  22.4 0.0 copy-start.13
  22.4 0.0 copy-start.14
  22.4 0.0 copy-start.15
  22.4 1.9 %shard_map.260 = f32[8,8,128]{2,1,0:T(8,128)} custom-call(bf16[256,128]{1,0:T(8,128)(2,1)} %avail.3, f32[256,128]{1,0:T(8,128)} %scarce.1, f32[64,128]{1,0:T(8,128)} %level.1, f32[64,128]{1,0:T(8,128)} %sdual.1, s32[1,64]{1,0:T(1,128)} %bitcast.27), custom_call_target="tpu_custom_call" | custom-call | tf_op jit(solution)/shard_map/pallas_call | solution.py:420
  24.3 0.0 copy-start.2
  24.3 13.1 %all-to-all-done.1 = bf16[64,5,2,128]{3,2,1,0:T(2,128)(2,1)S(1)} async-done(((bf16[64,5,2,128]{3,2,1,0:T(2,128)(2,1)}), bf16[64,5,2,128]{3,2,1,0:T(2,128)(2,1)S(1)}, u32[]{:S(2)}, u32[]{:S(2)}) %all-to-all-start.1) | async-done | bytes 163872 | tf_op jit(solution)/shard_map/all_to_all | solution.py:432
  37.4 0.0 copy-start.5
  37.4 7.3 %all-to-all-start = ((f32[8,8,128]{2,1,0:T(8,128)}), f32[8,8,128]{2,1,0:T(8,128)S(1)}, u32[]{:S(2)}, u32[]{:S(2)}) async-start(f32[8,8,128]{2,1,0:T(8,128)} %shard_map.260), calls=%async_computation | async-start | bytes 65536 | tf_op jit(solution)/shard_map/all_to_all | solution.py:437
  44.7 0.0 copy-start.4
  44.7 0.0 copy-done.2
  44.7 0.0 copy-start.1
  44.7 0.0 copy-start.3
  44.7 1.2 %shard_map.262 = (bf16[256,128]{1,0:T(8,128)(2,1)}, bf16[256,128]{1,0:T(8,128)(2,1)S(1)}, bf16[256,64]{1,0:T(8,128)(2,1)S(1)}, f32[256,128]{1,0:T(8,128)S(1)}) custom-call(bf16[640,128]{1,0:T(8,128)(2,1)S(1)} %bitcast.21, f32[64,128]{1,0:T(8,128)S(1)} %copy-done.2), custom_call_target="tpu_custom_call" | custom-call | tf_op jit(solution)/shard_map/pallas_call | solution.py:420
  45.9 3.5 %all-to-all-done.got = f32[8,8,128]{2,1,0:T(8,128)S(1)} async-done(((f32[8,8,128]{2,1,0:T(8,128)}), f32[8,8,128]{2,1,0:T(8,128)S(1)}, u32[]{:S(2)}, u32[]{:S(2)}) %all-to-all-start) | async-done | bytes 32800 | tf_op jit(solution)/shard_map/all_to_all | solution.py:437
  49.4 0.0 copy-start
  49.4 6.2 %all-to-all-start.2 = ((bf16[64,1,4,128]{3,2,1,0:T(4,128)(2,1)}), bf16[64,1,4,128]{3,2,1,0:T(4,128)(2,1)S(1)}, u32[]{:S(2)}, u32[]{:S(2)}) async-start(bf16[64,1,4,128]{3,2,1,0:T(4,128)(2,1)} %bitcast.15), calls=%async_computation.2 | async-start | bytes 131072 | tf_op jit(solution)/shard_map/all_to_all | solution.py:432
  55.6 0.0 copy-done.7
  55.6 0.0 copy-done.8
  55.6 0.0 copy-done.9
  55.6 0.0 copy-done.10
  55.6 0.0 copy-done.11
  55.7 0.0 copy-done.12
  55.7 0.0 copy-done.13
  55.7 0.0 copy-done.14
  55.7 0.0 copy-done.15
  55.7 0.0 copy-done.5
  55.7 0.0 copy-done.4
  55.7 0.0 copy-done.1
  55.7 0.0 copy-done.3
  55.7 0.0 copy-done
  55.7 0.0 copy-start.6
  55.8 1.2 %shard_map.263 = (f32[256,128]{1,0:T(8,128)S(1)}, f32[2,128]{1,0:T(2,128)S(1)}, f32[64,128]{1,0:T(8,128)S(1)}, f32[64,128]{1,0:T(8,128)S(1)}, f32[256,128]{1,0:T...) custom-call(s32[1]{0:T(128)} %bitcast.season, ...), custom_call_target="tpu_custom_call" | custom-call | tf_op jit(solution)/shard_map/pallas_call | solution.py:420
  56.9 12.2 %all-to-all-done.2 = bf16[64,1,4,128]{3,2,1,0:T(4,128)(2,1)S(1)} async-done(((bf16[64,1,4,128]{3,2,1,0:T(4,128)(2,1)}), bf16[64,1,4,128]{3,2,1,0:T(4,128)(2,1)S(1)}, u32[]{:S(2)}, u32[]{:S(2)}) %all-to-all-start.2) | async-done | bytes 65568 | tf_op jit(solution)/shard_map/all_to_all | solution.py:432
  69.1 0.0 copy-done.6
  69.1 0.6 shard_map.264
  69.8 18.5 %all_to_all.25 = bf16[64,5,2,128]{3,2,1,0:T(2,128)(2,1)S(1)} all-to-all(bf16[64,5,2,128]{3,2,1,0:T(2,128)(2,1)S(1)} %bitcast.26), channel_id=1, replica_groups=mesh['region'=64,'season'=8] {'region'}, dimensions={0} | all-to-all | bytes 327680 | tf_op jit(solution)/shard_map/all_to_all | solution.py:432
  88.3 0.1 shard_map.265
  88.4 11.2 %all_to_all.26.got = f32[8,8,128]{2,1,0:T(8,128)S(1)} all-to-all(f32[8,8,128]{2,1,0:T(8,128)S(1)} %shard_map.265), channel_id=1, replica_groups=mesh['region'=64,'season'=8] {'season'}, dimensions={0} | all-to-all | bytes 65536 | tf_op jit(solution)/shard_map/all_to_all | solution.py:437
  99.6 1.9 %shard_map.266 = (f32[256,128]{1,0:T(8,128)}, f32[2,128]{1,0:T(2,128)}, f32[256,128]{1,0:T(8,128)}, f32[64,128]{1,0:T(8,128)}, f32[64,128]{1,0:T(8,128)}, /*inde...) custom-call(s32[1]{0:T(128)} %bitcast.season, bf16[256,128]{1,0:T(8,128)(2,1)S(1)} %copy-done, ...), custom_call_target="tpu_custom_call" | custom-call | tf_op jit(solution)/shard_map/pallas_call | solution.py:420
Async XLA Ops:
  3.0 34.4 %all-to-all-start.1 = ((bf16[64,5,2,128]{3,2,1,0:T(2,128)(2,1)}), bf16[64,5,2,128]{3,2,1,0:T(2,128)(2,1)S(1)}, u32[]{:S(2)}, u32[]{:S(2)}) async-start(bf16[64,5,2,128]{3,2,1,0:T(2,128)(2,1)} %bitcast.12), calls=%async_computation.1 | async-start | bytes 327680 | tf_op jit(solution)/shard_map/all_to_all | solution.py:432
  22.3 33.3 %copy-start.7 = (f32[64,128]{1,0:T(8,128)S(1)}, f32[64,128]{1,0:T(8,128)}, u32[]{:S(2)}) copy-start(f32[64,128]{1,0:T(8,128)} %disch.1) | copy-start | bytes 98308
  22.3 33.3 %copy-start.8 = (s32[64,1]{0,1:T(1,128)S(1)}, s32[64,1]{0,1:T(1,128)}, u32[]{:S(2)}) copy-start(s32[64,1]{0,1:T(1,128)} %param.33) | copy-start | bytes 772
  22.4 33.3 %copy-start.9 = (s32[256]{0:T(256)S(1)}, s32[256]{0:T(256)}, u32[]{:S(2)}) copy-start(s32[256]{0:T(256)} %param.23) | copy-start | bytes 3076
  22.4 33.3 %copy-start.10 = (f32[256]{0:T(256)S(1)}, f32[256]{0:T(256)}, u32[]{:S(2)}) copy-start(f32[256]{0:T(256)} %param.24) | copy-start | bytes 3076
  22.4 33.3 %copy-start.11 = (f32[256]{0:T(256)S(1)}, f32[256]{0:T(256)}, u32[]{:S(2)}) copy-start(f32[256]{0:T(256)} %param.25) | copy-start | bytes 3076
  22.4 33.3 %copy-start.12 = (f32[64]{0:T(128)S(1)}, f32[64]{0:T(128)}, u32[]{:S(2)}) copy-start(f32[64]{0:T(128)} %param.30) | copy-start | bytes 772
  22.4 33.3 %copy-start.13 = (f32[64]{0:T(128)S(1)}, f32[64]{0:T(128)}, u32[]{:S(2)}) copy-start(f32[64]{0:T(128)} %param.31) | copy-start | bytes 772
  22.4 33.3 %copy-start.14 = (f32[64]{0:T(128)S(1)}, f32[64]{0:T(128)}, u32[]{:S(2)}) copy-start(f32[64]{0:T(128)} %param.32) | copy-start | bytes 772
  22.4 33.3 %copy-start.15 = (f32[256]{0:T(256)S(1)}, f32[256]{0:T(256)}, u32[]{:S(2)}) copy-start(f32[256]{0:T(256)} %param.35) | copy-start | bytes 3076
  24.3 20.4 %copy-start.2 = (f32[64,128]{1,0:T(8,128)S(1)}, f32[64,128]{1,0:T(8,128)}, u32[]{:S(2)}) copy-start(f32[64,128]{1,0:T(8,128)} %price.5) | copy-start | bytes 98308
  37.4 18.3 %copy-start.5 = (f32[64,128]{1,0:T(8,128)S(1)}, f32[64,128]{1,0:T(8,128)}, u32[]{:S(2)}) copy-start(f32[64,128]{1,0:T(8,128)} %sdual.1) | copy-start | bytes 98308
  37.4 12.0 %all-to-all-start = ((f32[8,8,128]{2,1,0:T(8,128)}), f32[8,8,128]{2,1,0:T(8,128)S(1)}, u32[]{:S(2)}, u32[]{:S(2)}) async-start(f32[8,8,128]{2,1,0:T(8,128)} %shard_map.260), calls=%async_computation | async-start | bytes 65536 | tf_op jit(solution)/shard_map/all_to_all | solution.py:437
  44.7 11.0 %copy-start.4 = (f32[64,128]{1,0:T(8,128)S(1)}, f32[64,128]{1,0:T(8,128)}, u32[]{:S(2)}) copy-start(f32[64,128]{1,0:T(8,128)} %level.1) | copy-start | bytes 98308
  44.7 11.0 %copy-start.1 = (f32[256,128]{1,0:T(8,128)S(1)}, f32[256,128]{1,0:T(8,128)}, u32[]{:S(2)}) copy-start(f32[256,128]{1,0:T(8,128)} %scarce.1) | copy-start | bytes 393220
  44.7 11.0 %copy-start.3 = (f32[256,128]{1,0:T(8,128)S(1)}, f32[256,128]{1,0:T(8,128)}, u32[]{:S(2)}) copy-start(f32[256,128]{1,0:T(8,128)} %disp.1) | copy-start | bytes 393220
  49.4 6.3 %copy-start = (bf16[256,128]{1,0:T(8,128)(2,1)S(1)}, bf16[256,128]{1,0:T(8,128)(2,1)}, u32[]{:S(2)}) copy-start(bf16[256,128]{1,0:T(8,128)(2,1)} %avail.3) | copy-start | bytes 196612
  49.4 19.7 %all-to-all-start.2 = ((bf16[64,1,4,128]{3,2,1,0:T(4,128)(2,1)}), bf16[64,1,4,128]{3,2,1,0:T(4,128)(2,1)S(1)}, u32[]{:S(2)}, u32[]{:S(2)}) async-start(bf16[64,1,4,128]{3,2,1,0:T(4,128)(2,1)} %bitcast.15), calls=%async_computation.2 | async-start | bytes 131072 | tf_op jit(solution)/shard_map/all_to_all | solution.py:432
  55.7 13.4 %copy-start.6 = (f32[64,128]{1,0:T(8,128)S(1)}, f32[64,128]{1,0:T(8,128)}, u32[]{:S(2)}) copy-start(f32[64,128]{1,0:T(8,128)} %demand.3) | copy-start | bytes 98308

commit v13 on v10

--- a/solution.py
+++ b/solution.py
@@ -13,6 +13,7 @@
 I32 = jnp.int32
 REGIONS, SEASONS = 64, 8
 BUS, SLOT, HOUR = 64, 256, 128
+FIRST = 40
 LINES = GROUP * LINK_CAP
 ROWS_EACH = 2 * LINK_CAP + 2
 PACKED = GROUP * ROWS_EACH
@@ -73,7 +74,13 @@
     return jnp.where(j < LINK_CAP, first, jnp.where(j < 2 * LINK_CAP, second, third))
 
 
+def rolled(value, by):
+    return jnp.concatenate([value[by:], value[:by]], axis=0)
+
+
 def pack(first, second, third, out_ref):
+    first = rolled(first, FIRST * LINK_CAP)
+    second = rolled(second, FIRST * LINK_CAP)
     shape = (PACKED, UNPACKED)
     place = as_bf(pack_target(iota(shape, 0)) == iota(shape, 1))
     for g in range(REGIONS // GROUP):
@@ -97,7 +104,8 @@
     first = jnp.concatenate([p[:LINES] for p in parts], axis=0)
     second = jnp.concatenate([p[LINES : 2 * LINES] for p in parts], axis=0)
     third = jnp.concatenate([p[2 * LINES :] for p in parts], axis=0)
-    return first, second, third
+    back = REGIONS - FIRST
+    return rolled(first, back * LINK_CAP), rolled(second, back * LINK_CAP), rolled(third, back)
 
 
 def fetch(sources, held, sems):
@@ -153,7 +161,7 @@
     for at, value in enumerate((wide(row256(line_to)), high, low)):
         spots = as_bf(iota((SLOT, 128), 1) == slot_kind + LINK_CAP * at)
         held = held + dot(spread * narrow(value), spots)
-    pack(narrow(f0), near, narrow(held), sent)
+    pack(narrow(f0), near, narrow(rolled(held, FIRST)), sent)
 
 
 def season_block(sums, level, dual_f, link_column):
@@ -179,7 +187,7 @@
         sent[s] = rows
 
 
-def ends_in(got, price, sent, arrive, cap):
+def ends_in(got, price, sent, far, arrive, cap):
     _, _, held = unpack(got)
     shape = (SLOT, REGIONS)
     spread = as_bf(iota(shape, 1) == iota(shape, 0) >> 2)
@@ -190,7 +198,9 @@
     limits = (lane == kind + LINK_CAP) | (lane == kind + 2 * LINK_CAP)
     limit = jnp.sum(jnp.where(limits, lines, 0.0), axis=1, keepdims=True)
     arrive_t = onehot_rows(ends, BUS)
-    sent[...] = narrow(dot(arrive_t, narrow(price[...])))
+    values = narrow(dot(arrive_t, narrow(price[...])))
+    far[...] = values
+    sent[...] = rolled(values, FIRST * LINK_CAP)
     arrive[...] = arrive_t
     cap[...] = jnp.broadcast_to(limit, (SLOT, HOUR))
 
@@ -311,7 +321,8 @@
 ):
     f0 = flow0[...]
     leave_t = leave[...]
-    moved, flow_x = line_step(f0, wide(near0[...]), wide(got[...]), cap[...], step_size)
+    far = wide(rolled(got[...], (REGIONS - FIRST) * LINK_CAP))
+    moved, flow_x = line_step(f0, wide(near0[...]), far, cap[...], step_size)
     f1 = mean(moved, f0)
     flow1[...] = f1
     p0 = price[...]
@@ -399,7 +410,8 @@
 
 def region_exchange(value, rows, per_pair):
     cut = value.reshape(REGIONS, per_pair, rows, HOUR)
-    got = lax.all_to_all(cut, "region", split_axis=0, concat_axis=0, tiled=True)
+    members = [[(FIRST + place) % REGIONS for place in range(REGIONS)]]
+    got = lax.all_to_all(cut, "region", 0, 0, axis_index_groups=members, tiled=True)
     return got.reshape(value.shape)
 
 
@@ -465,7 +477,9 @@
     got1 = region_exchange(sent1, 2, 5)
     (rows1,) = call(season_out, [seasons], avail, scarcity, soc, soc_dual, link, turn=True, fetched=True)
     season1 = season_exchange(rows1)
-    sent2, arrive, came_cap = call(ends_in, [lines_b, picks, lines], got1, price)
+    sent2, came_far0, arrive, came_cap = call(
+        ends_in, [lines_b, lines_b, picks, lines], got1, price
+    )
     got2 = region_exchange(sent2, LINK_CAP, 1)
     disp1, build1, disch1, level1, scarce1, sdual1, came1, balance, rows2, moves = call(
         first_local,
@@ -483,7 +497,7 @@
         got1,
         arrive,
         came_cap,
-        sent2,
+        came_far0,
         scalar=True,
         turn=True,
     )

time: 102 us -> 95.8 us (0.939)
  waiting for transfers between devices: 27.4 us -> 10.4 us
  starting transfers between devices: 32.7 us -> 44.1 us
    all_to_all x2, waiting for transfers between devices: 23.9 us -> 6.92 us  [region_exchange(): lax.all_to_all(cut, 'region', 0, 0, axis_index_groups=members, tiled=True)]
    all_to_all x2, starting transfers between devices: 25.5 us -> 38.4 us  [region_exchange(): lax.all_to_all(cut, 'region', 0, 0, axis_index_groups=members, tiled=True)]
    all_to_all x1, blocking collectives: 18.5 us -> 20.5 us  [region_exchange(): lax.all_to_all(cut, 'region', 0, 0, axis_index_groups=members, tiled=True)]
    all_to_all x1, starting transfers between devices: 7.27 us -> 5.72 us  [season_exchange(): lax.all_to_all(value, 'season', split_axis=0, concat_axis=0, tiled=True)]
    all_to_all x1, blocking collectives: 11.2 us -> 10.1 us  [season_exchange(): lax.all_to_all(value, 'season', split_axis=0, concat_axis=0, tiled=True)]
  transfers between devices with their start and end apart: 3 -> 3, of which waited for: 3 -> 3; matrix products, arithmetic and copies ran while one was open for 0% -> 0% of each run, Pallas kernels for 5% -> 4%
where the time goes in v13:
time: 95.8 us; the launch traced here: 95.4 us
  starting transfers between devices  44.1 us (46%)
  blocking collectives  30.6 us (32%)
  waiting for transfers between devices  10.4 us (11%)
  Pallas kernels  9.27 us (10%)
    all_to_all x2, starting transfers between devices, region_exchange(): lax.all_to_all(cut, 'region', 0, 0, axis_index_groups=members, tiled=True)  38.4 us
    all_to_all x1, blocking collectives, region_exchange(): lax.all_to_all(cut, 'region', 0, 0, axis_index_groups=members, tiled=True)  20.5 us
    all_to_all x1, blocking collectives, season_exchange(): lax.all_to_all(value, 'season', split_axis=0, concat_axis=0, tiled=True)  10.1 us
    pallas_call x7, Pallas kernels, call(): pl.pallas_call(body, out_shape=[jax.ShapeDtypeStruct(shape, kind) for sha...  9.27 us
    all_to_all x2, waiting for transfers between devices, region_exchange(): lax.all_to_all(cut, 'region', 0, 0, axis_index_groups=members, tiled=True)  6.92 us
    all_to_all x1, starting transfers between devices, season_exchange(): lax.all_to_all(value, 'season', split_axis=0, concat_axis=0, tiled=True)  5.72 us
    all_to_all x1, waiting for transfers between devices, season_exchange(): lax.all_to_all(value, 'season', split_axis=0, concat_axis=0, tiled=True)  3.48 us
  transfers between devices with their start and end apart: 3, of which 3 were waited for; matrix products, arithmetic and copies ran while one was open for 0% of the time, Pallas kernels for 4%

profile of v13, /device:TPU:1, one launch (start us, length us, event | category | flops | bytes accessed | tf_op | source)
XLA Modules:
  0.0 95.4 jit_solution(10289903644255796739)
XLA Ops:
  0.6 2.4 %shard_map.261 = (bf16[640,128]{1,0:T(8,128)(2,1)}, f32[256,128]{1,0:T(8,128)S(1)}, bf16[256,128]{1,0:T(8,128)(2,1)S(1)}, f32[256,128]{1,0:T(8,128)S(1)}, bf16[256,64]{1,0:T(8,128)(2,1)S(1)}) custom-call(f32[256,128]{1,0:T(8,128)} %refs_0_.3, f32[64,128]{1,0:T(8,128)} %price.5, s32[2,128]{1,0:T(2,128)} %bitcast.43, s32[2,128]{1,0:T(2,128)} %bitcast.44, ...), custom_call_target="tpu_custom_call" | custom-call | tf_op jit(solution)/shard_map/pallas_call | solution.py:401
  3.0 23.1 %all-to-all-start.1 = ((bf16[64,5,2,128]{3,2,1,0:T(2,128)(2,1)}), bf16[64,5,2,128]{3,2,1,0:T(2,128)(2,1)S(1)}, u32[]{:S(2)}, u32[]{:S(2)}) async-start(bf16[64,5,2,128]{3,2,1,0:T(2,128)(2,1)} %bitcast.12), calls=%async_computation.1 | async-start | bytes 327680 | tf_op jit(solution)/shard_map/all_to_all | solution.py:414
  26.1 0.0 copy-start.7
  26.1 0.0 copy-start.8
  26.1 0.0 copy-start.9
  26.1 0.0 copy-start.10
  26.1 0.0 copy-start.11
  26.2 0.0 copy-start.12
  26.2 0.0 copy-start.13
  26.2 0.0 copy-start.14
  26.2 0.0 copy-start.15
  26.2 1.9 %shard_map.260 = f32[8,8,128]{2,1,0:T(8,128)} custom-call(bf16[256,128]{1,0:T(8,128)(2,1)} %avail.3, f32[256,128]{1,0:T(8,128)} %scarce.1, f32[64,128]{1,0:T(8,128)} %level.1, f32[64,128]{1,0:T(8,128)} %sdual.1, s32[1,64]{1,0:T(1,128)} %bitcast.27), custom_call_target="tpu_custom_call" | custom-call | tf_op jit(solution)/shard_map/pallas_call | solution.py:401
  28.1 0.0 copy-start.2
  28.1 5.4 %all-to-all-done.1 = bf16[64,5,2,128]{3,2,1,0:T(2,128)(2,1)S(1)} async-done(((bf16[64,5,2,128]{3,2,1,0:T(2,128)(2,1)}), bf16[64,5,2,128]{3,2,1,0:T(2,128)(2,1)S(1)}, u32[]{:S(2)}, u32[]{:S(2)}) %all-to-all-start.1) | async-done | bytes 163872 | tf_op jit(solution)/shard_map/all_to_all | solution.py:414
  33.5 0.0 copy-start.5
  33.5 5.7 %all-to-all-start = ((f32[8,8,128]{2,1,0:T(8,128)}), f32[8,8,128]{2,1,0:T(8,128)S(1)}, u32[]{:S(2)}, u32[]{:S(2)}) async-start(f32[8,8,128]{2,1,0:T(8,128)} %shard_map.260), calls=%async_computation | async-start | bytes 65536 | tf_op jit(solution)/shard_map/all_to_all | solution.py:419
  39.2 0.0 copy-start.4
  39.2 0.0 copy-done.2
  39.2 0.0 copy-start.1
  39.2 0.0 copy-start.3
  39.2 1.2 %shard_map.262 = (bf16[256,128]{1,0:T(8,128)(2,1)}, bf16[256,128]{1,0:T(8,128)(2,1)S(1)}, bf16[256,64]{1,0:T(8,128)(2,1)S(1)}, f32[256,128]{1,0:T(8,128)S(1)}) custom-call(bf16[640,128]{1,0:T(8,128)(2,1)S(1)} %bitcast.21, f32[64,128]{1,0:T(8,128)S(1)} %copy-done.2), custom_call_target="tpu_custom_call" | custom-call | tf_op jit(solution)/shard_map/pallas_call | solution.py:401
  40.5 3.5 %all-to-all-done.got = f32[8,8,128]{2,1,0:T(8,128)S(1)} async-done(((f32[8,8,128]{2,1,0:T(8,128)}), f32[8,8,128]{2,1,0:T(8,128)S(1)}, u32[]{:S(2)}, u32[]{:S(2)}) %all-to-all-start) | async-done | bytes 32800 | tf_op jit(solution)/shard_map/all_to_all | solution.py:419
  43.9 0.0 copy-start
  43.9 15.3 %all-to-all-start.2 = ((bf16[64,1,4,128]{3,2,1,0:T(4,128)(2,1)}), bf16[64,1,4,128]{3,2,1,0:T(4,128)(2,1)S(1)}, u32[]{:S(2)}, u32[]{:S(2)}) async-start(bf16[64,1,4,128]{3,2,1,0:T(4,128)(2,1)} %bitcast.15), calls=%async_computation.2 | async-start | bytes 131072 | tf_op jit(solution)/shard_map/all_to_all | solution.py:414
  59.3 0.0 copy-done.7
  59.3 0.0 copy-done.8
  59.3 0.0 copy-done.9
  59.3 0.0 copy-done.10
  59.3 0.0 copy-done.11
  59.3 0.0 copy-done.12
  59.3 0.0 copy-done.13
  59.3 0.0 copy-done.14
  59.4 0.0 copy-done.15
  59.4 0.0 copy-done.5
  59.4 0.0 copy-done.4
  59.4 0.0 copy-done.1
  59.4 0.0 copy-done.3
  59.4 0.0 copy-done
  59.4 0.0 copy-start.6
  59.4 1.2 %shard_map.263 = (f32[256,128]{1,0:T(8,128)S(1)}, f32[2,128]{1,0:T(2,128)S(1)}, f32[64,128]{1,0:T(8,128)S(1)}, f32[64,128]{1,0:T(8,128)S(1)}, f32[256,128]{1,0:T...) custom-call(s32[1]{0:T(128)} %bitcast.season, ...), custom_call_target="tpu_custom_call" | custom-call | tf_op jit(solution)/shard_map/pallas_call | solution.py:401
  60.6 1.5 %all-to-all-done.2 = bf16[64,1,4,128]{3,2,1,0:T(4,128)(2,1)S(1)} async-done(((bf16[64,1,4,128]{3,2,1,0:T(4,128)(2,1)}), bf16[64,1,4,128]{3,2,1,0:T(4,128)(2,1)S(1)}, u32[]{:S(2)}, u32[]{:S(2)}) %all-to-all-start.2) | async-done | bytes 65568 | tf_op jit(solution)/shard_map/all_to_all | solution.py:414
  62.1 0.0 copy-done.6
  62.1 0.6 shard_map.264
  62.8 20.5 %all_to_all.25 = bf16[64,5,2,128]{3,2,1,0:T(2,128)(2,1)S(1)} all-to-all(bf16[64,5,2,128]{3,2,1,0:T(2,128)(2,1)S(1)} %bitcast.26), channel_id=1, replica_groups={{320,328,336,344,352,360,368,376,384,392,400,408,416,424,432,440,448,45..., dimensions={0} | all-to-all | bytes 327680 | tf_op jit(solution)/shard_map/all_to_all | solution.py:414
  83.3 0.1 shard_map.265
  83.4 10.1 %all_to_all.26.got = f32[8,8,128]{2,1,0:T(8,128)S(1)} all-to-all(f32[8,8,128]{2,1,0:T(8,128)S(1)} %shard_map.265), channel_id=1, replica_groups=mesh['region'=64,'season'=8] {'season'}, dimensions={0} | all-to-all | bytes 65536 | tf_op jit(solution)/shard_map/all_to_all | solution.py:419
  93.5 1.8 %shard_map.266 = (f32[256,128]{1,0:T(8,128)}, f32[2,128]{1,0:T(2,128)}, f32[256,128]{1,0:T(8,128)}, f32[64,128]{1,0:T(8,128)}, f32[64,128]{1,0:T(8,128)}, /*inde...) custom-call(s32[1]{0:T(128)} %bitcast.season, bf16[256,128]{1,0:T(8,128)(2,1)S(1)} %copy-done, ...), custom_call_target="tpu_custom_call" | custom-call | tf_op jit(solution)/shard_map/pallas_call | solution.py:401
Async XLA Ops:
  3.0 30.5 %all-to-all-start.1 = ((bf16[64,5,2,128]{3,2,1,0:T(2,128)(2,1)}), bf16[64,5,2,128]{3,2,1,0:T(2,128)(2,1)S(1)}, u32[]{:S(2)}, u32[]{:S(2)}) async-start(bf16[64,5,2,128]{3,2,1,0:T(2,128)(2,1)} %bitcast.12), calls=%async_computation.1 | async-start | bytes 327680 | tf_op jit(solution)/shard_map/all_to_all | solution.py:414
  26.1 33.2 %copy-start.7 = (f32[64,128]{1,0:T(8,128)S(1)}, f32[64,128]{1,0:T(8,128)}, u32[]{:S(2)}) copy-start(f32[64,128]{1,0:T(8,128)} %disch.1) | copy-start | bytes 98308
  26.1 33.2 %copy-start.8 = (s32[64,1]{0,1:T(1,128)S(1)}, s32[64,1]{0,1:T(1,128)}, u32[]{:S(2)}) copy-start(s32[64,1]{0,1:T(1,128)} %param.33) | copy-start | bytes 772
  26.1 33.2 %copy-start.9 = (s32[256]{0:T(256)S(1)}, s32[256]{0:T(256)}, u32[]{:S(2)}) copy-start(s32[256]{0:T(256)} %param.23) | copy-start | bytes 3076
  26.1 33.2 %copy-start.10 = (f32[256]{0:T(256)S(1)}, f32[256]{0:T(256)}, u32[]{:S(2)}) copy-start(f32[256]{0:T(256)} %param.24) | copy-start | bytes 3076
  26.1 33.2 %copy-start.11 = (f32[256]{0:T(256)S(1)}, f32[256]{0:T(256)}, u32[]{:S(2)}) copy-start(f32[256]{0:T(256)} %param.25) | copy-start | bytes 3076
  26.2 33.2 %copy-start.12 = (f32[64]{0:T(128)S(1)}, f32[64]{0:T(128)}, u32[]{:S(2)}) copy-start(f32[64]{0:T(128)} %param.30) | copy-start | bytes 772
  26.2 33.2 %copy-start.13 = (f32[64]{0:T(128)S(1)}, f32[64]{0:T(128)}, u32[]{:S(2)}) copy-start(f32[64]{0:T(128)} %param.31) | copy-start | bytes 772
  26.2 33.2 %copy-start.14 = (f32[64]{0:T(128)S(1)}, f32[64]{0:T(128)}, u32[]{:S(2)}) copy-start(f32[64]{0:T(128)} %param.32) | copy-start | bytes 772
  26.2 33.2 %copy-start.15 = (f32[256]{0:T(256)S(1)}, f32[256]{0:T(256)}, u32[]{:S(2)}) copy-start(f32[256]{0:T(256)} %param.35) | copy-start | bytes 3076
  28.1 11.1 %copy-start.2 = (f32[64,128]{1,0:T(8,128)S(1)}, f32[64,128]{1,0:T(8,128)}, u32[]{:S(2)}) copy-start(f32[64,128]{1,0:T(8,128)} %price.5) | copy-start | bytes 98308
  33.5 25.9 %copy-start.5 = (f32[64,128]{1,0:T(8,128)S(1)}, f32[64,128]{1,0:T(8,128)}, u32[]{:S(2)}) copy-start(f32[64,128]{1,0:T(8,128)} %sdual.1) | copy-start | bytes 98308
  33.5 10.4 %all-to-all-start = ((f32[8,8,128]{2,1,0:T(8,128)}), f32[8,8,128]{2,1,0:T(8,128)S(1)}, u32[]{:S(2)}, u32[]{:S(2)}) async-start(f32[8,8,128]{2,1,0:T(8,128)} %shard_map.260), calls=%async_computation | async-start | bytes 65536 | tf_op jit(solution)/shard_map/all_to_all | solution.py:419
  39.2 20.2 %copy-start.4 = (f32[64,128]{1,0:T(8,128)S(1)}, f32[64,128]{1,0:T(8,128)}, u32[]{:S(2)}) copy-start(f32[64,128]{1,0:T(8,128)} %level.1) | copy-start | bytes 98308
  39.2 20.2 %copy-start.1 = (f32[256,128]{1,0:T(8,128)S(1)}, f32[256,128]{1,0:T(8,128)}, u32[]{:S(2)}) copy-start(f32[256,128]{1,0:T(8,128)} %scarce.1) | copy-start | bytes 393220
  39.2 20.2 %copy-start.3 = (f32[256,128]{1,0:T(8,128)S(1)}, f32[256,128]{1,0:T(8,128)}, u32[]{:S(2)}) copy-start(f32[256,128]{1,0:T(8,128)} %disp.1) | copy-start | bytes 393220
  43.9 15.5 %copy-start = (bf16[256,128]{1,0:T(8,128)(2,1)S(1)}, bf16[256,128]{1,0:T(8,128)(2,1)}, u32[]{:S(2)}) copy-start(bf16[256,128]{1,0:T(8,128)(2,1)} %avail.3) | copy-start | bytes 196612
  43.9 18.2 %all-to-all-start.2 = ((bf16[64,1,4,128]{3,2,1,0:T(4,128)(2,1)}), bf16[64,1,4,128]{3,2,1,0:T(4,128)(2,1)S(1)}, u32[]{:S(2)}, u32[]{:S(2)}) async-start(bf16[64,1,4,128]{3,2,1,0:T(4,128)(2,1)} %bitcast.15), calls=%async_computation.2 | async-start | bytes 131072 | tf_op jit(solution)/shard_map/all_to_all | solution.py:414
  59.4 2.7 %copy-start.6 = (f32[64,128]{1,0:T(8,128)S(1)}, f32[64,128]{1,0:T(8,128)}, u32[]{:S(2)}) copy-start(f32[64,128]{1,0:T(8,128)} %demand.3) | copy-start | bytes 98308

commit v14 on v13

--- a/solution.py
+++ b/solution.py
@@ -13,7 +13,7 @@
 I32 = jnp.int32
 REGIONS, SEASONS = 64, 8
 BUS, SLOT, HOUR = 64, 256, 128
-FIRST = 40
+FIRST, FIRST_SEASON = 40, 4
 LINES = GROUP * LINK_CAP
 ROWS_EACH = 2 * LINK_CAP + 2
 PACKED = GROUP * ROWS_EACH
@@ -218,8 +218,8 @@
 
 def season_parts(got, season):
     sums = tree([got[s, 0:2] for s in range(SEASONS)])
-    before = got[(season + SEASONS - 1) & (SEASONS - 1), 2:4]
-    after = got[(season + 1) & (SEASONS - 1), 2:4]
+    before = got[((season + SEASONS - 1) & (SEASONS - 1)) ^ FIRST_SEASON, 2:4]
+    after = got[((season + 1) & (SEASONS - 1)) ^ FIRST_SEASON, 2:4]
     return sums, before, after
 
 
@@ -416,7 +416,8 @@
 
 
 def season_exchange(value):
-    return lax.all_to_all(value, "season", split_axis=0, concat_axis=0, tiled=True)
+    members = [[place ^ FIRST_SEASON for place in range(SEASONS)]]
+    return lax.all_to_all(value, "season", 0, 0, axis_index_groups=members, tiled=True)
 
 
 def on_device(

time: 95.8 us -> 94.8 us (0.990)
  waiting for transfers between devices: 10.4 us -> 7.7 us
  starting transfers between devices: 44.1 us -> 45.7 us
    all_to_all x1, waiting for transfers between devices: 3.48 us -> 0.78 us  [season_exchange(): lax.all_to_all(value, 'season', 0, 0, axis_index_groups=members, tiled=True)]
    all_to_all x1, starting transfers between devices: 5.72 us -> 7.35 us  [season_exchange(): lax.all_to_all(value, 'season', 0, 0, axis_index_groups=members, tiled=True)]
  transfers between devices with their start and end apart: 3 -> 3, of which waited for: 3 -> 3; matrix products, arithmetic and copies ran while one was open for 0% -> 0% of each run, Pallas kernels for 4% -> 5%
where the time goes in v14:
time: 94.8 us; the launch traced here: 94.3 us
  starting transfers between devices  45.7 us (48%)
  blocking collectives  30.6 us (32%)
  Pallas kernels  9.26 us (10%)
  waiting for transfers between devices  7.7 us (8%)
    all_to_all x2, starting transfers between devices, region_exchange(): lax.all_to_all(cut, 'region', 0, 0, axis_index_groups=members, tiled=True)  38.4 us
    all_to_all x1, blocking collectives, region_exchange(): lax.all_to_all(cut, 'region', 0, 0, axis_index_groups=members, tiled=True)  20.5 us
    all_to_all x1, blocking collectives, season_exchange(): lax.all_to_all(value, 'season', 0, 0, axis_index_groups=members, tiled=True)  10.1 us
    pallas_call x7, Pallas kernels, call(): pl.pallas_call(body, out_shape=[jax.ShapeDtypeStruct(shape, kind) for sha...  9.26 us
    all_to_all x1, starting transfers between devices, season_exchange(): lax.all_to_all(value, 'season', 0, 0, axis_index_groups=members, tiled=True)  7.35 us
    all_to_all x2, waiting for transfers between devices, region_exchange(): lax.all_to_all(cut, 'region', 0, 0, axis_index_groups=members, tiled=True)  6.92 us
  transfers between devices with their start and end apart: 3, of which 3 were waited for; matrix products, arithmetic and copies ran while one was open for 0% of the time, Pallas kernels for 5%

profile of v14, /device:TPU:1, one launch (start us, length us, event | category | flops | bytes accessed | tf_op | source)
XLA Modules:
  0.0 94.3 jit_solution(5193443112097794335)
XLA Ops:
  0.6 2.4 %shard_map.261 = (bf16[640,128]{1,0:T(8,128)(2,1)}, f32[256,128]{1,0:T(8,128)S(1)}, bf16[256,128]{1,0:T(8,128)(2,1)S(1)}, f32[256,128]{1,0:T(8,128)S(1)}, bf16[256,64]{1,0:T(8,128)(2,1)S(1)}) custom-call(f32[256,128]{1,0:T(8,128)} %refs_0_.3, f32[64,128]{1,0:T(8,128)} %price.5, s32[2,128]{1,0:T(2,128)} %bitcast.43, s32[2,128]{1,0:T(2,128)} %bitcast.44, ...), custom_call_target="tpu_custom_call" | custom-call | tf_op jit(solution)/shard_map/pallas_call | solution.py:401
  3.0 23.1 %all-to-all-start.1 = ((bf16[64,5,2,128]{3,2,1,0:T(2,128)(2,1)}), bf16[64,5,2,128]{3,2,1,0:T(2,128)(2,1)S(1)}, u32[]{:S(2)}, u32[]{:S(2)}) async-start(bf16[64,5,2,128]{3,2,1,0:T(2,128)(2,1)} %bitcast.12), calls=%async_computation.1 | async-start | bytes 327680 | tf_op jit(solution)/shard_map/all_to_all | solution.py:414
  26.1 0.0 copy-start.7
  26.1 0.0 copy-start.8
  26.1 0.0 copy-start.9
  26.1 0.0 copy-start.10
  26.1 0.0 copy-start.11
  26.2 0.0 copy-start.12
  26.2 0.0 copy-start.13
  26.2 0.0 copy-start.14
  26.2 0.0 copy-start.15
  26.2 1.9 %shard_map.260 = f32[8,8,128]{2,1,0:T(8,128)} custom-call(bf16[256,128]{1,0:T(8,128)(2,1)} %avail.3, f32[256,128]{1,0:T(8,128)} %scarce.1, f32[64,128]{1,0:T(8,128)} %level.1, f32[64,128]{1,0:T(8,128)} %sdual.1, s32[1,64]{1,0:T(1,128)} %bitcast.27), custom_call_target="tpu_custom_call" | custom-call | tf_op jit(solution)/shard_map/pallas_call | solution.py:401
  28.1 0.0 copy-start.2
  28.1 5.4 %all-to-all-done.1 = bf16[64,5,2,128]{3,2,1,0:T(2,128)(2,1)S(1)} async-done(((bf16[64,5,2,128]{3,2,1,0:T(2,128)(2,1)}), bf16[64,5,2,128]{3,2,1,0:T(2,128)(2,1)S(1)}, u32[]{:S(2)}, u32[]{:S(2)}) %all-to-all-start.1) | async-done | bytes 163872 | tf_op jit(solution)/shard_map/all_to_all | solution.py:414
  33.5 0.0 copy-start.5
  33.5 7.3 %all-to-all-start = ((f32[8,8,128]{2,1,0:T(8,128)}), f32[8,8,128]{2,1,0:T(8,128)S(1)}, u32[]{:S(2)}, u32[]{:S(2)}) async-start(f32[8,8,128]{2,1,0:T(8,128)} %shard_map.260), calls=%async_computation | async-start | bytes 65536 | tf_op jit(solution)/shard_map/all_to_all | solution.py:420
  40.9 0.0 copy-start.4
  40.9 0.0 copy-done.2
  40.9 0.0 copy-start.1
  40.9 0.0 copy-start.3
  40.9 1.2 %shard_map.262 = (bf16[256,128]{1,0:T(8,128)(2,1)}, bf16[256,128]{1,0:T(8,128)(2,1)S(1)}, bf16[256,64]{1,0:T(8,128)(2,1)S(1)}, f32[256,128]{1,0:T(8,128)S(1)}) custom-call(bf16[640,128]{1,0:T(8,128)(2,1)S(1)} %bitcast.21, f32[64,128]{1,0:T(8,128)S(1)} %copy-done.2), custom_call_target="tpu_custom_call" | custom-call | tf_op jit(solution)/shard_map/pallas_call | solution.py:401
  42.1 0.8 all-to-all-done.got
  42.9 0.0 copy-start
  42.9 15.3 %all-to-all-start.2 = ((bf16[64,1,4,128]{3,2,1,0:T(4,128)(2,1)}), bf16[64,1,4,128]{3,2,1,0:T(4,128)(2,1)S(1)}, u32[]{:S(2)}, u32[]{:S(2)}) async-start(bf16[64,1,4,128]{3,2,1,0:T(4,128)(2,1)} %bitcast.15), calls=%async_computation.2 | async-start | bytes 131072 | tf_op jit(solution)/shard_map/all_to_all | solution.py:414
  58.2 0.0 copy-done.7
  58.2 0.0 copy-done.8
  58.2 0.0 copy-done.9
  58.2 0.0 copy-done.10
  58.2 0.0 copy-done.11
  58.2 0.0 copy-done.12
  58.3 0.0 copy-done.13
  58.3 0.0 copy-done.14
  58.3 0.0 copy-done.15
  58.3 0.0 copy-done.5
  58.3 0.0 copy-done.4
  58.3 0.0 copy-done.1
  58.3 0.0 copy-done.3
  58.3 0.0 copy-done
  58.3 0.0 copy-start.6
  58.3 1.2 %shard_map.263 = (f32[256,128]{1,0:T(8,128)S(1)}, f32[2,128]{1,0:T(2,128)S(1)}, f32[64,128]{1,0:T(8,128)S(1)}, f32[64,128]{1,0:T(8,128)S(1)}, f32[256,128]{1,0:T...) custom-call(s32[1]{0:T(128)} %bitcast.season, ...), custom_call_target="tpu_custom_call" | custom-call | tf_op jit(solution)/shard_map/pallas_call | solution.py:401
  59.5 1.5 %all-to-all-done.2 = bf16[64,1,4,128]{3,2,1,0:T(4,128)(2,1)S(1)} async-done(((bf16[64,1,4,128]{3,2,1,0:T(4,128)(2,1)}), bf16[64,1,4,128]{3,2,1,0:T(4,128)(2,1)S(1)}, u32[]{:S(2)}, u32[]{:S(2)}) %all-to-all-start.2) | async-done | bytes 65568 | tf_op jit(solution)/shard_map/all_to_all | solution.py:414
  61.1 0.0 copy-done.6
  61.1 0.6 shard_map.264
  61.7 20.5 %all_to_all.25 = bf16[64,5,2,128]{3,2,1,0:T(2,128)(2,1)S(1)} all-to-all(bf16[64,5,2,128]{3,2,1,0:T(2,128)(2,1)S(1)} %bitcast.26), channel_id=1, replica_groups={{320,328,336,344,352,360,368,376,384,392,400,408,416,424,432,440,448,45..., dimensions={0} | all-to-all | bytes 327680 | tf_op jit(solution)/shard_map/all_to_all | solution.py:414
  82.2 0.1 shard_map.265
  82.4 10.1 %all_to_all.26.got = f32[8,8,128]{2,1,0:T(8,128)S(1)} all-to-all(f32[8,8,128]{2,1,0:T(8,128)S(1)} %shard_map.265), channel_id=1, replica_groups={{4,5,6,7,0,1,2,3},{12,13,14,15,8,9,10,11},{20,21,22,23,16,17,18,19},{28..., dimensions={0} | all-to-all | bytes 65536 | tf_op jit(solution)/shard_map/all_to_all | solution.py:420
  92.4 1.8 %shard_map.266 = (f32[256,128]{1,0:T(8,128)}, f32[2,128]{1,0:T(2,128)}, f32[256,128]{1,0:T(8,128)}, f32[64,128]{1,0:T(8,128)}, f32[64,128]{1,0:T(8,128)}, /*inde...) custom-call(s32[1]{0:T(128)} %bitcast.season, bf16[256,128]{1,0:T(8,128)(2,1)S(1)} %copy-done, ...), custom_call_target="tpu_custom_call" | custom-call | tf_op jit(solution)/shard_map/pallas_call | solution.py:401
Async XLA Ops:
  3.0 30.5 %all-to-all-start.1 = ((bf16[64,5,2,128]{3,2,1,0:T(2,128)(2,1)}), bf16[64,5,2,128]{3,2,1,0:T(2,128)(2,1)S(1)}, u32[]{:S(2)}, u32[]{:S(2)}) async-start(bf16[64,5,2,128]{3,2,1,0:T(2,128)(2,1)} %bitcast.12), calls=%async_computation.1 | async-start | bytes 327680 | tf_op jit(solution)/shard_map/all_to_all | solution.py:414
  26.1 32.1 %copy-start.7 = (f32[64,128]{1,0:T(8,128)S(1)}, f32[64,128]{1,0:T(8,128)}, u32[]{:S(2)}) copy-start(f32[64,128]{1,0:T(8,128)} %disch.1) | copy-start | bytes 98308
  26.1 32.1 %copy-start.8 = (s32[64,1]{0,1:T(1,128)S(1)}, s32[64,1]{0,1:T(1,128)}, u32[]{:S(2)}) copy-start(s32[64,1]{0,1:T(1,128)} %param.33) | copy-start | bytes 772
  26.1 32.1 %copy-start.9 = (s32[256]{0:T(256)S(1)}, s32[256]{0:T(256)}, u32[]{:S(2)}) copy-start(s32[256]{0:T(256)} %param.23) | copy-start | bytes 3076
  26.1 32.1 %copy-start.10 = (f32[256]{0:T(256)S(1)}, f32[256]{0:T(256)}, u32[]{:S(2)}) copy-start(f32[256]{0:T(256)} %param.24) | copy-start | bytes 3076
  26.1 32.1 %copy-start.11 = (f32[256]{0:T(256)S(1)}, f32[256]{0:T(256)}, u32[]{:S(2)}) copy-start(f32[256]{0:T(256)} %param.25) | copy-start | bytes 3076
  26.2 32.1 %copy-start.12 = (f32[64]{0:T(128)S(1)}, f32[64]{0:T(128)}, u32[]{:S(2)}) copy-start(f32[64]{0:T(128)} %param.30) | copy-start | bytes 772
  26.2 32.1 %copy-start.13 = (f32[64]{0:T(128)S(1)}, f32[64]{0:T(128)}, u32[]{:S(2)}) copy-start(f32[64]{0:T(128)} %param.31) | copy-start | bytes 772
  26.2 32.1 %copy-start.14 = (f32[64]{0:T(128)S(1)}, f32[64]{0:T(128)}, u32[]{:S(2)}) copy-start(f32[64]{0:T(128)} %param.32) | copy-start | bytes 772
  26.2 32.1 %copy-start.15 = (f32[256]{0:T(256)S(1)}, f32[256]{0:T(256)}, u32[]{:S(2)}) copy-start(f32[256]{0:T(256)} %param.35) | copy-start | bytes 3076
  28.1 12.8 %copy-start.2 = (f32[64,128]{1,0:T(8,128)S(1)}, f32[64,128]{1,0:T(8,128)}, u32[]{:S(2)}) copy-start(f32[64,128]{1,0:T(8,128)} %price.5) | copy-start | bytes 98308
  33.5 24.8 %copy-start.5 = (f32[64,128]{1,0:T(8,128)S(1)}, f32[64,128]{1,0:T(8,128)}, u32[]{:S(2)}) copy-start(f32[64,128]{1,0:T(8,128)} %sdual.1) | copy-start | bytes 98308
  33.5 9.4 %all-to-all-start = ((f32[8,8,128]{2,1,0:T(8,128)}), f32[8,8,128]{2,1,0:T(8,128)S(1)}, u32[]{:S(2)}, u32[]{:S(2)}) async-start(f32[8,8,128]{2,1,0:T(8,128)} %shard_map.260), calls=%async_computation | async-start | bytes 65536 | tf_op jit(solution)/shard_map/all_to_all | solution.py:420
  40.9 17.4 %copy-start.4 = (f32[64,128]{1,0:T(8,128)S(1)}, f32[64,128]{1,0:T(8,128)}, u32[]{:S(2)}) copy-start(f32[64,128]{1,0:T(8,128)} %level.1) | copy-start | bytes 98308
  40.9 17.4 %copy-start.1 = (f32[256,128]{1,0:T(8,128)S(1)}, f32[256,128]{1,0:T(8,128)}, u32[]{:S(2)}) copy-start(f32[256,128]{1,0:T(8,128)} %scarce.1) | copy-start | bytes 393220
  40.9 17.5 %copy-start.3 = (f32[256,128]{1,0:T(8,128)S(1)}, f32[256,128]{1,0:T(8,128)}, u32[]{:S(2)}) copy-start(f32[256,128]{1,0:T(8,128)} %disp.1) | copy-start | bytes 393220
  42.9 15.5 %copy-start = (bf16[256,128]{1,0:T(8,128)(2,1)S(1)}, bf16[256,128]{1,0:T(8,128)(2,1)}, u32[]{:S(2)}) copy-start(bf16[256,128]{1,0:T(8,128)(2,1)} %avail.3) | copy-start | bytes 196612
  42.9 18.2 %all-to-all-start.2 = ((bf16[64,1,4,128]{3,2,1,0:T(4,128)(2,1)}), bf16[64,1,4,128]{3,2,1,0:T(4,128)(2,1)S(1)}, u32[]{:S(2)}, u32[]{:S(2)}) async-start(bf16[64,1,4,128]{3,2,1,0:T(4,128)(2,1)} %bitcast.15), calls=%async_computation.2 | async-start | bytes 131072 | tf_op jit(solution)/shard_map/all_to_all | solution.py:414
  58.3 2.7 %copy-start.6 = (f32[64,128]{1,0:T(8,128)S(1)}, f32[64,128]{1,0:T(8,128)}, u32[]{:S(2)}) copy-start(f32[64,128]{1,0:T(8,128)} %demand.3) | copy-start | bytes 98308
